TPU v7x, 128 devices: a whole 4x4x4 slice. The times are simulated.
128 devices in a mesh: band: 8 (over x, y_hi), grow: 16 (over y_lo, z, core).
Axes of the slice: x: 4, y: 4 (y_hi: 2, y_lo: 2; y = y_hi * 2 + y_lo), z: 4, core: 2. Of those that a mesh axis runs over, the one named last changes fastest.
Arguments:
- chi_prev: float32 [15360, 4096], P('band', 'grow'), may hold values from -6 to 6
- zeta_rows: bfloat16 [15360, 8192], P(('band', 'grow')), may hold values from -0.0625 to 0.0625
- zeta_slab: bfloat16 [4096, 8192], P('grow'), may hold values from -0.0625 to 0.0625
- valence_store: bfloat16 [8, 128, 8192], P('band'), may hold values from -6 to 6
- valence_energy: float32 [8, 128], replicated, may hold values from -6 to -0.5
- conduction: bfloat16 [16, 8192], P('grow'), may hold values from -6 to 6
- conduction_energy: float32 [16], replicated, may hold values from 0.5 to 8
- owners: int32 [2], replicated, may hold values from 0 to 7, as said below
- gmap_rows: int32 [15360], P(('band', 'grow')), may hold values from 0 to 262143
- gmap_slab: int32 [4096], P('grow'), may hold values from 0 to 262143
Outputs:
- chi_new: float32 [15360, 4096], P('band', 'grow')
Inputs may be any that keep to these rules, and one draw needn't show every extreme that they name: `owners`: 2 different indices of stored panels; the last stored panel is always one of them, at a varying place.
All inputs are finite; a program needn't handle non-finite values.
Results may differ from a plain program's by a relative error of at most 0.0039.
Values may be sent and summed in bfloat16 or wider, within the bound.
No kernel may reach another device: no remote copies, remote signals or barrier semaphores. Data moves between devices by JAX's collectives and lax.ppermute only.
A program may use at most 256 MiB of HBM per device.

v0:
```python
import math

import jax
import jax.numpy as jnp
from jax import lax
from jax.sharding import PartitionSpec as P

BOX = 64


def from_root(shard, axis, root):
    mine = lax.axis_index(axis) == root
    return lax.psum(jnp.where(mine, shard, jnp.zeros_like(shard)), axis)


def coulomb_root(box_index):
    plane_size = BOX * BOX
    half_box = BOX // 2
    leading = box_index // plane_size
    middle = box_index // BOX % BOX
    trailing = box_index % BOX

    def centred(offset_idx):
        return jnp.where(offset_idx >= half_box, offset_idx - BOX, offset_idx).astype(jnp.float32)

    length_sq = centred(leading) ** 2 + centred(middle) ** 2 + centred(trailing) ** 2
    return 32.0 / jnp.sqrt(length_sq + 64.0)


def contract_last(left, right):
    return lax.dot_general(
        left, right, (((1,), (1,)), ((), ())), preferred_element_type=jnp.float32
    )


def on_device(
    chi_prev,
    zeta_rows,
    zeta_slab,
    valence_store,
    valence_energy,
    conduction,
    conduction_energy,
    owners,
    gmap_rows,
    gmap_slab,
):
    panel_count = owners.shape[0]
    points = valence_store.shape[2]
    panel_list = []
    for panel_idx in range(panel_count):
        panel_list.append(from_root(valence_store[0], "band", owners[panel_idx]))
    valence = jnp.concatenate(panel_list, axis=0)
    val_energy = jnp.take(valence_energy, owners, axis=0).reshape(-1)
    cond_all = lax.all_gather(conduction, "grow", axis=0, tiled=True)
    band_count = lax.axis_size("band")
    val_total = valence.shape[0]
    cond_total = cond_all.shape[0]
    norm_factor = 4.0 / math.sqrt(val_total * cond_total)
    weights = norm_factor / (conduction_energy[None, :] - val_energy[:, None])
    own_count = val_total // band_count
    cond_wide = cond_all.astype(jnp.float32)[None, :, :]

    def pairs_of(val_block):
        return (
            (val_block.astype(jnp.float32)[:, None, :] * cond_wide)
            .astype(jnp.bfloat16)
            .reshape(-1, points)
        )

    first_valence = lax.axis_index("band") * own_count
    own_valence = lax.dynamic_slice_in_dim(valence, first_valence, own_count, 0)
    own_weight = lax.dynamic_slice_in_dim(weights, first_valence, own_count, 0).reshape(-1)
    slab_local = (
        coulomb_root(gmap_slab)[:, None]
        * contract_last(zeta_slab, pairs_of(own_valence))
        * own_weight[None, :]
    ).astype(jnp.bfloat16)
    slab_all = lax.all_gather(slab_local, "band", axis=1, tiled=True)
    root_rows = coulomb_root(gmap_rows)
    rho_list = []
    for block_idx in range(band_count):
        val_block = valence[block_idx * own_count : (block_idx + 1) * own_count]
        rho_list.append(
            (root_rows[:, None] * contract_last(zeta_rows, pairs_of(val_block))).astype(
                jnp.bfloat16
            )
        )
    rho_rows = jnp.concatenate(rho_list, axis=1)
    row_slab = contract_last(rho_rows, lax.all_gather(slab_all, "grow", axis=0, tiled=True))
    summed = lax.all_to_all(row_slab, "grow", split_axis=1, concat_axis=0, tiled=True)
    return chi_prev - summed


def solution(mesh):
    placed = (
        P("band", "grow"),
        P(("band", "grow"), None),
        P("grow", None),
        P("band", None, None),
        P(),
        P("grow", None),
        P(),
        P(),
        P(("band", "grow")),
        P("grow"),
    )
    return jax.shard_map(
        on_device, mesh=mesh, in_specs=placed, out_specs=P("band", "grow"), check_vma=False
    )
```

profile of v0, /device:TPU:1, one launch (start us, length us, event | category | flops | bytes accessed | tf_op | source)
XLA Modules:
  0.0 534.7 jit_solution(4918579515711943906)
XLA Ops:
  6.6 0.0 all-reduce.3.cloned.1.call-start
  6.6 1.4 fusion.45
  9.3 3.9 select_bitcast_fusion
  13.2 0.0 all-reduce.3.cloned.1.call-update
  13.2 0.0 all-gather.4.cloned.1.call-start
  13.2 28.2 %all-gather = bf16[16,1,8192]{2,1,0:T(2,128)(2,1)S(1)} all-gather(bf16[1,1,8192]{2,1,0:T(2,128)(2,1)S(1)} %bitcast.107), channel_id=1, replica_groups=mesh['band'=8,'grow'=16] {'grow'}, dimensions={0}, use_global_device_ids=true | all-gather | bytes 278528 | tf_op jit(solution)/shard_map/all_gather | solution.py:55
  41.5 0.3 copy.21
  41.9 0.6 gather_fusion
  42.4 0.1 select_bitcast_fusion.2
  42.5 0.1 dynamic-slice
  42.6 0.1 subtract_divide_fusion
  42.7 0.1 copy.14
  42.7 0.1 mul.231
  42.8 160.1 %all-reduce.3.cloned.1.call-done = (bf16[128,8192]{1,0:T(8,128)(2,1)}, bf16[128,8192]{1,0:T(8,128)(2,1)}) async-done(((bf16[128,8192]{1,0:T(8,128)(2,1)}, bf16[128,8192]{1,0:T(8,128)(2,1)}), (bf16[128,8192]{1,0:T(8,128)(2,1)}, bf16[128,8192]{1,0:T(8,128)(2,1)})) %all-reduce.3.cloned.1.call-update) | async-done | bytes 4194320 | tf_op jit(solution)/shard_map/psum | solution.py:13
  202.9 5.7 %fusion.28 = (f32[32,8192]{1,0:T(8,128)S(1)}, f32[32,8192]{1,0:T(8,128)}, f32[32,8192]{1,0:T(8,128)}, f32[32,8192]{1,0:T(8,128)}, f32[32,8192]{1,0:T(8,128)}, /*...) fusion(s32[]{:T(128)S(6)} %select_n.115, ...), kind=kLoop, calls=%fused_computation.62 | loop fusion | flops 3145728 | bytes 17825796 | tf_op jit(solution)/shard_map/convert_element_type | solution.py:66
  208.6 30.6 %multiply_convert_fusion = (bf16[32,16,8192]{2,1,0:T(8,128)(2,1)}, bf16[32,16,8192]{2,1,0:T(8,128)(2,1)}, bf16[32,16,8192]{2,1,0:T(8,128)(2,1)}, bf16[32,16,8192...) fusion(f32[32,8192]{1,0:T(8,128)S(1)} %get-tuple-element.7, ...), kind=kLoop, calls=%fused_computation.1 | loop fusion | flops 75497472 | bytes 85458944 | tf_op jit(solution)/shard_map/convert_element_type | solution.py:67
  239.3 7.6 %fusion.2 = bf16[256,512]{0,1:T(8,128)(2,1)} fusion(bf16[512,8192]{1,0:T(8,128)(2,1)} %bitcast.103, bf16[256,8192]{1,0:T(8,128)(2,1)} %param.12, f32[512]{0:T(512)S(1)} %mul.231, f32[256]{0:T(256)S(1)} %rsqrt_multiply_fusion), kind=kOutput, calls=%fused_computation.19 | convolution fusion | flops 2147876864 | bytes 12848128 | tf_op jit(solution)/shard_map/dot_general | solution.py:31
  247.0 0.2 all-gather.6.cloned.1.call-start
  247.2 55.3 %all-gather.4.cloned.1.call-done = bf16[256,4096]{0,1:T(8,128)(2,1)} async-done(((bf16[256,512]{0,1:T(8,128)(2,1)}), bf16[256,4096]{0,1:T(8,128)(2,1)}) %all-gather.4.cloned.1.call-update) | async-done | bytes 2097168 | tf_op jit(solution)/shard_map/all_gather | solution.py:79
  302.6 6.4 %fusion.26 = bf16[120,4096]{1,0:T(8,128)(2,1)S(1)} fusion(bf16[512,8192]{1,0:T(8,128)(2,1)} %bitcast.102, bf16[120,8192]{1,0:T(8,128)(2,1)S(1)} %copy-done, f32[120]{0:T(128)S(1)} %rsqrt_multiply_fusion.1), kind=kOutput, calls=%fused_computation.51 | convolution fusion | flops 1006755840 | bytes 10478048 | tf_op jit(solution)/shard_map/dot_general | solution.py:31
  309.0 6.4 %fusion.24 = bf16[120,4096]{1,0:T(8,128)(2,1)S(1)} fusion(bf16[120,4096]{1,0:T(8,128)(2,1)S(1)} %fusion.26, bf16[512,8192]{1,0:T(8,128)(2,1)} %bitcast.101, bf16[120,8192]{1,0:T(8,128)(2,1)S(1)} %copy-done, f32[120]{0:T(128)S(1)} %rsqrt_multiply_fusion.1), kind=kOutput, calls=%fused_computation.49 | convolution fusion | flops 1006755840 | bytes 10478080 | tf_op jit(solution)/shard_map/dot_general | solution.py:31
  315.4 2.9 fusion.22
  318.4 2.9 fusion.20
  321.4 2.9 fusion.18
  324.4 3.1 fusion.16
  327.5 2.9 fusion.14
  330.5 2.9 fusion.12
  333.4 150.9 %all-gather.6.cloned.1.call-done = bf16[4096,4096]{0,1:T(8,128)(2,1)} async-done(((bf16[256,4096]{0,1:T(8,128)(2,1)}), bf16[4096,4096]{0,1:T(8,128)(2,1)}) %all-gather.6.cloned.1.call-update) | async-done | bytes 33554448 | tf_op jit(solution)/shard_map/all_gather | solution.py:90
  484.3 12.9 %fusion.46 = f32[120,4096]{1,0:T(8,128)S(1)} fusion(bf16[120,4096]{1,0:T(8,128)(2,1)S(1)} %fusion.12, bf16[4096,4096]{0,1:T(8,128)(2,1)} %all-gather.6.cloned.1.call-done), kind=kOutput, calls=%fused_computation.115 | convolution fusion | flops 4026531840 | bytes 36503552 | tf_op jit(solution)/shard_map/dot_general | solution.py:31
  497.3 0.1 copy.20
  497.4 29.2 %all_to_all.19 = f32[120,16,256]{2,0,1:T(8,128)S(1)} all-to-all(f32[120,16,256]{2,0,1:T(8,128)S(1)} %bitcast.105), channel_id=1, replica_groups=mesh['band'=8,'grow'=16] {'grow'}, dimensions={1} | all-to-all | bytes 3932160 | tf_op jit(solution)/shard_map/all_to_all | solution.py:91
  526.6 1.5 bitcast_subtract_fusion
  (53 shorter events, 0.2 us)
Async XLA Ops:
  6.5 296.0 %copy-start = (bf16[120,8192]{1,0:T(8,128)(2,1)S(1)}, bf16[120,8192]{1,0:T(8,128)(2,1)}, u32[]{:S(2)}) copy-start(bf16[120,8192]{1,0:T(8,128)(2,1)} %param.11) | copy-start | bytes 5898244
  6.5 35.3 %copy-start.4 = (s32[2]{0:T(128)S(1)}, s32[2]{0:T(128)}, u32[]{:S(2)}) copy-start(s32[2]{0:T(128)} %param.17) | copy-start | bytes 28
  6.5 6.7 %copy-start.2 = (bf16[1,8192]{1,0:T(2,128)(2,1)S(1)}, bf16[1,8192]{1,0:T(2,128)(2,1)}, u32[]{:S(2)}) copy-start(bf16[1,8192]{1,0:T(2,128)(2,1)} %param.15) | copy-start | bytes 49156
  6.5 35.3 %copy-start.3 = (f32[8,128]{1,0:T(8,128)S(1)}, f32[8,128]{1,0:T(8,128)}, u32[]{:S(2)}) copy-start(f32[8,128]{1,0:T(8,128)} %param.14) | copy-start | bytes 12292
  6.5 36.0 %copy-start.6 = (f32[16]{0:T(128)S(1)}, f32[16]{0:T(128)}, u32[]{:S(2)}) copy-start(f32[16]{0:T(128)} %param.16) | copy-start | bytes 196
  6.5 36.3 %copy-start.5 = (s32[256]{0:T(256)S(1)}, s32[256]{0:T(256)}, u32[]{:S(2)}) copy-start(s32[256]{0:T(256)} %param.19) | copy-start | bytes 3076
  6.6 196.4 %all-reduce.3.cloned.1.call-start = ((), (), s32[]{:S(2)}) async-start(), calls=%async_computation.3 | async-start | bytes 8388608 | tf_op jit(solution)/shard_map/psum | solution.py:13
  13.2 289.3 %all-gather.4.cloned.1.call-start = ((), (), s32[]{:S(2)}) async-start(), calls=%async_computation.1 | async-start | bytes 2359296 | tf_op jit(solution)/shard_map/all_gather | solution.py:79
  239.3 63.2 %copy-start.7 = (s32[120]{0:T(128)S(1)}, s32[120]{0:T(128)}, u32[]{:S(2)}) copy-start(s32[120]{0:T(128)} %param.18) | copy-start | bytes 1444
  247.0 237.4 %all-gather.6.cloned.1.call-start = ((), (), s32[]{:S(2)}) async-start(), calls=%async_computation.2 | async-start | bytes 35651584 | tf_op jit(solution)/shard_map/all_gather | solution.py:90
  302.5 12.9 %slice-start.10 = ((s8[8388608]{0:T(1024)(128)(4,1)}), s8[4194304]{0:T(1024)(128)(4,1)S(1)}, s32[]{:S(2)}) async-start(s8[8388608]{0:T(1024)(128)(4,1)} %bitcast.98), calls=%async_computation.14 | async-start | bytes 8388608
  302.5 12.9 %slice-start.11 = ((s8[8388608]{0:T(1024)(128)(4,1)}), s8[4194304]{0:T(1024)(128)(4,1)S(1)}, s32[]{:S(2)}) async-start(s8[8388608]{0:T(1024)(128)(4,1)} %bitcast.98), calls=%async_computation.15 | async-start | bytes 8388608
  302.5 15.8 %slice-start.8 = ((s8[8388608]{0:T(1024)(128)(4,1)}), s8[4194304]{0:T(1024)(128)(4,1)S(1)}, s32[]{:S(2)}) async-start(s8[8388608]{0:T(1024)(128)(4,1)} %bitcast.95), calls=%async_computation.12 | async-start | bytes 8388608
  309.0 9.4 %slice-start.9 = ((s8[8388608]{0:T(1024)(128)(4,1)}), s8[4194304]{0:T(1024)(128)(4,1)S(1)}, s32[]{:S(2)}) async-start(s8[8388608]{0:T(1024)(128)(4,1)} %bitcast.95), calls=%async_computation.13 | async-start | bytes 8388608
  315.4 6.0 %slice-start.6 = ((s8[8388608]{0:T(1024)(128)(4,1)}), s8[4194304]{0:T(1024)(128)(4,1)S(1)}, s32[]{:S(2)}) async-start(s8[8388608]{0:T(1024)(128)(4,1)} %bitcast.92), calls=%async_computation.10 | async-start | bytes 8388608
  315.4 8.9 %slice-start.4 = ((s8[8388608]{0:T(1024)(128)(4,1)}), s8[4194304]{0:T(1024)(128)(4,1)S(1)}, s32[]{:S(2)}) async-start(s8[8388608]{0:T(1024)(128)(4,1)} %bitcast.89), calls=%async_computation.8 | async-start | bytes 8388608
  318.4 3.0 slice-start.7
  318.4 5.9 %slice-start.5 = ((s8[8388608]{0:T(1024)(128)(4,1)}), s8[4194304]{0:T(1024)(128)(4,1)S(1)}, s32[]{:S(2)}) async-start(s8[8388608]{0:T(1024)(128)(4,1)} %bitcast.89), calls=%async_computation.9 | async-start | bytes 8388608
  321.3 6.2 %slice-start.2 = ((s8[8388608]{0:T(1024)(128)(4,1)}), s8[4194304]{0:T(1024)(128)(4,1)S(1)}, s32[]{:S(2)}) async-start(s8[8388608]{0:T(1024)(128)(4,1)} %bitcast.86), calls=%async_computation.6 | async-start | bytes 8388608
  324.3 3.2 slice-start.3
  324.3 6.1 %slice-start = ((s8[8388608]{0:T(1024)(128)(4,1)}), s8[4194304]{0:T(1024)(128)(4,1)S(1)}, s32[]{:S(2)}) async-start(s8[8388608]{0:T(1024)(128)(4,1)} %bitcast.83), calls=%async_computation.4 | async-start | bytes 8388608
  327.5 2.9 slice-start.1
  497.2 29.4 %copy-start.1 = (f32[1920,256]{1,0:T(8,128)S(1)}, f32[1920,256]{1,0:T(8,128)}, u32[]{:S(2)}) copy-start(f32[1920,256]{1,0:T(8,128)} %param.10) | copy-start | bytes 5898244
Sparse Core Ops, SparseCore 0:
  13.3 189.5 all-reduce.2
  247.1 55.3 all-gather.3
  304.1 180.2 all-gather.5
where the time goes:
time: 535 us
  waiting for transfers between devices  366 us (68%)
  blocking collectives  57.5 us (11%)
  matrix products  51.1 us (10%)
  other arithmetic  42 us (8%)
  between operations  14.8 us (3%)
    psum x1, waiting for transfers between devices, from_root(): return lax.psum(jnp.where(mine, shard, jnp.zeros_like(shard)), axis)  160 us
    all_gather x1, waiting for transfers between devices, on_device(): lax.all_gather(slab_all, 'grow', axis=0, tiled=True)  151 us
    all_gather x1, waiting for transfers between devices, on_device(): slab_all = lax.all_gather(slab_local, 'band', axis=1, tiled=True)  55.3 us
    dot_general x10, matrix products, contract_last(): lax.dot_general(left, right, (((1,), (1,)), ((), ())), preferred_element_...  51.1 us
    convert_element_type x1, other arithmetic, pairs_of(): return (val_block.astype(jnp.float32)[:, None, :] * cond_wide).astype(jnp...  30.6 us
    all_to_all x1, blocking collectives, on_device(): lax.all_to_all(row_slab, 'grow', split_axis=1, concat_axis=0, tiled=True)  29.2 us
    all_gather x1, blocking collectives, on_device(): cond_all = lax.all_gather(conduction, 'grow', axis=0, tiled=True)  28.2 us
  transfers between devices with their start and end apart: 3, of which 3 were waited for; matrix products, arithmetic and copies ran while one was open for 6% of the time, Pallas kernels for 0%

commit v1 on v0

v1 whole, which is shorter than its diff:
```python
import math

import jax
import jax.numpy as jnp
from jax import lax
from jax.experimental import pallas as pl
from jax.experimental.pallas import tpu as pltpu
from jax.sharding import PartitionSpec as P

BOX = 64
KC = 1024
VMEM = 56 * 1024 * 1024
BF = jnp.bfloat16
F32 = jnp.float32


def coulomb_root(box_index):
    plane_size = BOX * BOX
    half_box = BOX // 2
    leading = box_index // plane_size
    middle = box_index // BOX % BOX
    trailing = box_index % BOX

    def centred(offset_idx):
        return jnp.where(offset_idx >= half_box, offset_idx - BOX, offset_idx).astype(F32)

    length_sq = centred(leading) ** 2 + centred(middle) ** 2 + centred(trailing) ** 2
    return 32.0 / jnp.sqrt(length_sq + 64.0)


def linear(x, y, z, core):
    return ((x * 2 + y // 2) * 16) + (y % 2) * 8 + z * 2 + core


def route(step):
    pairs = []
    for x in range(4):
        for y in range(4):
            for z in range(4):
                for core in range(2):
                    pairs.append((linear(x, y, z, core), linear(*step(x, y, z, core))))
    return pairs


Z_UP = route(lambda x, y, z, c: (x, y, (z + 1) % 4, c))
Z_DOWN = route(lambda x, y, z, c: (x, y, (z + 3) % 4, c))
CORE = route(lambda x, y, z, c: (x, y, z, 1 - c))
X_PAIR = route(lambda x, y, z, c: (x ^ 1, y, z, c))
Y_PAIR = route(lambda x, y, z, c: (x, y ^ 1, z, c))
Y_CROSS = route(lambda x, y, z, c: (x, 3 - y, z, c))


def send(value, pairs):
    return lax.ppermute(value, ("band", "grow"), pairs)


def nt_dot(left, right):
    return lax.dot_general(left, right, (((1,), (1,)), ((), ())), preferred_element_type=F32)


def slab_body(val, cond, zeta, weight, root, out, lhs, acc):
    step = pl.program_id(0)
    conds = cond.shape[0]
    for c in range(conds):
        lhs[c * 128 : (c + 1) * 128, :] = val[...] * cond[c : c + 1, :]
    part = nt_dot(lhs[...], zeta[...])

    @pl.when(step == 0)
    def _():
        acc[...] = part

    @pl.when(step > 0)
    def _():
        acc[...] += part

    @pl.when(step == pl.num_programs(0) - 1)
    def _():
        out[...] = (acc[...] * root[...] * weight[...]).astype(BF)


def slab_kernel(val, cond, zeta, weight, root):
    conds, points = cond.shape
    pairs = conds * 128
    cols = zeta.shape[0]
    return pl.pallas_call(
        slab_body,
        grid=(points // KC,),
        in_specs=[
            pl.BlockSpec((128, KC), lambda k: (0, k)),
            pl.BlockSpec((conds, KC), lambda k: (0, k)),
            pl.BlockSpec((cols, KC), lambda k: (0, k)),
            pl.BlockSpec((pairs, 1), lambda k: (0, 0)),
            pl.BlockSpec((1, cols), lambda k: (0, 0)),
        ],
        out_specs=pl.BlockSpec((pairs, cols), lambda k: (0, 0)),
        out_shape=jax.ShapeDtypeStruct((pairs, cols), BF),
        scratch_shapes=[pltpu.VMEM((pairs, KC), BF), pltpu.VMEM((pairs, cols), F32)],
        compiler_params=pltpu.CompilerParams(vmem_limit_bytes=VMEM),
        cost_estimate=pl.CostEstimate(
            flops=2 * pairs * cols * points, bytes_accessed=8 << 20, transcendentals=0
        ),
        name="slab_pairs",
    )(val, cond, zeta, weight, root)


def rho_body(zeta, cond, val_a, val_b, root, out, lhs, rhs, acc):
    step = pl.program_id(0)
    conds = cond.shape[0]
    rows = zeta.shape[0]

    @pl.when(step == 0)
    def _():
        lhs[...] = jnp.zeros_like(lhs)

    for c in range(conds):
        lhs[c * 128 : c * 128 + rows, :] = zeta[...] * cond[c : c + 1, :]
    rhs[0:128, :] = val_a[...]
    rhs[128:256, :] = val_b[...]
    part = nt_dot(lhs[...], rhs[...])

    @pl.when(step == 0)
    def _():
        acc[...] = part

    @pl.when(step > 0)
    def _():
        acc[...] += part

    @pl.when(step == pl.num_programs(0) - 1)
    def _():
        for c in range(conds):
            block = acc[c * 128 : c * 128 + rows, :] * root[...]
            out[0, :, c * 128 : (c + 1) * 128] = block[:, 0:128].astype(BF)
            out[1, :, c * 128 : (c + 1) * 128] = block[:, 128:256].astype(BF)


def rho_kernel(zeta, cond, val_a, val_b, root):
    conds, points = cond.shape
    rows = zeta.shape[0]
    return pl.pallas_call(
        rho_body,
        grid=(points // KC,),
        in_specs=[
            pl.BlockSpec((rows, KC), lambda k: (0, k)),
            pl.BlockSpec((conds, KC), lambda k: (0, k)),
            pl.BlockSpec((128, KC), lambda k: (0, k)),
            pl.BlockSpec((128, KC), lambda k: (0, k)),
            pl.BlockSpec((rows, 1), lambda k: (0, 0)),
        ],
        out_specs=pl.BlockSpec((2, rows, conds * 128), lambda k: (0, 0, 0)),
        out_shape=jax.ShapeDtypeStruct((2, rows, conds * 128), BF),
        scratch_shapes=[
            pltpu.VMEM((conds * 128, KC), BF),
            pltpu.VMEM((256, KC), BF),
            pltpu.VMEM((conds * 128, 256), F32),
        ],
        compiler_params=pltpu.CompilerParams(vmem_limit_bytes=VMEM),
        cost_estimate=pl.CostEstimate(
            flops=2 * conds * 128 * 256 * points, bytes_accessed=8 << 20, transcendentals=0
        ),
        name="rho_rows",
    )(zeta, cond, val_a, val_b, root)


def chi_kernel(parts, slab_a, slab_b, out_dtype, name):
    _, rows, depth = parts[0][0].shape
    cols = slab_a.shape[1]
    count = len(parts)
    blk = 1024

    def body(*refs):
        ins = refs[:count]
        slab_0, slab_1, out, lhs, acc = refs[count:]
        step = pl.program_id(0)

        @pl.when(step == 0)
        def _():
            lhs[...] = jnp.zeros_like(lhs)
            acc[...] = jnp.zeros_like(acc)

        total = acc[...]
        for half, slab in ((0, slab_0), (1, slab_1)):
            for i in range(count):
                which = 1 - half if parts[i][1] else half
                lhs[half, i * 128 : i * 128 + rows, :] = ins[i][which]
            total += jnp.dot(lhs[half], slab[...], preferred_element_type=F32)
        acc[...] = total

        @pl.when(step == pl.num_programs(0) - 1)
        def _():
            for i in range(count):
                out[i] = acc[i * 128 : i * 128 + rows, :].astype(out_dtype)

    return pl.pallas_call(
        body,
        grid=(depth // blk,),
        in_specs=[pl.BlockSpec((2, rows, blk), lambda k: (0, 0, k))] * count
        + [pl.BlockSpec((blk, cols), lambda k: (k, 0))] * 2,
        out_specs=pl.BlockSpec((count, rows, cols), lambda k: (0, 0, 0)),
        out_shape=jax.ShapeDtypeStruct((count, rows, cols), out_dtype),
        scratch_shapes=[
            pltpu.VMEM((2, count * 128, blk), BF),
            pltpu.VMEM((count * 128, cols), F32),
        ],
        compiler_params=pltpu.CompilerParams(vmem_limit_bytes=VMEM),
        cost_estimate=pl.CostEstimate(
            flops=2 * count * rows * cols * 2 * depth,
            bytes_accessed=count * rows * depth * 4 + depth * cols * 4,
            transcendentals=0,
        ),
        name=name,
    )(*[p[0] for p in parts], slab_a, slab_b)


def finish_kernel(place, chi, mine_a, mine_b, theirs_a, theirs_b):
    total_rows, cols = chi.shape
    rows = mine_a.shape[1]
    chi_blocks = chi.reshape(total_rows // rows, rows, cols)

    def body(place_ref, chi_ref, ma, mb, ta, tb, out):
        step = pl.program_id(0)
        core = place_ref[8]
        for first, src in ((0, ma), (3, mb), (4, ta), (7, tb)):
            last = {0: 3, 3: 4, 4: 7, 7: 8}[first]

            @pl.when(jnp.logical_and(step >= first, step < last))
            def _(src=src):
                out[core] = chi_ref[core] - src[0].astype(F32)
                out[1 - core] = chi_ref[1 - core] - src[1].astype(F32)

    def slot(first, count):
        return lambda i, place_ref: (jnp.clip(i - first, 0, count - 1), 0, 0)

    where = lambda i, place_ref: (place_ref[i], 0, 0)
    grid_spec = pltpu.PrefetchScalarGridSpec(
        num_scalar_prefetch=1,
        grid=(8,),
        in_specs=[
            pl.BlockSpec((2, rows, cols), where),
            pl.BlockSpec((2, rows, cols), slot(0, 3)),
            pl.BlockSpec((2, rows, cols), slot(3, 1)),
            pl.BlockSpec((2, rows, cols), slot(4, 3)),
            pl.BlockSpec((2, rows, cols), slot(7, 1)),
        ],
        out_specs=pl.BlockSpec((2, rows, cols), where),
    )
    return pl.pallas_call(
        body,
        grid_spec=grid_spec,
        out_shape=jax.ShapeDtypeStruct(chi_blocks.shape, F32),
        compiler_params=pltpu.CompilerParams(vmem_limit_bytes=VMEM),
        cost_estimate=pl.CostEstimate(flops=0, bytes_accessed=6 << 20, transcendentals=0),
        name="finish",
    )(place, chi_blocks, mine_a, mine_b, theirs_a, theirs_b).reshape(total_rows, cols)


def on_device(
    chi_prev,
    zeta_rows,
    zeta_slab,
    valence_store,
    valence_energy,
    conduction,
    conduction_energy,
    owners,
    gmap_rows,
    gmap_slab,
):
    band = lax.axis_index("band")
    grow = lax.axis_index("grow")
    core = grow % 2
    yz = grow // 2
    turn = (band // 2 + band % 2) % 2
    points = valence_store.shape[2]

    store = valence_store[0]
    piece_a = lax.dynamic_slice_in_dim(store, yz * 16 + core * 8, 8, 0)
    piece_b = lax.dynamic_slice_in_dim(store, yz * 16 + (1 - core) * 8, 8, 0)
    turns = [(b // 2 + b % 2) % 2 for b in range(8)]
    pieces = jnp.stack([piece_b if t else piece_a for t in turns])
    panels = lax.all_to_all(pieces, "band", split_axis=0, concat_axis=0, tiled=True)
    chosen = jnp.concatenate(
        [lax.dynamic_slice_in_dim(panels, owners[i], 1, 0)[0] for i in range(2)], axis=0
    )
    payload = jnp.concatenate([chosen, conduction.reshape(16, points // 16)], axis=1)
    width = payload.shape[1]
    groups = [list(range(0, 16, 2)), list(range(1, 16, 2))]
    mine = lax.all_to_all(
        jnp.broadcast_to(payload[None], (8, 16, width)),
        "grow",
        split_axis=0,
        concat_axis=0,
        tiled=True,
        axis_index_groups=groups,
    ).reshape(128, width)
    other = send(mine, CORE)

    cond_mine = mine[:, points:].reshape(8, points)
    cond_other = other[:, points:].reshape(8, points)
    cond = jnp.concatenate(
        [
            jnp.where(core == 0, cond_mine, cond_other),
            jnp.where(core == 0, cond_other, cond_mine),
        ],
        axis=0,
    )
    energy_c = conduction_energy.reshape(8, 2).T.reshape(16)
    energy_v = jnp.take(valence_energy, owners, axis=0).reshape(2, 8, 2, 8)
    half = (core + turn) % 2
    energy_v = lax.dynamic_index_in_dim(energy_v, half, 2, keepdims=False)
    energy_v = energy_v.transpose(1, 0, 2).reshape(128)
    weight = (4.0 / math.sqrt(4096)) / (energy_c[:, None] - energy_v[None, :])

    rho = rho_kernel(zeta_rows, cond, mine, other, coulomb_root(gmap_rows)[:, None])
    slab_pp = slab_kernel(
        mine, cond, zeta_slab, weight.reshape(2048, 1), coulomb_root(gmap_slab)[None, :]
    )

    from_down = send(rho, Z_UP)
    from_up = send(rho, Z_DOWN)
    rho_x = send(rho, CORE)
    slab_px = send(slab_pp, X_PAIR)
    slab_yp = send(slab_pp, Y_PAIR)
    slab_yx = send(slab_pp, Y_CROSS)
    far_0 = send(from_down[0], Z_UP)
    far_1 = send(from_up[1], Z_DOWN)
    from_down_x = send(from_down, CORE)
    from_up_x = send(from_up, CORE)
    far = jnp.stack([far_0, far_1])
    far_x = send(far, CORE)

    near = [
        (rho, False),
        (rho_x, True),
        (from_down, False),
        (from_down_x, True),
        (from_up, False),
        (from_up_x, True),
    ]
    rest = [(far, False), (far_x, True)]
    near_out = chi_kernel(near, slab_yp, slab_yx, BF, "chi_near_out")
    near_in = chi_kernel(near, slab_pp, slab_px, F32, "chi_near_in")
    got_near = send(near_out, Y_PAIR)
    rest_out = chi_kernel(rest, slab_yp, slab_yx, BF, "chi_far_out")
    got_rest = send(rest_out, Y_PAIR)
    rest_in = chi_kernel(rest, slab_pp, slab_px, F32, "chi_far_in")

    yl = grow // 8
    z = yz % 4
    slots = jnp.stack([z, (z + 3) % 4, (z + 1) % 4, (z + 2) % 4]).astype(jnp.int32)
    place = jnp.concatenate([yl * 4 + slots, (1 - yl) * 4 + slots, core[None]]).astype(jnp.int32)
    return finish_kernel(place, chi_prev, near_in, rest_in, got_near, got_rest)


def solution(mesh):
    placed = (
        P("band", "grow"),
        P(("band", "grow"), None),
        P("grow", None),
        P("band", None, None),
        P(),
        P("grow", None),
        P(),
        P(),
        P(("band", "grow")),
        P("grow"),
    )
    return jax.shard_map(
        on_device, mesh=mesh, in_specs=placed, out_specs=P("band", "grow"), check_vma=False
    )
```

time: 535 us -> 171 us (0.32)
  waiting for transfers between devices: 366 us -> 35.4 us
  Pallas kernels: 0 us -> 53.3 us
  matrix products: 51.1 us -> 0 us
  other arithmetic: 42 us -> 2.61 us
  blocking collectives: 57.5 us -> 31.2 us
  starting transfers between devices: 0.3 us -> 23.2 us
  local copies, waits for them, and re-layouts: 2.71 us -> 18.3 us
  between operations: 14.8 us -> 3.88 us
    all_gather x2 -> x0, waiting for transfers between devices: 206 us -> none  [the longest x1 151 us: on_device(): lax.all_gather(slab_all, 'grow', axis=0, tiled=True)]
    psum x1 -> x0, waiting for transfers between devices: 160 us -> none  [from_root(): return lax.psum(jnp.where(mine, shard, jnp.zeros_like(shard)), axis)]
    pallas_call x0 -> x7, Pallas kernels: none -> 53.3 us  [the longest x4 16.7 us: chi_kernel(): pl.pallas_call(body, grid=(depth // blk,), in_specs=[pl.BlockSpec((2, row...]
    dot_general x10 -> x0, matrix products: 51.1 us -> none  [contract_last(): lax.dot_general(left, right, (((1,), (1,)), ((), ())), preferred_element_...]
    convert_element_type x2 -> x0, other arithmetic: 36.4 us -> none  [the longest x1 30.6 us: pairs_of(): return (val_block.astype(jnp.float32)[:, None, :] * cond_wide).astype(jnp...]
    all_gather x1 -> x0, blocking collectives: 28.2 us -> none  [on_device(): cond_all = lax.all_gather(conduction, 'grow', axis=0, tiled=True)]
    ppermute x0 -> x14, waiting for transfers between devices: none -> 24.3 us  [send(): return lax.ppermute(value, ('band', 'grow'), pairs)]
    ppermute x0 -> x14, starting transfers between devices: none -> 15.8 us  [send(): return lax.ppermute(value, ('band', 'grow'), pairs)]
  transfers between devices with their start and end apart: 3 -> 15, of which waited for: 3 -> 9; matrix products, arithmetic and copies ran while one was open for 6% -> 3% of each run, Pallas kernels for 0% -> 19%
where the time goes in v1:
time: 171 us; the launch traced here: 168 us
  Pallas kernels  53.3 us (31%)
  waiting for transfers between devices  35.4 us (21%)
  blocking collectives  31.2 us (18%)
  starting transfers between devices  23.2 us (14%)
  local copies, waits for them, and re-layouts  18.3 us (11%)
  between operations  3.88 us (2%)
  other arithmetic  2.61 us (2%)
    all_to_all x1, blocking collectives, on_device(): lax.all_to_all(jnp.broadcast_to(payload[None], (8, 16, width)), 'grow', s...  31.2 us
    ppermute x14, waiting for transfers between devices, send(): return lax.ppermute(value, ('band', 'grow'), pairs)  24.3 us
    pallas_call x4, Pallas kernels, chi_kernel(): pl.pallas_call(body, grid=(depth // blk,), in_specs=[pl.BlockSpec((2, row...  16.7 us
    ppermute x14, starting transfers between devices, send(): return lax.ppermute(value, ('band', 'grow'), pairs)  15.8 us
    pallas_call x1, Pallas kernels, slab_kernel(): pl.pallas_call(slab_body, grid=(points // KC,), in_specs=[pl.BlockSpec((1...  14.9 us
    pallas_call x1, Pallas kernels, rho_kernel(): pl.pallas_call(rho_body, grid=(points // KC,), in_specs=[pl.BlockSpec((ro...  14.8 us
    unnamed x36, local copies, waits for them, and re-layouts  12.6 us
    all_to_all x1, waiting for transfers between devices, on_device(): lax.all_to_all(pieces, 'band', split_axis=0, concat_axis=0, tiled=True)  11.1 us
  transfers between devices with their start and end apart: 15, of which 9 were waited for; matrix products, arithmetic and copies ran while one was open for 3% of the time, Pallas kernels for 19%

profile of v1, /device:TPU:1, one launch (start us, length us, event | category | flops | bytes accessed | tf_op | source)
XLA Modules:
  0.0 168.0 jit_solution(11649458851138933203)
XLA Ops:
  0.0 1.6 dynamic-slice_dynamic-update-slice_fusion.6
  1.6 1.6 dynamic-slice_dynamic-update-slice_fusion.2
  3.2 1.6 dynamic-slice_dynamic-update-slice_fusion.1
  4.8 1.6 dynamic-slice_dynamic-update-slice_fusion.5
  6.3 1.6 dynamic-slice_dynamic-update-slice_fusion.4
  7.9 1.6 dynamic-slice_dynamic-update-slice_fusion
  9.5 1.6 dynamic-slice_dynamic-update-slice_fusion.3
  11.0 1.6 dynamic-slice_dynamic-update-slice_fusion.7
  12.6 7.5 %all-to-all-start = ((bf16[8,8,8192]{2,1,0:T(8,128)(2,1)}), bf16[8,8,8192]{2,1,0:T(8,128)(2,1)S(1)}, u32[]{:S(2)}, u32[]{:S(2)}) async-start(bf16[8,8,8192]{2,1,0:T(8,128)(2,1)} %dynamic-slice_dynamic-update-slice_fusion.7), calls=%async_computation | async-start | bytes 2097152 | tf_op jit(solution)/shard_map/all_to_all | solution.py:281
  24.5 11.1 %all-to-all-done = bf16[8,8,8192]{2,1,0:T(8,128)(2,1)S(1)} async-done(((bf16[8,8,8192]{2,1,0:T(8,128)(2,1)}), bf16[8,8,8192]{2,1,0:T(8,128)(2,1)S(1)}, u32[]{:S(2)}, u32[]{:S(2)}) %all-to-all-start) | async-done | bytes 1048608 | tf_op jit(solution)/shard_map/all_to_all | solution.py:281
  35.8 31.2 %all_to_all.10 = bf16[8,16,8704]{2,1,0:T(8,128)(2,1)S(1)} all-to-all(bf16[8,16,8704]{2,1,0:T(8,128)(2,1)S(1)} %broadcast_in_dim.28), channel_id=1, replica_groups={{0,2,4,6,8,10,12,14},{1,3,5,7,9,11,13,15},{16,18,20,22,24,26,28,30},{17..., dimensions={0} | all-to-all | bytes 4456448 | tf_op jit(solution)/shard_map/all_to_all | solution.py:288
  67.0 3.0 %collective-permute-start = (bf16[128,8704]{1,0:T(8,128)(2,1)S(1)}, bf16[128,8704]{1,0:T(8,128)(2,1)}, u32[]{:S(2)}, u32[]{:S(2)}) collective-permute-start(bf16[128,8704]{1,0:T(8,128)(2,1)S(1)} %bitcast.29), channel_id=1, source_target_pairs={{0,1},{1,0},{2,3},{3,2},{4,5},{5,4},{6,7},{7,6},{8,9},{9,8},{10,11... | collective-permute-start | bytes 6684680 | tf_op jit(solution)/shard_map/ppermute | solution.py:54
  72.0 1.4 copy.19.weight
  76.0 14.8 %rho_rows.1.refs_0_ = bf16[2,120,2048]{2,1,0:T(8,128)(2,1)} custom-call(bf16[120,8192]{1,0:T(8,128)(2,1)} %zeta.2, bf16[16,8192]{1,0:T(8,128)(2,1)} %copy-done.8, bf16[128,8704]{1,0:T(8,128)(2,1)} %bitcast.31, bf16[128,8704]{1,0:T(8,128)(2,1)} %collective-permute-done.val_b, f32[120,1]{1,0:T(8,128)} %copy.15.root), custom_call_target="tpu_custom_call" | custom-call | flops 8589934592 | bytes 8388608 | tf_op jit(solution)/shard_map/rho_rows/pallas_call | solution.py:140
  92.8 0.9 collective-permute-start.1
  93.8 14.9 %slab_pairs.1.refs_6_.refs_2_ = bf16[2048,256]{1,0:T(8,128)(2,1)} custom-call(bf16[128,8704]{1,0:T(8,128)(2,1)} %bitcast.32, bf16[16,8192]{1,0:T(8,128)(2,1)} %copy-done.8, bf16[256,8192]{1,0:T(8,128)(2,1)} %zeta.3, f32[2048,1]{1,0:T(8,128)} %copy.19.weight, f32[1,256]{1,0:T(1,128)} %bitcast.38), custom_call_target="tpu_custom_call" | custom-call | flops 8589934592 | bytes 8388608 | tf_op jit(solution)/shard_map/slab_pairs/pallas_call | solution.py:85
  108.7 1.4 collective-permute-start.11
  110.1 3.9 %collective-permute-done.4.refs_4_ = bf16[2,120,2048]{2,1,0:T(8,128)(2,1)S(1)} collective-permute-done((bf16[2,120,2048]{2,1,0:T(8,128)(2,1)}, bf16[2,120,2048]{2,1,0:T(8,128)(2,1)S(1)}, u32[]{:S(2)}, u32[]{:S(2)}) %collective-permute-start.4) | collective-permute-done | bytes 983072 | tf_op jit(solution)/shard_map/ppermute | solution.py:54
  114.1 2.1 %collective-permute-start.8 = (bf16[120,2048]{1,0:T(8,128)(2,1)S(1)}, bf16[120,2048]{1,0:T(8,128)(2,1)S(1)}, u32[]{:S(2)}, u32[]{:S(2)}) collective-permute-start(bf16[120,2048]{1,0:T(8,128)(2,1)S(1)} %slice_bitcast_fusion), channel_id=1, source_target_pairs={{0,6},{1,7},{2,0},{3,1},{4,2},{5,3},{6,4},{7,5},{8,14},{9,15},{10,... | collective-permute-start | bytes 1474568 | tf_op jit(solution)/shard_map/ppermute | solution.py:54
  117.1 1.8 %collective-permute-start.5 = (bf16[2,120,2048]{2,1,0:T(8,128)(2,1)S(1)}, bf16[2,120,2048]{2,1,0:T(8,128)(2,1)}, u32[]{:S(2)}, u32[]{:S(2)}) collective-permute-start(bf16[2,120,2048]{2,1,0:T(8,128)(2,1)S(1)} %collective-permute-done.4.refs_4_), channel_id=1, source_target_pairs={{0,1},{1,0},{2,3},{3,2},{4,5},{5,4},{6,7},{7,6},{8,9},{9,8},{10,11... | collective-permute-start | bytes 2949128 | tf_op jit(solution)/shard_map/ppermute | solution.py:54
  118.9 7.0 %collective-permute-done.8 = bf16[120,2048]{1,0:T(8,128)(2,1)S(1)} collective-permute-done((bf16[120,2048]{1,0:T(8,128)(2,1)S(1)}, bf16[120,2048]{1,0:T(8,128)(2,1)S(1)}, u32[]{:S(2)}, u32[]{:S(2)}) %collective-permute-start.8) | collective-permute-done | bytes 491552 | tf_op jit(solution)/shard_map/ppermute | solution.py:54
  125.9 1.9 %collective-permute-start.3 = (bf16[2,120,2048]{2,1,0:T(8,128)(2,1)S(1)}, bf16[2,120,2048]{2,1,0:T(8,128)(2,1)}, u32[]{:S(2)}, u32[]{:S(2)}) collective-permute-start(bf16[2,120,2048]{2,1,0:T(8,128)(2,1)S(1)} %collective-permute-done.2.refs_2_), channel_id=1, source_target_pairs={{0,1},{1,0},{2,3},{3,2},{4,5},{5,4},{6,7},{7,6},{8,9},{9,8},{10,11... | collective-permute-start | bytes 2949128 | tf_op jit(solution)/shard_map/ppermute | solution.py:54
  127.8 1.3 collective-permute-done.7
  129.3 5.7 %collective-permute-done.11.refs_7_.refs_3_ = bf16[2048,256]{1,0:T(8,128)(2,1)} collective-permute-done((bf16[2048,256]{1,0:T(8,128)(2,1)}, bf16[2048,256]{1,0:T(8,128)(2,1)}, u32[]{:S(2)}, u32[]{:S(2)}) %collective-permute-start.11) | collective-permute-done | bytes 1048608 | tf_op jit(solution)/shard_map/ppermute | solution.py:54
  135.9 4.2 %collective-permute-done.10.refs_6_.refs_2_ = bf16[2048,256]{1,0:T(8,128)(2,1)} collective-permute-done((bf16[2048,256]{1,0:T(8,128)(2,1)}, bf16[2048,256]{1,0:T(8,128)(2,1)}, u32[]{:S(2)}, u32[]{:S(2)}) %collective-permute-start.10) | collective-permute-done | bytes 1048608 | tf_op jit(solution)/shard_map/ppermute | solution.py:54
  140.1 5.0 %chi_near_out.1 = bf16[6,120,256]{2,1,0:T(8,128)(2,1)} custom-call(bf16[2,120,2048]{2,1,0:T(8,128)(2,1)} %rho_rows.1.refs_0_, bf16[2,120,2048]{2,1,0:T(8,128)(2,1)} %copy-done.4, bf16[2,120,2048]{2,1,0:T(8,128)(2,1)} %copy-done.3, bf16[2,120,2048]{2,1,0:T(8,128)(2,1)} %collective-permute-done.3.refs_3_, bf16[2,120,2048]{2,1,0:T(8,128)(2,1)} %copy-done.2, ...), custom_call_target="tpu_custom_call" | custom-call | flops 1509949440 | bytes 7995392 | tf_op jit(solution)/shard_map/chi_near_out/pallas_call | solution.py:194
  146.3 3.2 %chi_far_out.1 = bf16[2,120,256]{2,1,0:T(8,128)(2,1)} custom-call(bf16[2,120,2048]{2,1,0:T(8,128)(2,1)} %copy-done.1, bf16[2,120,2048]{2,1,0:T(8,128)(2,1)} %collective-permute-done.9.refs_1_, bf16[2048,256]{1,0:T(8,128)(2,1)} %collective-permute-done.10.refs_6_.refs_2_, bf16[2048,256]{1,0:T(8,128)(2,1)} %collective-permute-done.11.refs_7_.refs_3_), custom_call_target="tpu_custom_call" | custom-call | flops 503316480 | bytes 4063232 | tf_op jit(solution)/shard_map/chi_far_out/pallas_call | solution.py:194
  149.5 1.0 collective-permute-start.13
  150.5 1.3 collective-permute-done.6.refs_7_.refs_3_
  151.8 5.2 %chi_near_in.1.ma = f32[6,120,256]{2,1,0:T(8,128)} custom-call(bf16[2,120,2048]{2,1,0:T(8,128)(2,1)} %rho_rows.1.refs_0_, bf16[2,120,2048]{2,1,0:T(8,128)(2,1)} %copy-done.4, bf16[2,120,2048]{2,1,0:T(8,128)(2,1)} %copy-done.3, bf16[2,120,2048]{2,1,0:T(8,128)(2,1)} %collective-permute-done.3.refs_3_, bf16[2,120,2048]{2,1,0:T(8,128)(2,1)} %copy-done.2, ...), custom_call_target="tpu_custom_call" | custom-call | flops 1509949440 | bytes 7995392 | tf_op jit(solution)/shard_map/chi_near_in/pallas_call | solution.py:194
  157.0 3.3 %chi_far_in.1.mb = f32[2,120,256]{2,1,0:T(8,128)} custom-call(bf16[2,120,2048]{2,1,0:T(8,128)(2,1)} %copy-done.1, bf16[2,120,2048]{2,1,0:T(8,128)(2,1)} %collective-permute-done.9.refs_1_, bf16[2048,256]{1,0:T(8,128)(2,1)} %slab_pairs.1.refs_6_.refs_2_, bf16[2048,256]{1,0:T(8,128)(2,1)} %collective-permute-done.6.refs_7_.refs_3_), custom_call_target="tpu_custom_call" | custom-call | flops 503316480 | bytes 4063232 | tf_op jit(solution)/shard_map/chi_far_in/pallas_call | solution.py:194
  161.0 6.9 %finish.1 = f32[16,120,256]{2,1,0:T(8,128)} custom-call(s32[9]{0:T(128)} %pad_add_fusion.1.place_ref, f32[16,120,256]{2,1,0:T(8,128)} %bitcast.33, f32[6,120,256]{2,1,0:T(8,128)} %chi_near_in.1.ma, f32[2,120,256]{2,1,0:T(8,128)} %chi_far_in.1.mb, bf16[6,120,256]{2,1,0:T(8,128)(2,1)} %copy-done.6, bf16[2,120,256]{2,1,0:T(8,128)(2,1)} %copy-done.7), custom_call_target="tpu_custom_call" | custom-call | bytes 6291456 | tf_op jit(solution)/shard_map/finish/pallas_call | solution.py:247
  (76 shorter events, 11.4 us)
Async XLA Ops:
  0.0 70.3 %copy-start = (f32[8,128]{1,0:T(8,128)S(1)}, f32[8,128]{1,0:T(8,128)}, u32[]{:S(2)}) copy-start(f32[8,128]{1,0:T(8,128)} %param.14) | copy-start | bytes 12292
  0.0 20.1 %copy-start.10 = (s32[2]{0:T(128)S(1)}, s32[2]{0:T(128)}, u32[]{:S(2)}) copy-start(s32[2]{0:T(128)} %param.17) | copy-start | bytes 28
  0.0 23.1 %copy-start.9 = (bf16[1,8192]{1,0:T(2,128)(2,1)S(1)}, bf16[1,8192]{1,0:T(2,128)(2,1)}, u32[]{:S(2)}) copy-start(bf16[1,8192]{1,0:T(2,128)(2,1)} %param.15) | copy-start | bytes 49156
  12.6 23.0 %all-to-all-start = ((bf16[8,8,8192]{2,1,0:T(8,128)(2,1)}), bf16[8,8,8192]{2,1,0:T(8,128)(2,1)S(1)}, u32[]{:S(2)}, u32[]{:S(2)}) async-start(bf16[8,8,8192]{2,1,0:T(8,128)(2,1)} %dynamic-slice_dynamic-update-slice_fusion.7), calls=%async_computation | async-start | bytes 2097152 | tf_op jit(solution)/shard_map/all_to_all | solution.py:281
  35.8 34.3 %copy-start.12 = (f32[16]{0:T(128)S(1)}, f32[16]{0:T(128)}, u32[]{:S(2)}) copy-start(f32[16]{0:T(128)} %param.16) | copy-start | bytes 196
  35.8 35.4 %copy-start.13 = (s32[120]{0:T(128)S(1)}, s32[120]{0:T(128)}, u32[]{:S(2)}) copy-start(s32[120]{0:T(128)} %param.18) | copy-start | bytes 1444
  67.0 8.3 %copy-start.5 = (bf16[8,16,8704]{2,1,0:T(8,128)(2,1)}, bf16[8,16,8704]{2,1,0:T(8,128)(2,1)S(1)}, u32[]{:S(2)}) copy-start(bf16[8,16,8704]{2,1,0:T(8,128)(2,1)S(1)} %all_to_all.10) | copy-start | bytes 6684676
  67.0 7.1 %collective-permute-start = (bf16[128,8704]{1,0:T(8,128)(2,1)S(1)}, bf16[128,8704]{1,0:T(8,128)(2,1)}, u32[]{:S(2)}, u32[]{:S(2)}) collective-permute-start(bf16[128,8704]{1,0:T(8,128)(2,1)S(1)} %bitcast.29), channel_id=1, source_target_pairs={{0,1},{1,0},{2,3},{3,2},{4,5},{5,4},{6,7},{7,6},{8,9},{9,8},{10,11... | collective-permute-start | bytes 6684680 | tf_op jit(solution)/shard_map/ppermute | solution.py:54
  75.3 0.7 copy-start.8
  76.0 15.6 %copy-start.11 = (s32[256]{0:T(256)S(1)}, s32[256]{0:T(256)}, u32[]{:S(2)}) copy-start(s32[256]{0:T(256)} %param.19) | copy-start | bytes 3076
  90.8 23.3 %collective-permute-start.4 = (bf16[2,120,2048]{2,1,0:T(8,128)(2,1)}, bf16[2,120,2048]{2,1,0:T(8,128)(2,1)S(1)}, u32[]{:S(2)}, u32[]{:S(2)}) collective-permute-start(bf16[2,120,2048]{2,1,0:T(8,128)(2,1)} %rho_rows.1.refs_0_), channel_id=1, source_target_pairs={{0,6},{1,7},{2,0},{3,1},{4,2},{5,3},{6,4},{7,5},{8,14},{9,15},{10,... | collective-permute-start | bytes 2949128 | tf_op jit(solution)/shard_map/ppermute | solution.py:54
  92.2 24.2 %collective-permute-start.2 = (bf16[2,120,2048]{2,1,0:T(8,128)(2,1)}, bf16[2,120,2048]{2,1,0:T(8,128)(2,1)S(1)}, u32[]{:S(2)}, u32[]{:S(2)}) collective-permute-start(bf16[2,120,2048]{2,1,0:T(8,128)(2,1)} %rho_rows.1.refs_0_), channel_id=1, source_target_pairs={{0,2},{1,3},{2,4},{3,5},{4,6},{5,7},{6,0},{7,1},{8,10},{9,11},{10,... | collective-permute-start | bytes 2949128 | tf_op jit(solution)/shard_map/ppermute | solution.py:54
  92.8 24.3 %collective-permute-start.1 = (bf16[2,120,2048]{2,1,0:T(8,128)(2,1)}, bf16[2,120,2048]{2,1,0:T(8,128)(2,1)S(1)}, u32[]{:S(2)}, u32[]{:S(2)}) collective-permute-start(bf16[2,120,2048]{2,1,0:T(8,128)(2,1)} %rho_rows.1.refs_0_), channel_id=1, source_target_pairs={{0,1},{1,0},{2,3},{3,2},{4,5},{5,4},{6,7},{7,6},{8,9},{9,8},{10,11... | collective-permute-start | bytes 2949128 | tf_op jit(solution)/shard_map/ppermute | solution.py:54
  108.7 26.3 %collective-permute-start.11 = (bf16[2048,256]{1,0:T(8,128)(2,1)}, bf16[2048,256]{1,0:T(8,128)(2,1)}, u32[]{:S(2)}, u32[]{:S(2)}) collective-permute-start(bf16[2048,256]{1,0:T(8,128)(2,1)} %slab_pairs.1.refs_6_.refs_2_), channel_id=1, source_target_pairs={{0,24},{1,25},{2,26},{3,27},{4,28},{5,29},{6,30},{7,31},{8,16},{9,... | collective-permute-start | bytes 3145736 | tf_op jit(solution)/shard_map/ppermute | solution.py:54
  114.0 26.1 %copy-start.2 = (bf16[2,120,2048]{2,1,0:T(8,128)(2,1)}, bf16[2,120,2048]{2,1,0:T(8,128)(2,1)S(1)}, u32[]{:S(2)}) copy-start(bf16[2,120,2048]{2,1,0:T(8,128)(2,1)S(1)} %collective-permute-done.4.refs_4_) | copy-start | bytes 2949124
  114.1 11.8 %collective-permute-start.8 = (bf16[120,2048]{1,0:T(8,128)(2,1)S(1)}, bf16[120,2048]{1,0:T(8,128)(2,1)S(1)}, u32[]{:S(2)}, u32[]{:S(2)}) collective-permute-start(bf16[120,2048]{1,0:T(8,128)(2,1)S(1)} %slice_bitcast_fusion), channel_id=1, source_target_pairs={{0,6},{1,7},{2,0},{3,1},{4,2},{5,3},{6,4},{7,5},{8,14},{9,15},{10,... | collective-permute-start | bytes 1474568 | tf_op jit(solution)/shard_map/ppermute | solution.py:54
  116.4 23.8 %copy-start.3 = (bf16[2,120,2048]{2,1,0:T(8,128)(2,1)}, bf16[2,120,2048]{2,1,0:T(8,128)(2,1)S(1)}, u32[]{:S(2)}) copy-start(bf16[2,120,2048]{2,1,0:T(8,128)(2,1)S(1)} %collective-permute-done.2.refs_2_) | copy-start | bytes 2949124
  116.4 12.7 %collective-permute-start.7 = (bf16[120,2048]{1,0:T(8,128)(2,1)S(1)}, bf16[120,2048]{1,0:T(8,128)(2,1)S(1)}, u32[]{:S(2)}, u32[]{:S(2)}) collective-permute-start(bf16[120,2048]{1,0:T(8,128)(2,1)S(1)} %slice_bitcast_fusion.1), channel_id=1, source_target_pairs={{0,2},{1,3},{2,4},{3,5},{4,6},{5,7},{6,0},{7,1},{8,10},{9,11},{10,... | collective-permute-start | bytes 1474568 | tf_op jit(solution)/shard_map/ppermute | solution.py:54
  116.5 23.6 %collective-permute-start.10 = (bf16[2048,256]{1,0:T(8,128)(2,1)}, bf16[2048,256]{1,0:T(8,128)(2,1)}, u32[]{:S(2)}, u32[]{:S(2)}) collective-permute-start(bf16[2048,256]{1,0:T(8,128)(2,1)} %slab_pairs.1.refs_6_.refs_2_), channel_id=1, source_target_pairs={{0,8},{1,9},{2,10},{3,11},{4,12},{5,13},{6,14},{7,15},{8,0},{9,1},... | collective-permute-start | bytes 3145736 | tf_op jit(solution)/shard_map/ppermute | solution.py:54
  117.1 12.2 %copy-start.4 = (bf16[2,120,2048]{2,1,0:T(8,128)(2,1)}, bf16[2,120,2048]{2,1,0:T(8,128)(2,1)S(1)}, u32[]{:S(2)}) copy-start(bf16[2,120,2048]{2,1,0:T(8,128)(2,1)S(1)} %collective-permute-done.1.refs_1_) | copy-start | bytes 2949124
  117.1 23.0 %collective-permute-start.5 = (bf16[2,120,2048]{2,1,0:T(8,128)(2,1)S(1)}, bf16[2,120,2048]{2,1,0:T(8,128)(2,1)}, u32[]{:S(2)}, u32[]{:S(2)}) collective-permute-start(bf16[2,120,2048]{2,1,0:T(8,128)(2,1)S(1)} %collective-permute-done.4.refs_4_), channel_id=1, source_target_pairs={{0,1},{1,0},{2,3},{3,2},{4,5},{5,4},{6,7},{7,6},{8,9},{9,8},{10,11... | collective-permute-start | bytes 2949128 | tf_op jit(solution)/shard_map/ppermute | solution.py:54
  125.9 14.2 %collective-permute-start.3 = (bf16[2,120,2048]{2,1,0:T(8,128)(2,1)S(1)}, bf16[2,120,2048]{2,1,0:T(8,128)(2,1)}, u32[]{:S(2)}, u32[]{:S(2)}) collective-permute-start(bf16[2,120,2048]{2,1,0:T(8,128)(2,1)S(1)} %collective-permute-done.2.refs_2_), channel_id=1, source_target_pairs={{0,1},{1,0},{2,3},{3,2},{4,5},{5,4},{6,7},{7,6},{8,9},{9,8},{10,11... | collective-permute-start | bytes 2949128 | tf_op jit(solution)/shard_map/ppermute | solution.py:54
  129.1 22.7 %collective-permute-start.6 = (bf16[2048,256]{1,0:T(8,128)(2,1)}, bf16[2048,256]{1,0:T(8,128)(2,1)}, u32[]{:S(2)}, u32[]{:S(2)}) collective-permute-start(bf16[2048,256]{1,0:T(8,128)(2,1)} %slab_pairs.1.refs_6_.refs_2_), channel_id=1, source_target_pairs={{0,32},{1,33},{2,34},{3,35},{4,36},{5,37},{6,38},{7,39},{8,40},{9,... | collective-permute-start | bytes 3145736 | tf_op jit(solution)/shard_map/ppermute | solution.py:54
  129.3 15.9 %copy-start.1 = (bf16[2,120,2048]{2,1,0:T(8,128)(2,1)}, bf16[2,120,2048]{2,1,0:T(8,128)(2,1)S(1)}, u32[]{:S(2)}) copy-start(bf16[2,120,2048]{2,1,0:T(8,128)(2,1)S(1)} %pad_maximum_fusion.refs_0_) | copy-start | bytes 2949124
  135.1 11.2 %collective-permute-start.9 = (bf16[2,120,2048]{2,1,0:T(8,128)(2,1)S(1)}, bf16[2,120,2048]{2,1,0:T(8,128)(2,1)}, u32[]{:S(2)}, u32[]{:S(2)}) collective-permute-start(bf16[2,120,2048]{2,1,0:T(8,128)(2,1)S(1)} %pad_maximum_fusion.refs_0_), channel_id=1, source_target_pairs={{0,1},{1,0},{2,3},{3,2},{4,5},{5,4},{6,7},{7,6},{8,9},{9,8},{10,11... | collective-permute-start | bytes 2949128 | tf_op jit(solution)/shard_map/ppermute | solution.py:54
  145.2 15.1 %collective-permute-start.12 = (bf16[6,120,256]{2,1,0:T(8,128)(2,1)}, bf16[6,120,256]{2,1,0:T(8,128)(2,1)S(1)}, u32[]{:S(2)}, u32[]{:S(2)}) collective-permute-start(bf16[6,120,256]{2,1,0:T(8,128)(2,1)} %chi_near_out.1), channel_id=1, source_target_pairs={{0,8},{1,9},{2,10},{3,11},{4,12},{5,13},{6,14},{7,15},{8,0},{9,1},... | collective-permute-start | bytes 1105928 | tf_op jit(solution)/shard_map/ppermute | solution.py:54
  149.5 10.8 %collective-permute-start.13 = (bf16[2,120,256]{2,1,0:T(8,128)(2,1)}, bf16[2,120,256]{2,1,0:T(8,128)(2,1)S(1)}, u32[]{:S(2)}, u32[]{:S(2)}) collective-permute-start(bf16[2,120,256]{2,1,0:T(8,128)(2,1)} %chi_far_out.1), channel_id=1, source_target_pairs={{0,8},{1,9},{2,10},{3,11},{4,12},{5,13},{6,14},{7,15},{8,0},{9,1},... | collective-permute-start | bytes 368648 | tf_op jit(solution)/shard_map/ppermute | solution.py:54
  160.2 0.7 copy-start.6
  160.3 0.8 copy-start.7

commit v2 on v1

v2 whole, which is shorter than its diff:
```python
import math

import jax
import jax.numpy as jnp
from jax import lax
from jax.experimental import pallas as pl
from jax.experimental.pallas import tpu as pltpu
from jax.sharding import PartitionSpec as P

BOX = 64
KC = 2048
VMEM = 56 * 1024 * 1024
BF = jnp.bfloat16
F32 = jnp.float32


def coulomb_root(box_index):
    plane_size = BOX * BOX
    half_box = BOX // 2
    leading = box_index // plane_size
    middle = box_index // BOX % BOX
    trailing = box_index % BOX

    def centred(offset_idx):
        return jnp.where(offset_idx >= half_box, offset_idx - BOX, offset_idx).astype(F32)

    length_sq = centred(leading) ** 2 + centred(middle) ** 2 + centred(trailing) ** 2
    return 32.0 / jnp.sqrt(length_sq + 64.0)


def linear(x, y, z, core):
    return ((x * 2 + y // 2) * 16) + (y % 2) * 8 + z * 2 + core


def route(step):
    pairs = []
    for x in range(4):
        for y in range(4):
            for z in range(4):
                for core in range(2):
                    pairs.append((linear(x, y, z, core), linear(*step(x, y, z, core))))
    return pairs


Z_UP = route(lambda x, y, z, c: (x, y, (z + 1) % 4, c))
Z_DOWN = route(lambda x, y, z, c: (x, y, (z + 3) % 4, c))
CORE = route(lambda x, y, z, c: (x, y, z, 1 - c))
X_PAIR = route(lambda x, y, z, c: (x ^ 1, y, z, c))
Y_PAIR = route(lambda x, y, z, c: (x, y ^ 1, z, c))
Y_CROSS = route(lambda x, y, z, c: (x, 3 - y, z, c))


def send(value, pairs):
    return lax.ppermute(value, ("band", "grow"), pairs)


def nt_dot(left, right):
    return lax.dot_general(left, right, (((1,), (1,)), ((), ())), preferred_element_type=F32)


def slab_body(val, cond, zeta, weight, root, out, acc):
    step = pl.program_id(0)
    conds = cond.shape[0]
    for c in range(0, conds, 4):
        lhs = jnp.concatenate([val[...] * cond[c + i : c + i + 1, :] for i in range(4)], axis=0)
        part = nt_dot(lhs, zeta[...])
        rows = slice(c * 128, (c + 4) * 128)
        acc[rows] = jnp.where(step == 0, part, acc[rows] + part)

    @pl.when(step == pl.num_programs(0) - 1)
    def _():
        out[...] = (acc[...] * root[...] * weight[...]).astype(BF)


def slab_kernel(val, cond, zeta, weight, root):
    conds, points = cond.shape
    pairs = conds * 128
    cols = zeta.shape[0]
    return pl.pallas_call(
        slab_body,
        grid=(points // KC,),
        in_specs=[
            pl.BlockSpec((128, KC), lambda k: (0, k)),
            pl.BlockSpec((conds, KC), lambda k: (0, k)),
            pl.BlockSpec((cols, KC), lambda k: (0, k)),
            pl.BlockSpec((pairs, 1), lambda k: (0, 0)),
            pl.BlockSpec((1, cols), lambda k: (0, 0)),
        ],
        out_specs=pl.BlockSpec((pairs, cols), lambda k: (0, 0)),
        out_shape=jax.ShapeDtypeStruct((pairs, cols), BF),
        scratch_shapes=[pltpu.VMEM((pairs, cols), F32)],
        compiler_params=pltpu.CompilerParams(vmem_limit_bytes=VMEM),
        cost_estimate=pl.CostEstimate(
            flops=2 * pairs * cols * points, bytes_accessed=8 << 20, transcendentals=0
        ),
        name="slab_pairs",
    )(val, cond, zeta, weight, root)


def rho_body(zeta, cond, val_a, val_b, root, out, lhs, rhs, acc):
    step = pl.program_id(0)
    conds = cond.shape[0]
    rows = zeta.shape[0]

    @pl.when(step == 0)
    def _():
        lhs[...] = jnp.zeros_like(lhs)

    rhs[0:128, :] = val_a[...]
    rhs[128:256, :] = val_b[...]
    lhs[0:rows, :] = zeta[...]
    for c in range(0, conds, 4):
        left = jnp.concatenate([lhs[...] * cond[c + i : c + i + 1, :] for i in range(4)], axis=0)
        part = nt_dot(left, rhs[...])
        span = slice(c * 128, (c + 4) * 128)
        acc[span] = jnp.where(step == 0, part, acc[span] + part)

    @pl.when(step == pl.num_programs(0) - 1)
    def _():
        for c in range(conds):
            block = acc[c * 128 : c * 128 + rows, :] * root[...]
            out[0, :, c * 128 : (c + 1) * 128] = block[:, 0:128].astype(BF)
            out[1, :, c * 128 : (c + 1) * 128] = block[:, 128:256].astype(BF)


def rho_kernel(zeta, cond, val_a, val_b, root):
    conds, points = cond.shape
    rows = zeta.shape[0]
    return pl.pallas_call(
        rho_body,
        grid=(points // KC,),
        in_specs=[
            pl.BlockSpec((rows, KC), lambda k: (0, k)),
            pl.BlockSpec((conds, KC), lambda k: (0, k)),
            pl.BlockSpec((128, KC), lambda k: (0, k)),
            pl.BlockSpec((128, KC), lambda k: (0, k)),
            pl.BlockSpec((rows, 1), lambda k: (0, 0)),
        ],
        out_specs=pl.BlockSpec((2, rows, conds * 128), lambda k: (0, 0, 0)),
        out_shape=jax.ShapeDtypeStruct((2, rows, conds * 128), BF),
        scratch_shapes=[
            pltpu.VMEM((128, KC), BF),
            pltpu.VMEM((256, KC), BF),
            pltpu.VMEM((conds * 128, 256), F32),
        ],
        compiler_params=pltpu.CompilerParams(vmem_limit_bytes=VMEM),
        cost_estimate=pl.CostEstimate(
            flops=2 * conds * 128 * 256 * points, bytes_accessed=8 << 20, transcendentals=0
        ),
        name="rho_rows",
    )(zeta, cond, val_a, val_b, root)


def chi_kernel(arrays, parts, slab_a, slab_b, out_dtype, name):
    rows, depth = arrays[0].shape[-2:]
    cols = slab_a.shape[1]
    given, count = len(arrays), len(parts)
    blk = 1024

    def body(*refs):
        ins = refs[:given]
        slab_0, slab_1, out, lhs, acc = refs[given:]
        step = pl.program_id(0)

        @pl.when(step == 0)
        def _():
            lhs[...] = jnp.zeros_like(lhs)
            acc[...] = jnp.zeros_like(acc)

        total = acc[...]
        for half, slab in ((0, slab_0), (1, slab_1)):
            for i in range(count):
                array, index = parts[i][half]
                block = ins[array][...] if index is None else ins[array][index]
                lhs[half, i * 128 : i * 128 + rows, :] = block
            total += jnp.dot(lhs[half], slab[...], preferred_element_type=F32)
        acc[...] = total

        @pl.when(step == pl.num_programs(0) - 1)
        def _():
            for i in range(count):
                out[i] = acc[i * 128 : i * 128 + rows, :].astype(out_dtype)

    def spec(array):
        if array.ndim == 3:
            return pl.BlockSpec((2, rows, blk), lambda k: (0, 0, k))
        return pl.BlockSpec((rows, blk), lambda k: (0, k))

    return pl.pallas_call(
        body,
        grid=(depth // blk,),
        in_specs=[spec(a) for a in arrays] + [pl.BlockSpec((blk, cols), lambda k: (k, 0))] * 2,
        out_specs=pl.BlockSpec((count, rows, cols), lambda k: (0, 0, 0)),
        out_shape=jax.ShapeDtypeStruct((count, rows, cols), out_dtype),
        scratch_shapes=[
            pltpu.VMEM((2, count * 128, blk), BF),
            pltpu.VMEM((count * 128, cols), F32),
        ],
        compiler_params=pltpu.CompilerParams(vmem_limit_bytes=VMEM),
        cost_estimate=pl.CostEstimate(
            flops=2 * count * rows * cols * 2 * depth,
            bytes_accessed=count * rows * depth * 4 + depth * cols * 4,
            transcendentals=0,
        ),
        name=name,
    )(*arrays, slab_a, slab_b)


def finish_kernel(place, chi, mine, theirs, before, name):
    blocks, rows, cols = chi.shape
    count = mine.shape[0] // 2

    def body(place_ref, chi_ref, mine_ref, theirs_ref, *rest):
        out = rest[-1]
        step = pl.program_id(0)
        core = place_ref[2 * count]
        for first, src in ((0, mine_ref), (count, theirs_ref)):

            @pl.when(jnp.logical_and(step >= first, step < first + count))
            def _(src=src):
                out[core] = chi_ref[core] - src[0].astype(F32)
                out[1 - core] = chi_ref[1 - core] - src[1].astype(F32)

    def where(i, place_ref):
        return (place_ref[i], 0, 0)

    block = (2, rows, cols)
    specs = [
        pl.BlockSpec(block, where),
        pl.BlockSpec(block, lambda i, place_ref: (jnp.minimum(i, count - 1), 0, 0)),
        pl.BlockSpec(block, lambda i, place_ref: (jnp.maximum(i - count, 0), 0, 0)),
    ]
    operands = [place, chi, mine, theirs]
    if before is not None:
        specs.append(pl.BlockSpec(memory_space=pl.ANY))
        operands.append(before)
    return pl.pallas_call(
        body,
        grid_spec=pltpu.PrefetchScalarGridSpec(
            num_scalar_prefetch=1,
            grid=(2 * count,),
            in_specs=specs,
            out_specs=pl.BlockSpec(block, where),
        ),
        out_shape=jax.ShapeDtypeStruct(chi.shape, F32),
        input_output_aliases={} if before is None else {4: 0},
        compiler_params=pltpu.CompilerParams(vmem_limit_bytes=VMEM),
        cost_estimate=pl.CostEstimate(flops=0, bytes_accessed=count << 20, transcendentals=0),
        name=name,
    )(*operands)


def on_device(
    chi_prev,
    zeta_rows,
    zeta_slab,
    valence_store,
    valence_energy,
    conduction,
    conduction_energy,
    owners,
    gmap_rows,
    gmap_slab,
):
    band = lax.axis_index("band")
    grow = lax.axis_index("grow")
    core = grow % 2
    yz = grow // 2
    turn = (band // 2 + band % 2) % 2
    points = valence_store.shape[2]

    groups = [list(range(0, 16, 2)), list(range(1, 16, 2))]

    def over_plane(value):
        copies = jnp.broadcast_to(value[None], (8,) + value.shape)
        return lax.all_to_all(
            copies, "grow", split_axis=0, concat_axis=0, tiled=True, axis_index_groups=groups
        )

    cond_mine = over_plane(conduction).reshape(8, points)
    cond_other = send(cond_mine, CORE)
    cond = jnp.concatenate(
        [
            jnp.where(core == 0, cond_mine, cond_other),
            jnp.where(core == 0, cond_other, cond_mine),
        ],
        axis=0,
    )

    store = valence_store[0]
    piece_a = lax.dynamic_slice_in_dim(store, yz * 16 + core * 8, 8, 0)
    piece_b = lax.dynamic_slice_in_dim(store, yz * 16 + (1 - core) * 8, 8, 0)
    turns = jnp.array([(b // 2 + b % 2) % 2 for b in range(8)])
    pieces = jnp.where(turns[:, None, None] == 1, piece_b[None], piece_a[None])
    panels = lax.all_to_all(pieces, "band", split_axis=0, concat_axis=0, tiled=True)
    chosen = jnp.concatenate(
        [lax.dynamic_slice_in_dim(panels, owners[i], 1, 0)[0] for i in range(2)], axis=0
    )

    energy_c = conduction_energy.reshape(8, 2).T.reshape(16)
    energy_v = jnp.take(valence_energy, owners, axis=0).reshape(2, 8, 2, 8)
    half = (core + turn) % 2
    energy_v = lax.dynamic_index_in_dim(energy_v, half, 2, keepdims=False)
    energy_v = energy_v.transpose(1, 0, 2).reshape(128)
    weight = (4.0 / math.sqrt(4096)) / (energy_c[:, None] - energy_v[None, :])

    weight = weight.reshape(2048, 1)
    root_rows = coulomb_root(gmap_rows)[:, None]
    root_slab = coulomb_root(gmap_slab)[None, :]
    chosen, weight, root_rows, root_slab, cond = lax.optimization_barrier(
        (chosen, weight, root_rows, root_slab, cond)
    )
    mine = over_plane(chosen).reshape(128, points)
    other = send(mine, CORE)

    rho = rho_kernel(zeta_rows, cond, mine, other, root_rows)
    slab_pp = slab_kernel(mine, cond, zeta_slab, weight, root_slab)

    from_down = send(rho, Z_UP)
    from_up = send(rho, Z_DOWN)
    rho_x = send(rho, CORE)
    slab_px = send(slab_pp, X_PAIR)
    slab_yp = send(slab_pp, Y_PAIR)
    slab_yx = send(slab_pp, Y_CROSS)
    far_0 = send(from_down[0], Z_UP)
    far_1 = send(from_up[1], Z_DOWN)
    from_down_x = send(from_down, CORE)
    from_up_x = send(from_up, CORE)
    far_0x = send(far_0, CORE)
    far_1x = send(far_1, CORE)

    near = [rho, rho_x, from_down, from_down_x, from_up, from_up_x]
    near_parts = [((i, i % 2), (i, 1 - i % 2)) for i in range(6)]
    rest = [far_0, far_1, far_0x, far_1x]
    rest_parts = [((0, None), (1, None)), ((3, None), (2, None))]
    near_out = chi_kernel(near, near_parts, slab_yp, slab_yx, BF, "chi_near_out")
    near_in = chi_kernel(near, near_parts, slab_pp, slab_px, F32, "chi_near_in")
    got_near = send(near_out, Y_PAIR)
    rest_out = chi_kernel(rest, rest_parts, slab_yp, slab_yx, BF, "chi_far_out")
    got_rest = send(rest_out, Y_PAIR)
    rest_in = chi_kernel(rest, rest_parts, slab_pp, slab_px, F32, "chi_far_in")

    yl = grow // 8
    z = yz % 4
    own_side, other_side = yl * 4, (1 - yl) * 4
    slots = jnp.stack([z, (z + 3) % 4, (z + 1) % 4]).astype(jnp.int32)
    place_near = jnp.concatenate([own_side + slots, other_side + slots, core[None]])
    opposite = (z + 2) % 4
    place_far = jnp.stack([own_side + opposite, other_side + opposite, core])
    total_rows, cols = chi_prev.shape
    chi = chi_prev.reshape(16, total_rows // 16, cols)
    done = finish_kernel(place_near.astype(jnp.int32), chi, near_in, got_near, None, "finish_near")
    done = finish_kernel(place_far.astype(jnp.int32), chi, rest_in, got_rest, done, "finish_far")
    return done.reshape(total_rows, cols)


def solution(mesh):
    placed = (
        P("band", "grow"),
        P(("band", "grow"), None),
        P("grow", None),
        P("band", None, None),
        P(),
        P("grow", None),
        P(),
        P(),
        P(("band", "grow")),
        P("grow"),
    )
    return jax.shard_map(
        on_device, mesh=mesh, in_specs=placed, out_specs=P("band", "grow"), check_vma=False
    )
```

time: 171 us -> 181 us (1.058); the launches traced: 168 us -> 181 us
  waiting for transfers between devices: 35.4 us -> 44.7 us
  starting transfers between devices: 23.2 us -> 30.8 us
  other arithmetic: 2.61 us -> 8.47 us
  local copies, waits for them, and re-layouts: 18.3 us -> 13.7 us
  Pallas kernels: 53.3 us -> 50.5 us
  blocking collectives: 31.2 us -> 28.8 us
    unnamed x36 -> x31, local copies, waits for them, and re-layouts: 12.6 us -> 4.95 us
    ppermute x14 -> x16, waiting for transfers between devices: 24.3 us -> 31.8 us  [send(): return lax.ppermute(value, ('band', 'grow'), pairs)]
    all_to_all x0 -> x1, starting transfers between devices: none -> 6.88 us  [over_plane(): lax.all_to_all(copies, 'grow', split_axis=0, concat_axis=0, tiled=True, a...]
    pallas_call x1, Pallas kernels: 14.8 us -> 12.3 us  [rho_kernel(): pl.pallas_call(rho_body, grid=(points // KC,), in_specs=[pl.BlockSpec((ro...]
    all_to_all x1, blocking collectives: 31.2 us -> 28.8 us  [over_plane(): lax.all_to_all(copies, 'grow', split_axis=0, concat_axis=0, tiled=True, a...]
    pallas_call x1, Pallas kernels: 14.9 us -> 12.7 us  [slab_kernel(): pl.pallas_call(slab_body, grid=(points // KC,), in_specs=[pl.BlockSpec((1...]
    optimization_barrier x0 -> x2, local copies, waits for them, and re-layouts: none -> 2.08 us  [on_device(): lax.optimization_barrier((chosen, weight, root_rows, root_slab, cond))]
    ppermute x14 -> x16, starting transfers between devices: 15.8 us -> 17.6 us  [send(): return lax.ppermute(value, ('band', 'grow'), pairs)]
  transfers between devices with their start and end apart: 15 -> 18, of which waited for: 9 -> 7; matrix products, arithmetic and copies ran while one was open for 3% -> 7% of each run, Pallas kernels for 19% -> 20%
where the time goes in v2:
time: 181 us
  Pallas kernels  50.5 us (28%)
  waiting for transfers between devices  44.7 us (25%)
  starting transfers between devices  30.8 us (17%)
  blocking collectives  28.8 us (16%)
  local copies, waits for them, and re-layouts  13.7 us (8%)
  other arithmetic  8.47 us (5%)
  between operations  3.86 us (2%)
    ppermute x16, waiting for transfers between devices, send(): return lax.ppermute(value, ('band', 'grow'), pairs)  31.8 us
    all_to_all x1, blocking collectives, over_plane(): lax.all_to_all(copies, 'grow', split_axis=0, concat_axis=0, tiled=True, a...  28.8 us
    ppermute x16, starting transfers between devices, send(): return lax.ppermute(value, ('band', 'grow'), pairs)  17.6 us
    pallas_call x4, Pallas kernels, chi_kernel(): pl.pallas_call(body, grid=(depth // blk,), in_specs=[spec(a) for a in arr...  17.1 us
    all_to_all x1, waiting for transfers between devices, on_device(): lax.all_to_all(pieces, 'band', split_axis=0, concat_axis=0, tiled=True)  12.9 us
    pallas_call x1, Pallas kernels, slab_kernel(): pl.pallas_call(slab_body, grid=(points // KC,), in_specs=[pl.BlockSpec((1...  12.7 us
    pallas_call x1, Pallas kernels, rho_kernel(): pl.pallas_call(rho_body, grid=(points // KC,), in_specs=[pl.BlockSpec((ro...  12.3 us
    pallas_call x2, Pallas kernels, finish_kernel(): pl.pallas_call(body, grid_spec=pltpu.PrefetchScalarGridSpec(num_scalar_pr...  8.33 us
  transfers between devices with their start and end apart: 18, of which 7 were waited for; matrix products, arithmetic and copies ran while one was open for 7% of the time, Pallas kernels for 20%

profile of v2, /device:TPU:1, one launch (start us, length us, event | category | flops | bytes accessed | tf_op | source)
XLA Modules:
  0.0 180.7 jit_solution(5350750419559009119)
XLA Ops:
  1.5 1.4 reduce.1
  3.7 6.9 %all-to-all-start.1 = ((bf16[8,2,4096]{2,1,0:T(2,128)(2,1)}), bf16[8,2,4096]{2,1,0:T(2,128)(2,1)S(1)}, u32[]{:S(2)}, u32[]{:S(2)}) async-start(bf16[8,2,4096]{2,1,0:T(2,128)(2,1)} %reshape.82), calls=%async_computation.1 | async-start | bytes 262144 | tf_op jit(solution)/shard_map/all_to_all | solution.py:276
  10.6 1.3 fusion.17
  18.8 1.0 dynamic-slice_bitcast_fusion.3
  19.8 1.8 broadcast_select_fusion
  22.2 6.4 %all-to-all-start = ((bf16[8,8,8192]{2,1,0:T(8,128)(2,1)}), bf16[8,8,8192]{2,1,0:T(8,128)(2,1)S(1)}, u32[]{:S(2)}, u32[]{:S(2)}) async-start(bf16[8,8,8192]{2,1,0:T(8,128)(2,1)} %broadcast_select_fusion), calls=%async_computation | async-start | bytes 2097152 | tf_op jit(solution)/shard_map/all_to_all | solution.py:295
  28.8 1.3 collective-permute-start
  31.3 12.9 %all-to-all-done = bf16[8,8,8192]{2,1,0:T(8,128)(2,1)S(1)} async-done(((bf16[8,8,8192]{2,1,0:T(8,128)(2,1)}), bf16[8,8,8192]{2,1,0:T(8,128)(2,1)S(1)}, u32[]{:S(2)}, u32[]{:S(2)}) %all-to-all-start) | async-done | bytes 1048608 | tf_op jit(solution)/shard_map/all_to_all | solution.py:295
  45.1 28.8 %all_to_all.15 = bf16[8,16,8192]{2,1,0:T(8,128)(2,1)S(1)} all-to-all(bf16[8,16,8192]{2,1,0:T(8,128)(2,1)S(1)} %broadcast_in_dim.76), channel_id=1, replica_groups={{0,2,4,6,8,10,12,14},{1,3,5,7,9,11,13,15},{16,18,20,22,24,26,28,30},{17..., dimensions={0} | all-to-all | bytes 4194304 | tf_op jit(solution)/shard_map/all_to_all | solution.py:276
  73.9 3.2 %collective-permute-start.1 = (bf16[128,8192]{1,0:T(8,128)(2,1)S(1)}, bf16[128,8192]{1,0:T(8,128)(2,1)}, u32[]{:S(2)}, u32[]{:S(2)}) collective-permute-start(bf16[128,8192]{1,0:T(8,128)(2,1)S(1)} %bitcast.39), channel_id=1, source_target_pairs={{0,1},{1,0},{2,3},{3,2},{4,5},{5,4},{6,7},{7,6},{8,9},{9,8},{10,11... | collective-permute-start | bytes 6291464 | tf_op jit(solution)/shard_map/ppermute | solution.py:54
  77.8 3.2 %collective-permute-done.1.val_b = bf16[128,8192]{1,0:T(8,128)(2,1)} collective-permute-done((bf16[128,8192]{1,0:T(8,128)(2,1)S(1)}, bf16[128,8192]{1,0:T(8,128)(2,1)}, u32[]{:S(2)}, u32[]{:S(2)}) %collective-permute-start.1) | collective-permute-done | bytes 2097184 | tf_op jit(solution)/shard_map/ppermute | solution.py:54
  81.0 12.3 %rho_rows.1.refs_0_ = bf16[2,120,2048]{2,1,0:T(8,128)(2,1)} custom-call(bf16[120,8192]{1,0:T(8,128)(2,1)} %zeta.2, bf16[16,8192]{1,0:T(8,128)(2,1)} %get-tuple-element.10.cond, bf16[128,8192]{1,0:T(8,128)(2,1)} %bitcast.40, bf16[128,8192]{1,0:T(8,128)(2,1)} %collective-permute-done.1.val_b, f32[120,1]{1,0:T(8,128)} %copy.30.root), custom_call_target="tpu_custom_call" | custom-call | flops 8589934592 | bytes 8388608 | tf_op jit(solution)/shard_map/rho_rows/pallas_call | solution.py:129
  93.3 2.7 %collective-permute-start.4 = (bf16[2,120,2048]{2,1,0:T(8,128)(2,1)}, bf16[2,120,2048]{2,1,0:T(8,128)(2,1)S(1)}, u32[]{:S(2)}, u32[]{:S(2)}) collective-permute-start(bf16[2,120,2048]{2,1,0:T(8,128)(2,1)} %rho_rows.1.refs_0_), channel_id=1, source_target_pairs={{0,6},{1,7},{2,0},{3,1},{4,2},{5,3},{6,4},{7,5},{8,14},{9,15},{10,... | collective-permute-start | bytes 2949128 | tf_op jit(solution)/shard_map/ppermute | solution.py:54
  96.0 1.3 copy.31.weight
  97.4 12.7 %slab_pairs.1.refs_4_.refs_6_ = bf16[2048,256]{1,0:T(8,128)(2,1)} custom-call(bf16[128,8192]{1,0:T(8,128)(2,1)} %bitcast.41, bf16[16,8192]{1,0:T(8,128)(2,1)} %get-tuple-element.10.cond, bf16[256,8192]{1,0:T(8,128)(2,1)} %zeta.3, f32[2048,1]{1,0:T(8,128)} %copy.31.weight, f32[1,256]{1,0:T(1,128)} %bitcast.45), custom_call_target="tpu_custom_call" | custom-call | flops 8589934592 | bytes 8388608 | tf_op jit(solution)/shard_map/slab_pairs/pallas_call | solution.py:79
  110.4 1.5 collective-permute-start.10
  111.9 1.5 collective-permute-start.12
  113.4 4.4 %collective-permute-done.2.refs_2_ = bf16[2,120,2048]{2,1,0:T(8,128)(2,1)S(1)} collective-permute-done((bf16[2,120,2048]{2,1,0:T(8,128)(2,1)}, bf16[2,120,2048]{2,1,0:T(8,128)(2,1)S(1)}, u32[]{:S(2)}, u32[]{:S(2)}) %collective-permute-start.2) | collective-permute-done | bytes 983072 | tf_op jit(solution)/shard_map/ppermute | solution.py:54
  117.8 1.1 collective-permute-start.13
  120.8 13.3 %collective-permute-done.9.refs_4_.refs_6_ = bf16[2048,256]{1,0:T(8,128)(2,1)S(1)} collective-permute-done((bf16[2048,256]{1,0:T(8,128)(2,1)}, bf16[2048,256]{1,0:T(8,128)(2,1)S(1)}, u32[]{:S(2)}, u32[]{:S(2)}) %collective-permute-start.9) | collective-permute-done | bytes 1048608 | tf_op jit(solution)/shard_map/ppermute | solution.py:54
  134.1 1.3 collective-permute-done.10.refs_5_.refs_7_
  135.4 1.4 collective-permute-start.5
  136.8 1.0 copy-done.5
  137.9 8.6 %collective-permute-done.3.refs_0_ = bf16[120,2048]{1,0:T(8,128)(2,1)S(1)} collective-permute-done((bf16[120,2048]{1,0:T(8,128)(2,1)}, bf16[120,2048]{1,0:T(8,128)(2,1)S(1)}, u32[]{:S(2)}, u32[]{:S(2)}) %collective-permute-start.3) | collective-permute-done | bytes 491552 | tf_op jit(solution)/shard_map/ppermute | solution.py:54
  146.5 2.7 %collective-permute-start.6 = (bf16[120,2048]{1,0:T(8,128)(2,1)S(1)}, bf16[120,2048]{1,0:T(8,128)(2,1)S(1)}, u32[]{:S(2)}, u32[]{:S(2)}) collective-permute-start(bf16[120,2048]{1,0:T(8,128)(2,1)S(1)} %collective-permute-done.3.refs_0_), channel_id=1, source_target_pairs={{0,1},{1,0},{2,3},{3,2},{4,5},{5,4},{6,7},{7,6},{8,9},{9,8},{10,11... | collective-permute-start | bytes 1474568 | tf_op jit(solution)/shard_map/ppermute | solution.py:54
  149.5 5.0 %chi_near_out.1 = bf16[6,120,256]{2,1,0:T(8,128)(2,1)} custom-call(bf16[2,120,2048]{2,1,0:T(8,128)(2,1)} %rho_rows.1.refs_0_, bf16[2,120,2048]{2,1,0:T(8,128)(2,1)} %copy-done.5, bf16[2,120,2048]{2,1,0:T(8,128)(2,1)} %copy-done.1, bf16[2,120,2048]{2,1,0:T(8,128)(2,1)} %collective-permute-done.13.refs_3_, bf16[2,120,2048]{2,1,0:T(8,128)(2,1)} %copy-done.2, ...), custom_call_target="tpu_custom_call" | custom-call | flops 1509949440 | bytes 7995392 | tf_op jit(solution)/shard_map/chi_near_out/pallas_call | solution.py:189
  157.9 3.4 %chi_far_out.1 = bf16[2,120,256]{2,1,0:T(8,128)(2,1)} custom-call(bf16[120,2048]{1,0:T(8,128)(2,1)} %copy-done.7, bf16[120,2048]{1,0:T(8,128)(2,1)} %collective-permute-done.5.refs_1_, bf16[120,2048]{1,0:T(8,128)(2,1)} %copy-done.8, bf16[120,2048]{1,0:T(8,128)(2,1)} %copy-done.9, bf16[2048,256]{1,0:T(8,128)(2,1)} %copy-done.3, ...), custom_call_target="tpu_custom_call" | custom-call | flops 503316480 | bytes 4063232 | tf_op jit(solution)/shard_map/chi_far_out/pallas_call | solution.py:189
  161.2 1.1 collective-permute-start.11
  162.3 3.4 %chi_far_in.1.mine_ref = f32[2,120,256]{2,1,0:T(8,128)} custom-call(bf16[120,2048]{1,0:T(8,128)(2,1)} %copy-done.7, bf16[120,2048]{1,0:T(8,128)(2,1)} %collective-permute-done.5.refs_1_, bf16[120,2048]{1,0:T(8,128)(2,1)} %copy-done.8, bf16[120,2048]{1,0:T(8,128)(2,1)} %copy-done.9, bf16[2048,256]{1,0:T(8,128)(2,1)} %slab_pairs.1.refs_4_.refs_6_, ...), custom_call_target="tpu_custom_call" | custom-call | flops 503316480 | bytes 4063232 | tf_op jit(solution)/shard_map/chi_far_in/pallas_call | solution.py:189
  165.7 5.2 %chi_near_in.1.mine_ref = f32[6,120,256]{2,1,0:T(8,128)} custom-call(bf16[2,120,2048]{2,1,0:T(8,128)(2,1)} %rho_rows.1.refs_0_, bf16[2,120,2048]{2,1,0:T(8,128)(2,1)} %copy-done.5, bf16[2,120,2048]{2,1,0:T(8,128)(2,1)} %copy-done.1, bf16[2,120,2048]{2,1,0:T(8,128)(2,1)} %collective-permute-done.13.refs_3_, bf16[2,120,2048]{2,1,0:T(8,128)(2,1)} %copy-done.2, ...), custom_call_target="tpu_custom_call" | custom-call | flops 1509949440 | bytes 7995392 | tf_op jit(solution)/shard_map/chi_near_in/pallas_call | solution.py:189
  171.7 5.7 %finish_near.1.rest_0_ = f32[16,120,256]{2,1,0:T(8,128)} custom-call(s32[7]{0:T(128)} %pad_add_fusion.2.place_ref, f32[16,120,256]{2,1,0:T(8,128)} %bitcast.37, f32[6,120,256]{2,1,0:T(8,128)} %chi_near_in.1.mine_ref, bf16[6,120,256]{2,1,0:T(8,128)(2,1)} %copy-done.10), custom_call_target="tpu_custom_call" | custom-call | bytes 3145728 | tf_op jit(solution)/shard_map/finish_near/pallas_call | solution.py:237
  178.0 2.7 %finish_far.1 = f32[16,120,256]{2,1,0:T(8,128)} custom-call(s32[3]{0:T(128)} %pad_add_fusion.place_ref, f32[16,120,256]{2,1,0:T(8,128)} %bitcast.38, f32[2,120,256]{2,1,0:T(8,128)} %chi_far_in.1.mine_ref, bf16[2,120,256]{2,1,0:T(8,128)(2,1)} %copy-done.11, f32[16,120,256]{2,1,0:T(8,128)} %finish_near.1.rest_0_), custom_call_target="tpu_custom_call", output_to_operand_aliasing={{}: (4, {})} | custom-call | bytes 1048576 | tf_op jit(solution)/shard_map/finish_far/pallas_call | solution.py:237
  (78 shorter events, 16.5 us)
Async XLA Ops:
  0.0 15.7 %copy-start = (f32[8,128]{1,0:T(8,128)S(1)}, f32[8,128]{1,0:T(8,128)}, u32[]{:S(2)}) copy-start(f32[8,128]{1,0:T(8,128)} %param.15) | copy-start | bytes 12292
  0.0 21.5 %copy-start.12 = (s32[256]{0:T(256)S(1)}, s32[256]{0:T(256)}, u32[]{:S(2)}) copy-start(s32[256]{0:T(256)} %param.20) | copy-start | bytes 3076
  3.7 18.5 %all-to-all-start.1 = ((bf16[8,2,4096]{2,1,0:T(2,128)(2,1)}), bf16[8,2,4096]{2,1,0:T(2,128)(2,1)S(1)}, u32[]{:S(2)}, u32[]{:S(2)}) async-start(bf16[8,2,4096]{2,1,0:T(2,128)(2,1)} %reshape.82), calls=%async_computation.1 | async-start | bytes 262144 | tf_op jit(solution)/shard_map/all_to_all | solution.py:276
  19.8 10.4 %copy-start.13 = (s32[120]{0:T(128)S(1)}, s32[120]{0:T(128)}, u32[]{:S(2)}) copy-start(s32[120]{0:T(128)} %param.19) | copy-start | bytes 1444
  22.2 22.0 %all-to-all-start = ((bf16[8,8,8192]{2,1,0:T(8,128)(2,1)}), bf16[8,8,8192]{2,1,0:T(8,128)(2,1)S(1)}, u32[]{:S(2)}, u32[]{:S(2)}) async-start(bf16[8,8,8192]{2,1,0:T(8,128)(2,1)} %broadcast_select_fusion), calls=%async_computation | async-start | bytes 2097152 | tf_op jit(solution)/shard_map/all_to_all | solution.py:295
  28.8 2.3 %collective-permute-start = (bf16[8,8192]{1,0:T(8,128)(2,1)S(1)}, bf16[8,8192]{1,0:T(8,128)(2,1)S(1)}, u32[]{:S(2)}, u32[]{:S(2)}) collective-permute-start(bf16[8,8192]{1,0:T(8,128)(2,1)S(1)} %bitcast.42), channel_id=1, source_target_pairs={{0,1},{1,0},{2,3},{3,2},{4,5},{5,4},{6,7},{7,6},{8,9},{9,8},{10,11... | collective-permute-start | bytes 393224 | tf_op jit(solution)/shard_map/ppermute | solution.py:54
  73.9 7.1 %copy-start.6 = (bf16[8,16,8192]{2,1,0:T(8,128)(2,1)}, bf16[8,16,8192]{2,1,0:T(8,128)(2,1)S(1)}, u32[]{:S(2)}) copy-start(bf16[8,16,8192]{2,1,0:T(8,128)(2,1)S(1)} %all_to_all.15) | copy-start | bytes 6291460
  73.9 7.1 %collective-permute-start.1 = (bf16[128,8192]{1,0:T(8,128)(2,1)S(1)}, bf16[128,8192]{1,0:T(8,128)(2,1)}, u32[]{:S(2)}, u32[]{:S(2)}) collective-permute-start(bf16[128,8192]{1,0:T(8,128)(2,1)S(1)} %bitcast.39), channel_id=1, source_target_pairs={{0,1},{1,0},{2,3},{3,2},{4,5},{5,4},{6,7},{7,6},{8,9},{9,8},{10,11... | collective-permute-start | bytes 6291464 | tf_op jit(solution)/shard_map/ppermute | solution.py:54
  93.3 24.5 %collective-permute-start.2 = (bf16[2,120,2048]{2,1,0:T(8,128)(2,1)}, bf16[2,120,2048]{2,1,0:T(8,128)(2,1)S(1)}, u32[]{:S(2)}, u32[]{:S(2)}) collective-permute-start(bf16[2,120,2048]{2,1,0:T(8,128)(2,1)} %rho_rows.1.refs_0_), channel_id=1, source_target_pairs={{0,2},{1,3},{2,4},{3,5},{4,6},{5,7},{6,0},{7,1},{8,10},{9,11},{10,... | collective-permute-start | bytes 2949128 | tf_op jit(solution)/shard_map/ppermute | solution.py:54
  93.3 25.6 %collective-permute-start.4 = (bf16[2,120,2048]{2,1,0:T(8,128)(2,1)}, bf16[2,120,2048]{2,1,0:T(8,128)(2,1)S(1)}, u32[]{:S(2)}, u32[]{:S(2)}) collective-permute-start(bf16[2,120,2048]{2,1,0:T(8,128)(2,1)} %rho_rows.1.refs_0_), channel_id=1, source_target_pairs={{0,6},{1,7},{2,0},{3,1},{4,2},{5,3},{6,4},{7,5},{8,14},{9,15},{10,... | collective-permute-start | bytes 2949128 | tf_op jit(solution)/shard_map/ppermute | solution.py:54
  97.4 14.6 %copy-start.4 = (bf16[2,120,2048]{2,1,0:T(8,128)(2,1)S(1)}, bf16[2,120,2048]{2,1,0:T(8,128)(2,1)}, u32[]{:S(2)}) copy-start(bf16[2,120,2048]{2,1,0:T(8,128)(2,1)} %rho_rows.1.refs_0_) | copy-start | bytes 2949124
  110.1 24.0 %collective-permute-start.9 = (bf16[2048,256]{1,0:T(8,128)(2,1)}, bf16[2048,256]{1,0:T(8,128)(2,1)S(1)}, u32[]{:S(2)}, u32[]{:S(2)}) collective-permute-start(bf16[2048,256]{1,0:T(8,128)(2,1)} %slab_pairs.1.refs_4_.refs_6_), channel_id=1, source_target_pairs={{0,8},{1,9},{2,10},{3,11},{4,12},{5,13},{6,14},{7,15},{8,0},{9,1},... | collective-permute-start | bytes 3145736 | tf_op jit(solution)/shard_map/ppermute | solution.py:54
  110.4 25.0 %collective-permute-start.10 = (bf16[2048,256]{1,0:T(8,128)(2,1)}, bf16[2048,256]{1,0:T(8,128)(2,1)}, u32[]{:S(2)}, u32[]{:S(2)}) collective-permute-start(bf16[2048,256]{1,0:T(8,128)(2,1)} %slab_pairs.1.refs_4_.refs_6_), channel_id=1, source_target_pairs={{0,24},{1,25},{2,26},{3,27},{4,28},{5,29},{6,30},{7,31},{8,16},{9,... | collective-permute-start | bytes 3145736 | tf_op jit(solution)/shard_map/ppermute | solution.py:54
  111.9 24.9 %collective-permute-start.12 = (bf16[2,120,2048]{2,1,0:T(8,128)(2,1)S(1)}, bf16[2,120,2048]{2,1,0:T(8,128)(2,1)S(1)}, u32[]{:S(2)}, u32[]{:S(2)}) collective-permute-start(bf16[2,120,2048]{2,1,0:T(8,128)(2,1)S(1)} %copy-done.4), channel_id=1, source_target_pairs={{0,1},{1,0},{2,3},{3,2},{4,5},{5,4},{6,7},{7,6},{8,9},{9,8},{10,11... | collective-permute-start | bytes 2949128 | tf_op jit(solution)/shard_map/ppermute | solution.py:54
  117.8 31.6 %copy-start.1 = (bf16[2,120,2048]{2,1,0:T(8,128)(2,1)}, bf16[2,120,2048]{2,1,0:T(8,128)(2,1)S(1)}, u32[]{:S(2)}) copy-start(bf16[2,120,2048]{2,1,0:T(8,128)(2,1)S(1)} %collective-permute-done.2.refs_2_) | copy-start | bytes 2949124
  117.8 31.6 %collective-permute-start.13 = (bf16[2,120,2048]{2,1,0:T(8,128)(2,1)S(1)}, bf16[2,120,2048]{2,1,0:T(8,128)(2,1)}, u32[]{:S(2)}, u32[]{:S(2)}) collective-permute-start(bf16[2,120,2048]{2,1,0:T(8,128)(2,1)S(1)} %collective-permute-done.2.refs_2_), channel_id=1, source_target_pairs={{0,1},{1,0},{2,3},{3,2},{4,5},{5,4},{6,7},{7,6},{8,9},{9,8},{10,11... | collective-permute-start | bytes 2949128 | tf_op jit(solution)/shard_map/ppermute | solution.py:54
  118.9 30.5 %copy-start.2 = (bf16[2,120,2048]{2,1,0:T(8,128)(2,1)}, bf16[2,120,2048]{2,1,0:T(8,128)(2,1)S(1)}, u32[]{:S(2)}) copy-start(bf16[2,120,2048]{2,1,0:T(8,128)(2,1)S(1)} %collective-permute-done.4.refs_4_) | copy-start | bytes 2949124
  118.9 30.5 %collective-permute-start.14 = (bf16[2,120,2048]{2,1,0:T(8,128)(2,1)S(1)}, bf16[2,120,2048]{2,1,0:T(8,128)(2,1)}, u32[]{:S(2)}, u32[]{:S(2)}) collective-permute-start(bf16[2,120,2048]{2,1,0:T(8,128)(2,1)S(1)} %collective-permute-done.4.refs_4_), channel_id=1, source_target_pairs={{0,1},{1,0},{2,3},{3,2},{4,5},{5,4},{6,7},{7,6},{8,9},{9,8},{10,11... | collective-permute-start | bytes 2949128 | tf_op jit(solution)/shard_map/ppermute | solution.py:54
  134.1 15.4 %copy-start.3 = (bf16[2048,256]{1,0:T(8,128)(2,1)}, bf16[2048,256]{1,0:T(8,128)(2,1)S(1)}, u32[]{:S(2)}) copy-start(bf16[2048,256]{1,0:T(8,128)(2,1)S(1)} %collective-permute-done.9.refs_4_.refs_6_) | copy-start | bytes 3145732
  134.1 12.4 %collective-permute-start.3 = (bf16[120,2048]{1,0:T(8,128)(2,1)}, bf16[120,2048]{1,0:T(8,128)(2,1)S(1)}, u32[]{:S(2)}, u32[]{:S(2)}) collective-permute-start(bf16[120,2048]{1,0:T(8,128)(2,1)} %slice_bitcast_fusion.1), channel_id=1, source_target_pairs={{0,2},{1,3},{2,4},{3,5},{4,6},{5,7},{6,0},{7,1},{8,10},{9,11},{10,... | collective-permute-start | bytes 1474568 | tf_op jit(solution)/shard_map/ppermute | solution.py:54
  135.4 13.7 %collective-permute-start.5 = (bf16[120,2048]{1,0:T(8,128)(2,1)}, bf16[120,2048]{1,0:T(8,128)(2,1)}, u32[]{:S(2)}, u32[]{:S(2)}) collective-permute-start(bf16[120,2048]{1,0:T(8,128)(2,1)} %slice_bitcast_fusion), channel_id=1, source_target_pairs={{0,6},{1,7},{2,0},{3,1},{4,2},{5,3},{6,4},{7,5},{8,14},{9,15},{10,... | collective-permute-start | bytes 1474568 | tf_op jit(solution)/shard_map/ppermute | solution.py:54
  136.8 1.0 copy-start.5
  137.8 24.5 %collective-permute-start.8 = (bf16[2048,256]{1,0:T(8,128)(2,1)}, bf16[2048,256]{1,0:T(8,128)(2,1)}, u32[]{:S(2)}, u32[]{:S(2)}) collective-permute-start(bf16[2048,256]{1,0:T(8,128)(2,1)} %slab_pairs.1.refs_4_.refs_6_), channel_id=1, source_target_pairs={{0,32},{1,33},{2,34},{3,35},{4,36},{5,37},{6,38},{7,39},{8,40},{9,... | collective-permute-start | bytes 3145736 | tf_op jit(solution)/shard_map/ppermute | solution.py:54
  146.5 8.0 %copy-start.7 = (bf16[120,2048]{1,0:T(8,128)(2,1)}, bf16[120,2048]{1,0:T(8,128)(2,1)S(1)}, u32[]{:S(2)}) copy-start(bf16[120,2048]{1,0:T(8,128)(2,1)S(1)} %collective-permute-done.3.refs_0_) | copy-start | bytes 1474564
  146.5 9.8 %collective-permute-start.6 = (bf16[120,2048]{1,0:T(8,128)(2,1)S(1)}, bf16[120,2048]{1,0:T(8,128)(2,1)S(1)}, u32[]{:S(2)}, u32[]{:S(2)}) collective-permute-start(bf16[120,2048]{1,0:T(8,128)(2,1)S(1)} %collective-permute-done.3.refs_0_), channel_id=1, source_target_pairs={{0,1},{1,0},{2,3},{3,2},{4,5},{5,4},{6,7},{7,6},{8,9},{9,8},{10,11... | collective-permute-start | bytes 1474568 | tf_op jit(solution)/shard_map/ppermute | solution.py:54
  149.2 7.1 %collective-permute-start.7 = (bf16[120,2048]{1,0:T(8,128)(2,1)}, bf16[120,2048]{1,0:T(8,128)(2,1)S(1)}, u32[]{:S(2)}, u32[]{:S(2)}) collective-permute-start(bf16[120,2048]{1,0:T(8,128)(2,1)} %collective-permute-done.5.refs_1_), channel_id=1, source_target_pairs={{0,1},{1,0},{2,3},{3,2},{4,5},{5,4},{6,7},{7,6},{8,9},{9,8},{10,11... | collective-permute-start | bytes 1474568 | tf_op jit(solution)/shard_map/ppermute | solution.py:54
  154.5 16.5 %collective-permute-start.15 = (bf16[6,120,256]{2,1,0:T(8,128)(2,1)}, bf16[6,120,256]{2,1,0:T(8,128)(2,1)S(1)}, u32[]{:S(2)}, u32[]{:S(2)}) collective-permute-start(bf16[6,120,256]{2,1,0:T(8,128)(2,1)} %chi_near_out.1), channel_id=1, source_target_pairs={{0,8},{1,9},{2,10},{3,11},{4,12},{5,13},{6,14},{7,15},{8,0},{9,1},... | collective-permute-start | bytes 1105928 | tf_op jit(solution)/shard_map/ppermute | solution.py:54
  156.3 0.8 copy-start.8
  157.1 0.8 copy-start.9
  161.2 16.2 %collective-permute-start.11 = (bf16[2,120,256]{2,1,0:T(8,128)(2,1)}, bf16[2,120,256]{2,1,0:T(8,128)(2,1)S(1)}, u32[]{:S(2)}, u32[]{:S(2)}) collective-permute-start(bf16[2,120,256]{2,1,0:T(8,128)(2,1)} %chi_far_out.1), channel_id=1, source_target_pairs={{0,8},{1,9},{2,10},{3,11},{4,12},{5,13},{6,14},{7,15},{8,0},{9,1},... | collective-permute-start | bytes 368648 | tf_op jit(solution)/shard_map/ppermute | solution.py:54
  171.0 0.7 copy-start.10
  177.4 0.7 copy-start.11

commit v3 on v2

v3 whole, which is shorter than its diff:
```python
import math

import jax
import jax.numpy as jnp
from jax import lax
from jax.experimental import pallas as pl
from jax.experimental.pallas import tpu as pltpu
from jax.sharding import PartitionSpec as P

BOX = 64
KC = 2048
VMEM = 56 * 1024 * 1024
BF = jnp.bfloat16
F32 = jnp.float32


def coulomb_root(box_index):
    plane_size = BOX * BOX
    half_box = BOX // 2
    leading = box_index // plane_size
    middle = box_index // BOX % BOX
    trailing = box_index % BOX

    def centred(offset_idx):
        return jnp.where(offset_idx >= half_box, offset_idx - BOX, offset_idx).astype(F32)

    length_sq = centred(leading) ** 2 + centred(middle) ** 2 + centred(trailing) ** 2
    return 32.0 / jnp.sqrt(length_sq + 64.0)


def linear(x, y, z, core):
    return ((x * 2 + y // 2) * 16) + (y % 2) * 8 + z * 2 + core


def route(step):
    pairs = []
    for x in range(4):
        for y in range(4):
            for z in range(4):
                for core in range(2):
                    pairs.append((linear(x, y, z, core), linear(*step(x, y, z, core))))
    return pairs


Z_UP = route(lambda x, y, z, c: (x, y, (z + 1) % 4, c))
Z_DOWN = route(lambda x, y, z, c: (x, y, (z + 3) % 4, c))
CORE = route(lambda x, y, z, c: (x, y, z, 1 - c))
Y_PAIR = route(lambda x, y, z, c: (x, y ^ 1, z, c))
Y_CROSS = route(lambda x, y, z, c: (x, 3 - y, z, c))


def send(value, pairs):
    return lax.ppermute(value, ("band", "grow"), pairs)


def nt_dot(left, right):
    return lax.dot_general(left, right, (((1,), (1,)), ((), ())), preferred_element_type=F32)


def slab_body(val, cond, zeta, weight, root, out, acc):
    step = pl.program_id(0)
    conds = cond.shape[0]
    for c in range(0, conds, 4):
        lhs = jnp.concatenate([val[...] * cond[c + i : c + i + 1, :] for i in range(4)], axis=0)
        part = nt_dot(lhs, zeta[...])
        rows = slice(c * 128, (c + 4) * 128)
        acc[rows] = jnp.where(step == 0, part, acc[rows] + part)

    @pl.when(step == pl.num_programs(0) - 1)
    def _():
        for c in range(conds):
            rows = slice(c * 128, (c + 1) * 128)
            out[rows] = (acc[rows] * root[...] * weight[:, c : c + 1]).astype(BF)


def slab_kernel(val, cond, zeta, weight, root, name):
    conds, points = cond.shape
    pairs = conds * 128
    cols = zeta.shape[0]
    return pl.pallas_call(
        slab_body,
        grid=(points // KC,),
        in_specs=[
            pl.BlockSpec((128, KC), lambda k: (0, k)),
            pl.BlockSpec((conds, KC), lambda k: (0, k)),
            pl.BlockSpec((cols, KC), lambda k: (0, k)),
            pl.BlockSpec((128, conds), lambda k: (0, 0)),
            pl.BlockSpec((1, cols), lambda k: (0, 0)),
        ],
        out_specs=pl.BlockSpec((pairs, cols), lambda k: (0, 0)),
        out_shape=jax.ShapeDtypeStruct((pairs, cols), BF),
        scratch_shapes=[pltpu.VMEM((pairs, cols), F32)],
        compiler_params=pltpu.CompilerParams(vmem_limit_bytes=VMEM),
        cost_estimate=pl.CostEstimate(flops=1 << 20, bytes_accessed=1 << 16, transcendentals=0),
        name=name,
    )(val, cond, zeta, weight, root)


def rho_body(zeta, cond_a, cond_b, val_a, val_b, root, out, lhs, rhs, acc):
    step = pl.program_id(0)
    conds = cond_a.shape[0]
    rows = zeta.shape[0]

    @pl.when(step == 0)
    def _():
        lhs[...] = jnp.zeros_like(lhs)

    rhs[0:128, :] = val_a[...]
    rhs[128:256, :] = val_b[...]
    lhs[0:rows, :] = zeta[...]
    for side, cond in ((0, cond_a), (1, cond_b)):
        for c in range(0, conds, 4):
            left = jnp.concatenate(
                [lhs[...] * cond[c + i : c + i + 1, :] for i in range(4)], axis=0
            )
            part = nt_dot(left, rhs[...])
            first = (side * conds + c) * 128
            span = slice(first, first + 512)
            acc[span] = jnp.where(step == 0, part, acc[span] + part)

    @pl.when(step == pl.num_programs(0) - 1)
    def _():
        for c in range(2 * conds):
            block = acc[c * 128 : c * 128 + rows, :] * root[:, 0:1]
            out[0, :, c * 128 : (c + 1) * 128] = block[:, 0:128].astype(BF)
            out[1, :, c * 128 : (c + 1) * 128] = block[:, 128:256].astype(BF)


def rho_kernel(zeta, cond_a, cond_b, val_a, val_b, root):
    conds, points = cond_a.shape
    rows = zeta.shape[0]
    pairs = 2 * conds * 128
    return pl.pallas_call(
        rho_body,
        grid=(points // KC,),
        in_specs=[
            pl.BlockSpec((rows, KC), lambda k: (0, k)),
            pl.BlockSpec((conds, KC), lambda k: (0, k)),
            pl.BlockSpec((conds, KC), lambda k: (0, k)),
            pl.BlockSpec((128, KC), lambda k: (0, k)),
            pl.BlockSpec((128, KC), lambda k: (0, k)),
            pl.BlockSpec((rows, 128), lambda k: (0, 0)),
        ],
        out_specs=pl.BlockSpec((2, rows, pairs), lambda k: (0, 0, 0)),
        out_shape=jax.ShapeDtypeStruct((2, rows, pairs), BF),
        scratch_shapes=[
            pltpu.VMEM((128, KC), BF),
            pltpu.VMEM((256, KC), BF),
            pltpu.VMEM((pairs, 256), F32),
        ],
        compiler_params=pltpu.CompilerParams(vmem_limit_bytes=VMEM),
        cost_estimate=pl.CostEstimate(flops=1 << 20, bytes_accessed=1 << 16, transcendentals=0),
        name="rho_rows",
    )(zeta, cond_a, cond_b, val_a, val_b, root)


def chi_kernel(parts, sides, name):
    arrays, picks = [], []
    for first, second, crossed in parts:
        pick = []
        for array, index in (first, second):
            known = [i for i, (a, x) in enumerate(arrays) if a is array]
            if not known:
                arrays.append((array, crossed))
                known = [len(arrays) - 1]
            pick.append((known[0], index))
        picks.append(pick)
    rows, depth = arrays[0][0].shape[-2:]
    given, count = len(arrays), len(parts)
    blk = depth // 2
    slabs, found = [], []
    for halves, _ in sides:
        for half in halves:
            found.append([len(slabs), len(slabs) + len(half) - 1])
            slabs += half
    cols = slabs[0].shape[1]

    def body(*refs):
        ins = refs[:given]
        slab_refs = refs[given : given + len(slabs)]
        outs = refs[given + len(slabs) : given + len(slabs) + len(sides)]
        lhs, acc = refs[given + len(slabs) + len(sides) :]
        step = pl.program_id(0)

        @pl.when(step == 0)
        def _():
            lhs[...] = jnp.zeros_like(lhs)

        for half in range(2):
            for i in range(count):
                array, index = picks[i][half]
                block = ins[array][...] if index is None else ins[array][index]
                lhs[half, i * 128 : i * 128 + rows, :] = block

        def product(side, block):
            first, second = found[2 * side][block], found[2 * side + 1][block]
            return jnp.dot(
                lhs[0], slab_refs[first][...], preferred_element_type=F32
            ) + jnp.dot(lhs[1], slab_refs[second][...], preferred_element_type=F32)

        @pl.when(step == 0)
        def _():
            for side in range(len(sides)):
                acc[side] = product(side, 0)

        @pl.when(step == 1)
        def _():
            for side, ref in enumerate(outs):
                total = acc[side] + product(side, 1)
                for i in range(count):
                    ref[i] = total[i * 128 : i * 128 + rows, :].astype(ref.dtype)

    def spec(array, crossed):
        if array.ndim == 3:
            return pl.BlockSpec((2, rows, blk), lambda k: (0, 0, 1 - k if crossed else k))
        return pl.BlockSpec((rows, blk), lambda k: (0, 1 - k if crossed else k))

    def slab_spec(slab):
        if slab.shape[0] == blk:
            return pl.BlockSpec((blk, cols), lambda k: (0, 0))
        return pl.BlockSpec((blk, cols), lambda k: (k, 0))

    whole = pl.BlockSpec((count, rows, cols), lambda k: (0, 0, 0))
    return pl.pallas_call(
        body,
        grid=(2,),
        in_specs=[spec(a, x) for a, x in arrays] + [slab_spec(slab) for slab in slabs],
        out_specs=[whole] * len(sides),
        out_shape=[jax.ShapeDtypeStruct((count, rows, cols), dtype) for _, dtype in sides],
        scratch_shapes=[
            pltpu.VMEM((2, count * 128, blk), BF),
            pltpu.VMEM((len(sides), count * 128, cols), F32),
        ],
        compiler_params=pltpu.CompilerParams(vmem_limit_bytes=VMEM),
        cost_estimate=pl.CostEstimate(flops=1 << 20, bytes_accessed=1 << 16, transcendentals=0),
        name=name,
    )(*[a for a, _ in arrays], *slabs)


def finish_kernel(place, chi, mine, theirs, before, name):
    blocks, rows, cols = chi.shape
    count = mine.shape[0] // 2

    def body(place_ref, chi_ref, mine_ref, theirs_ref, *rest):
        out = rest[-1]
        step = pl.program_id(0)
        core = place_ref[2 * count]
        for first, src in ((0, mine_ref), (count, theirs_ref)):

            @pl.when(jnp.logical_and(step >= first, step < first + count))
            def _(src=src):
                out[core] = chi_ref[core] - src[0].astype(F32)
                out[1 - core] = chi_ref[1 - core] - src[1].astype(F32)

    def where(i, place_ref):
        return (place_ref[i], 0, 0)

    block = (2, rows, cols)
    specs = [
        pl.BlockSpec(block, where),
        pl.BlockSpec(block, lambda i, place_ref: (jnp.minimum(i, count - 1), 0, 0)),
        pl.BlockSpec(block, lambda i, place_ref: (jnp.maximum(i - count, 0), 0, 0)),
    ]
    operands = [place, chi, mine, theirs]
    if before is not None:
        specs.append(pl.BlockSpec(memory_space=pl.ANY))
        operands.append(before)
    return pl.pallas_call(
        body,
        grid_spec=pltpu.PrefetchScalarGridSpec(
            num_scalar_prefetch=1,
            grid=(2 * count,),
            in_specs=specs,
            out_specs=pl.BlockSpec(block, where),
        ),
        out_shape=jax.ShapeDtypeStruct(chi.shape, F32),
        input_output_aliases={} if before is None else {4: 0},
        compiler_params=pltpu.CompilerParams(vmem_limit_bytes=VMEM),
        cost_estimate=pl.CostEstimate(flops=1 << 20, bytes_accessed=1 << 16, transcendentals=0),
        name=name,
    )(*operands)


def on_device(
    chi_prev,
    zeta_rows,
    zeta_slab,
    valence_store,
    valence_energy,
    conduction,
    conduction_energy,
    owners,
    gmap_rows,
    gmap_slab,
):
    band = lax.axis_index("band")
    grow = lax.axis_index("grow")
    core = grow % 2
    yz = grow // 2
    turn = (band // 2 + band % 2) % 2
    points = valence_store.shape[2]

    store = valence_store[0]
    piece_a = lax.dynamic_slice_in_dim(store, yz * 16 + core * 8, 8, 0)
    piece_b = lax.dynamic_slice_in_dim(store, yz * 16 + (1 - core) * 8, 8, 0)
    turns = jnp.array([(b // 2 + b % 2) % 2 for b in range(8)])
    pieces = jnp.where(turns[:, None, None] == 1, piece_b[None], piece_a[None])
    panels = lax.all_to_all(pieces, "band", split_axis=0, concat_axis=0, tiled=True)
    chosen = jnp.concatenate(
        [lax.dynamic_slice_in_dim(panels, owners[i], 1, 0)[0] for i in range(2)], axis=0
    )
    payload = jnp.concatenate([chosen, conduction.reshape(16, points // 16)], axis=1)
    width = payload.shape[1]

    half = (core + turn) % 2
    energy_v = jnp.take(valence_energy, owners, axis=0).reshape(2, 8, 2, 8)
    energy_v = energy_v.transpose(2, 1, 0, 3).reshape(2, 128)
    energy_v = jnp.where(half == 0, energy_v, energy_v[::-1])
    energy_c = conduction_energy.reshape(8, 2).T
    energy_c = jnp.where(core == 0, energy_c, energy_c[::-1])
    norm = 4.0 / math.sqrt(4096)
    weight = [
        [norm / (energy_c[j][None, :] - energy_v[i][:, None]) for j in range(2)] for i in range(2)
    ]
    weight = [[w[0], w[1], jnp.concatenate(w, axis=1)] for w in weight]
    root_rows = jnp.broadcast_to(coulomb_root(gmap_rows)[:, None], (gmap_rows.shape[0], 128))
    root_slab = coulomb_root(gmap_slab)[None, :]
    payload, weight, root_rows, root_slab = lax.optimization_barrier(
        (payload, weight, root_rows, root_slab)
    )

    groups = [list(range(0, 16, 2)), list(range(1, 16, 2))]
    mine = lax.all_to_all(
        jnp.broadcast_to(payload[None], (8, 16, width)),
        "grow",
        split_axis=0,
        concat_axis=0,
        tiled=True,
        axis_index_groups=groups,
    ).reshape(128, width)
    other = send(mine, CORE)
    cond_mine = mine[:, points:].reshape(8, points)
    cond_other = send(cond_mine, CORE)

    own_00 = slab_kernel(mine, cond_mine, zeta_slab, weight[0][0], root_slab, "slab_00")
    own_00, other, cond_other = lax.optimization_barrier((own_00, other, cond_other))
    out_00 = send(own_00, Y_PAIR)
    out_10 = send(own_00, Y_CROSS)
    rho = rho_kernel(zeta_rows, cond_mine, cond_other, mine, other, root_rows)
    rho, cond_other, out_00, out_10 = lax.optimization_barrier((rho, cond_other, out_00, out_10))

    from_down = send(rho, Z_UP)
    from_up = send(rho, Z_DOWN)
    rho_x = send(rho, CORE)
    own_01 = slab_kernel(mine, cond_other, zeta_slab, weight[0][1], root_slab, "slab_01")
    own_01, other = lax.optimization_barrier((own_01, other))
    out_01 = send(own_01, Y_PAIR)
    out_11 = send(own_01, Y_CROSS)
    cond = jnp.concatenate([cond_mine, cond_other], axis=0)
    own_1 = slab_kernel(other, cond, zeta_slab, weight[1][2], root_slab, "slab_1")
    from_down, from_up, rho_x, out_01, out_11, own_1 = lax.optimization_barrier(
        (from_down, from_up, rho_x, out_01, out_11, own_1)
    )
    out_side = ([[out_00, out_01], [out_10, out_11]], BF)
    in_side = ([[own_00, own_01], [own_1]], F32)

    def both(array, crossed):
        if crossed:
            return ((array, 1), (array, 0), True)
        return ((array, 0), (array, 1), False)

    far_0 = send(from_down[0], Z_UP)
    far_1 = send(from_up[1], Z_DOWN)
    from_down_x = send(from_down, CORE)
    from_up_x = send(from_up, CORE)
    near = [both(rho, False), both(rho_x, True)]
    near_out, near_in = chi_kernel(near, [out_side, in_side], "chi_own")
    got_near = send(near_out, Y_PAIR)
    mid = [both(from_down, False), both(from_down_x, True), both(from_up, False), both(from_up_x, True)]
    mid_out, mid_in = chi_kernel(mid, [out_side, in_side], "chi_next")
    got_mid = send(mid_out, Y_PAIR)
    far_0, far_1, near_in, mid_in, got_near = lax.optimization_barrier(
        (far_0, far_1, near_in, mid_in, got_near)
    )

    far_0x = send(far_0, CORE)
    far_1x = send(far_1, CORE)
    far = [((far_0, None), (far_1, None), False), ((far_1x, None), (far_0x, None), True)]
    (far_out,) = chi_kernel(far, [out_side], "chi_far_out")
    got_far = send(far_out, Y_PAIR)
    (far_in,) = chi_kernel(far, [in_side], "chi_far_in")

    yl = grow // 8
    z = yz % 4
    total_rows, cols = chi_prev.shape
    done = None
    chi = chi_prev.reshape(16, total_rows // 16, cols)
    for steps, inner, outer, name in (
        ((0,), near_in, got_near, "finish_own"),
        ((3, 1), mid_in, got_mid, "finish_next"),
        ((2,), far_in, got_far, "finish_far"),
    ):
        slots = jnp.stack([(z + s) % 4 for s in steps])
        place = jnp.concatenate([yl * 4 + slots, (1 - yl) * 4 + slots, core[None]])
        done = finish_kernel(place.astype(jnp.int32), chi, inner, outer, done, name)
    return done.reshape(total_rows, cols)


def solution(mesh):
    placed = (
        P("band", "grow"),
        P(("band", "grow"), None),
        P("grow", None),
        P("band", None, None),
        P(),
        P("grow", None),
        P(),
        P(),
        P(("band", "grow")),
        P("grow"),
    )
    return jax.shard_map(
        on_device, mesh=mesh, in_specs=placed, out_specs=P("band", "grow"), check_vma=False
    )
```

time: 181 us -> 155 us (0.86)
  waiting for transfers between devices: 44.7 us -> 10.7 us
  Pallas kernels: 50.5 us -> 69.1 us
  starting transfers between devices: 30.8 us -> 23 us
  local copies, waits for them, and re-layouts: 13.7 us -> 10.7 us
  other arithmetic: 8.47 us -> 5.98 us
  blocking collectives: 28.8 us -> 31.2 us
    ppermute x16 -> x18, waiting for transfers between devices: 31.8 us -> 2.29 us  [send(): return lax.ppermute(value, ('band', 'grow'), pairs)]
    pallas_call x1 -> x3, Pallas kernels: 12.7 us -> 27.8 us  [slab_kernel(): pl.pallas_call(slab_body, grid=(points // KC,), in_specs=[pl.BlockSpec((1...]
    all_to_all x1 -> x0, starting transfers between devices: 6.88 us -> none  [over_plane(): lax.all_to_all(copies, 'grow', split_axis=0, concat_axis=0, tiled=True, a...]
    all_to_all x1, waiting for transfers between devices: 12.9 us -> 8.36 us  [on_device(): lax.all_to_all(pieces, 'band', split_axis=0, concat_axis=0, tiled=True)]
    all_to_all x1, blocking collectives: 28.8 us -> 31.2 us  [on_device(): lax.all_to_all(jnp.broadcast_to(payload[None], (8, 16, width)), 'grow', s...]
    pallas_call x4, Pallas kernels: 17.1 us -> 19.2 us  [chi_kernel(): pl.pallas_call(body, grid=(2,), in_specs=[spec(a, x) for a, x in arrays]...]
    ppermute x16 -> x18, starting transfers between devices: 17.6 us -> 15.5 us  [send(): return lax.ppermute(value, ('band', 'grow'), pairs)]
    pallas_call x2 -> x3, Pallas kernels: 8.33 us -> 9.65 us  [finish_kernel(): pl.pallas_call(body, grid_spec=pltpu.PrefetchScalarGridSpec(num_scalar_pr...]
  transfers between devices with their start and end apart: 18 -> 19, of which waited for: 7 -> 3; matrix products, arithmetic and copies ran while one was open for 7% -> 4% of each run, Pallas kernels for 20% -> 43%
where the time goes in v3:
time: 155 us
  Pallas kernels  69.1 us (45%)
  blocking collectives  31.2 us (20%)
  starting transfers between devices  23 us (15%)
  local copies, waits for them, and re-layouts  10.7 us (7%)
  waiting for transfers between devices  10.7 us (7%)
  other arithmetic  5.98 us (4%)
  between operations  3.98 us (3%)
    all_to_all x1, blocking collectives, on_device(): lax.all_to_all(jnp.broadcast_to(payload[None], (8, 16, width)), 'grow', s...  31.2 us
    pallas_call x3, Pallas kernels, slab_kernel(): pl.pallas_call(slab_body, grid=(points // KC,), in_specs=[pl.BlockSpec((1...  27.8 us
    pallas_call x4, Pallas kernels, chi_kernel(): pl.pallas_call(body, grid=(2,), in_specs=[spec(a, x) for a, x in arrays]...  19.2 us
    ppermute x18, starting transfers between devices, send(): return lax.ppermute(value, ('band', 'grow'), pairs)  15.5 us
    pallas_call x1, Pallas kernels, rho_kernel(): pl.pallas_call(rho_body, grid=(points // KC,), in_specs=[pl.BlockSpec((ro...  12.4 us
    pallas_call x3, Pallas kernels, finish_kernel(): pl.pallas_call(body, grid_spec=pltpu.PrefetchScalarGridSpec(num_scalar_pr...  9.65 us
    all_to_all x1, waiting for transfers between devices, on_device(): lax.all_to_all(pieces, 'band', split_axis=0, concat_axis=0, tiled=True)  8.36 us
    all_to_all x1, starting transfers between devices, on_device(): lax.all_to_all(pieces, 'band', split_axis=0, concat_axis=0, tiled=True)  7.48 us
  transfers between devices with their start and end apart: 19, of which 3 were waited for; matrix products, arithmetic and copies ran while one was open for 4% of the time, Pallas kernels for 43%

profile of v3, /device:TPU:1, one launch (start us, length us, event | category | flops | bytes accessed | tf_op | source)
XLA Modules:
  0.0 154.6 jit_solution(4250005615979894480)
XLA Ops:
  0.1 1.0 dynamic-slice_bitcast_fusion.3
  1.1 1.8 %broadcast_select_fusion = bf16[8,8,8192]{2,1,0:T(8,128)(2,1)} fusion(pred[8]{0:T(512)(128)(4,1)} %constant.209, bf16[8,8192]{1,0:T(8,128)(2,1)S(1)} %get-tuple-element.68, bf16[8,8192]{1,0:T(8,128)(2,1)S(1)} %get-tuple-element.67), kind=kLoop, calls=%fused_computation.1 | loop fusion | flops 524288 | bytes 1310728 | tf_op jit(solution)/shard_map/jit(_where)/select_n | solution.py:307
  2.9 7.5 %all-to-all-start = ((bf16[8,8,8192]{2,1,0:T(8,128)(2,1)}), bf16[8,8,8192]{2,1,0:T(8,128)(2,1)S(1)}, u32[]{:S(2)}, u32[]{:S(2)}) async-start(bf16[8,8,8192]{2,1,0:T(8,128)(2,1)} %broadcast_select_fusion), calls=%async_computation | async-start | bytes 2097152 | tf_op jit(solution)/shard_map/all_to_all | solution.py:308
  17.5 8.4 %all-to-all-done = bf16[8,8,8192]{2,1,0:T(8,128)(2,1)S(1)} async-done(((bf16[8,8,8192]{2,1,0:T(8,128)(2,1)}), bf16[8,8,8192]{2,1,0:T(8,128)(2,1)S(1)}, u32[]{:S(2)}, u32[]{:S(2)}) %all-to-all-start) | async-done | bytes 1048608 | tf_op jit(solution)/shard_map/all_to_all | solution.py:308
  26.7 31.2 %all_to_all.10 = bf16[8,16,8704]{2,1,0:T(8,128)(2,1)S(1)} all-to-all(bf16[8,16,8704]{2,1,0:T(8,128)(2,1)S(1)} %broadcast_in_dim.74), channel_id=1, replica_groups={{0,2,4,6,8,10,12,14},{1,3,5,7,9,11,13,15},{16,18,20,22,24,26,28,30},{17..., dimensions={0} | all-to-all | bytes 4456448 | tf_op jit(solution)/shard_map/all_to_all | solution.py:333
  57.9 3.0 %collective-permute-start = (bf16[128,8704]{1,0:T(8,128)(2,1)S(1)}, bf16[128,8704]{1,0:T(8,128)(2,1)}, u32[]{:S(2)}, u32[]{:S(2)}) collective-permute-start(bf16[128,8704]{1,0:T(8,128)(2,1)S(1)} %bitcast.33), channel_id=1, source_target_pairs={{0,1},{1,0},{2,3},{3,2},{4,5},{5,4},{6,7},{7,6},{8,9},{9,8},{10,11... | collective-permute-start | bytes 6684680 | tf_op jit(solution)/shard_map/ppermute | solution.py:53
  61.7 7.7 %slab_00.1.refs_6_.refs_8_.refs_4_ = bf16[1024,256]{1,0:T(8,128)(2,1)} custom-call(bf16[128,8704]{1,0:T(8,128)(2,1)} %bitcast.35, bf16[8,8192]{1,0:T(8,128)(2,1)} %copy-done.8, bf16[256,8192]{1,0:T(8,128)(2,1)} %zeta.7, f32[128,8]{1,0:T(8,128)} %get-tuple-element.36.weight, f32[1,256]{1,0:T(1,128)} %bitcast.42), custom_call_target="tpu_custom_call" | custom-call | flops 1048576 | bytes 65536 | tf_op jit(solution)/shard_map/slab_00/pallas_call | solution.py:80
  69.5 1.5 collective-permute-start.3
  71.5 12.4 %rho_rows.1.refs_0_ = bf16[2,120,2048]{2,1,0:T(8,128)(2,1)} custom-call(bf16[120,8192]{1,0:T(8,128)(2,1)} %zeta.5, bf16[8,8192]{1,0:T(8,128)(2,1)} %copy-done.8, bf16[8,8192]{1,0:T(8,128)(2,1)} %copy-done.13, bf16[128,8704]{1,0:T(8,128)(2,1)} %bitcast.36, bf16[128,8704]{1,0:T(8,128)(2,1)} %collective-permute-done.val_b.val, f32[120,128]{1,0:T(8,128)} %broadcast_in_dim.72.root), custom_call_target="tpu_custom_call" | custom-call | flops 1048576 | bytes 65536 | tf_op jit(solution)/shard_map/rho_rows/pallas_call | solution.py:133
  83.9 1.6 %collective-permute-start.6 = (bf16[2,120,2048]{2,1,0:T(8,128)(2,1)}, bf16[2,120,2048]{2,1,0:T(8,128)(2,1)}, u32[]{:S(2)}, u32[]{:S(2)}) collective-permute-start(bf16[2,120,2048]{2,1,0:T(8,128)(2,1)} %rho_rows.1.refs_0_), channel_id=1, source_target_pairs={{0,1},{1,0},{2,3},{3,2},{4,5},{5,4},{6,7},{7,6},{8,9},{9,8},{10,11... | collective-permute-start | bytes 2949128 | tf_op jit(solution)/shard_map/ppermute | solution.py:53
  85.5 1.0 collective-permute-start.5
  87.7 7.8 %slab_01.1.refs_7_.refs_9_.refs_5_ = bf16[1024,256]{1,0:T(8,128)(2,1)} custom-call(bf16[128,8704]{1,0:T(8,128)(2,1)} %bitcast.37, bf16[8,8192]{1,0:T(8,128)(2,1)} %copy-done.13, bf16[256,8192]{1,0:T(8,128)(2,1)} %zeta.7, f32[128,8]{1,0:T(8,128)} %get-tuple-element.44.weight, f32[1,256]{1,0:T(1,128)} %bitcast.43), custom_call_target="tpu_custom_call" | custom-call | flops 1048576 | bytes 65536 | tf_op jit(solution)/shard_map/slab_01/pallas_call | solution.py:80
  95.5 1.4 collective-permute-start.8
  96.9 0.7 pad_maximum_fusion.1.cond
  97.6 12.3 %slab_1.1.refs_8_.refs_10_.refs_6_ = bf16[2048,256]{1,0:T(8,128)(2,1)} custom-call(bf16[128,8704]{1,0:T(8,128)(2,1)} %collective-permute-done.val_b.val, bf16[16,8192]{1,0:T(8,128)(2,1)} %pad_maximum_fusion.1.cond, bf16[256,8192]{1,0:T(8,128)(2,1)} %zeta.7, f32[128,16]{1,0:T(8,128)} %copy.27.weight, f32[1,256]{1,0:T(1,128)} %bitcast.44), custom_call_target="tpu_custom_call" | custom-call | flops 1048576 | bytes 65536 | tf_op jit(solution)/shard_map/slab_1/pallas_call | solution.py:80
  110.0 0.9 collective-permute-done.4.refs_0_
  111.0 1.1 collective-permute-start.11
  112.1 1.8 %collective-permute-start.10 = (bf16[120,2048]{1,0:T(8,128)(2,1)S(1)}, bf16[120,2048]{1,0:T(8,128)(2,1)S(1)}, u32[]{:S(2)}, u32[]{:S(2)}) collective-permute-start(bf16[120,2048]{1,0:T(8,128)(2,1)S(1)} %slice_bitcast_fusion), channel_id=1, source_target_pairs={{0,6},{1,7},{2,0},{3,1},{4,2},{5,3},{6,4},{7,5},{8,14},{9,15},{10,... | collective-permute-start | bytes 1474568 | tf_op jit(solution)/shard_map/ppermute | solution.py:53
  114.0 4.9 %chi_own.1 = (bf16[2,120,256]{2,1,0:T(8,128)(2,1)}, f32[2,120,256]{2,1,0:T(8,128)}) custom-call(bf16[2,120,2048]{2,1,0:T(8,128)(2,1)} %rho_rows.1.refs_0_, bf16[2,120,2048]{2,1,0:T(8,128)(2,1)} %collective-permute-done.6.refs_1_, bf16[1024,256]{1,0:T(8,128)(2,1)} %copy-done.3, bf16[1024,256]{1,0:T(8,128)(2,1)} %copy-done.5, bf16[1024,256]{1,0:T(8,128)(2,1)} %copy-done.2, ...), custom_call_target="tpu_custom_call" | custom-call | flops 1048576 | bytes 65536 | tf_op jit(solution)/shard_map/chi_own/pallas_call | solution.py:224
  118.9 1.3 collective-permute-start.13
  120.2 0.9 copy-done.15
  121.1 1.0 copy-done.16
  122.1 6.7 %chi_next.1 = (bf16[4,120,256]{2,1,0:T(8,128)(2,1)}, f32[4,120,256]{2,1,0:T(8,128)}) custom-call(bf16[2,120,2048]{2,1,0:T(8,128)(2,1)} %copy-done.7, bf16[2,120,2048]{2,1,0:T(8,128)(2,1)} %copy-done.15, bf16[2,120,2048]{2,1,0:T(8,128)(2,1)} %copy-done.6, bf16[2,120,2048]{2,1,0:T(8,128)(2,1)} %copy-done.16, bf16[1024,256]{1,0:T(8,128)(2,1)} %copy-done.3, ...), custom_call_target="tpu_custom_call" | custom-call | flops 1048576 | bytes 65536 | tf_op jit(solution)/shard_map/chi_next/pallas_call | solution.py:224
  129.5 1.0 collective-permute-start.15
  131.5 1.3 collective-permute-done.15.refs_3_
  132.8 0.8 copy-done.11
  133.6 0.8 copy-done.12
  134.4 3.8 %chi_far_out.1 = bf16[2,120,256]{2,1,0:T(8,128)(2,1)} custom-call(bf16[120,2048]{1,0:T(8,128)(2,1)} %collective-permute-done.9.refs_0_, bf16[120,2048]{1,0:T(8,128)(2,1)} %copy-done.10, bf16[120,2048]{1,0:T(8,128)(2,1)} %copy-done.12, bf16[120,2048]{1,0:T(8,128)(2,1)} %copy-done.11, bf16[1024,256]{1,0:T(8,128)(2,1)} %copy-done.3, ...), custom_call_target="tpu_custom_call" | custom-call | flops 1048576 | bytes 65536 | tf_op jit(solution)/shard_map/chi_far_out/pallas_call | solution.py:224
  139.8 2.7 %finish_own.1.rest_0_ = f32[16,120,256]{2,1,0:T(8,128)} custom-call(s32[3]{0:T(128)} %add_add_fusion.1.place_ref, f32[16,120,256]{2,1,0:T(8,128)} %bitcast.38, f32[2,120,256]{2,1,0:T(8,128)} %get-tuple-element.63.mine_ref, bf16[2,120,256]{2,1,0:T(8,128)(2,1)} %copy-done.18), custom_call_target="tpu_custom_call" | custom-call | flops 1048576 | bytes 65536 | tf_op jit(solution)/shard_map/finish_own/pallas_call | solution.py:268
  143.1 4.3 %finish_next.1.rest_0_ = f32[16,120,256]{2,1,0:T(8,128)} custom-call(s32[5]{0:T(128)} %pad_add_fusion.1.place_ref, f32[16,120,256]{2,1,0:T(8,128)} %bitcast.39, f32[4,120,256]{2,1,0:T(8,128)} %get-tuple-element.61.mine_ref, bf16[4,120,256]{2,1,0:T(8,128)(2,1)} %copy-done.17, f32[16,120,256]{2,1,0:T(8,128)} %finish_own.1.rest_0_), custom_call_target="tpu_custom_call", output_to_operand_aliasing={{}: (4, {})} | custom-call | flops 1048576 | bytes 65536 | tf_op jit(solution)/shard_map/finish_next/pallas_call | solution.py:268
  147.4 3.8 %chi_far_in.1.mine_ref = f32[2,120,256]{2,1,0:T(8,128)} custom-call(bf16[120,2048]{1,0:T(8,128)(2,1)} %collective-permute-done.9.refs_0_, bf16[120,2048]{1,0:T(8,128)(2,1)} %copy-done.10, bf16[120,2048]{1,0:T(8,128)(2,1)} %copy-done.12, bf16[120,2048]{1,0:T(8,128)(2,1)} %copy-done.11, bf16[1024,256]{1,0:T(8,128)(2,1)} %slab_00.1.refs_6_.refs_8_.refs_4_, ...), custom_call_target="tpu_custom_call" | custom-call | flops 1048576 | bytes 65536 | tf_op jit(solution)/shard_map/chi_far_in/pallas_call | solution.py:224
  151.9 2.7 %finish_far.1 = f32[16,120,256]{2,1,0:T(8,128)} custom-call(s32[3]{0:T(128)} %add_add_fusion.place_ref, f32[16,120,256]{2,1,0:T(8,128)} %bitcast.40, f32[2,120,256]{2,1,0:T(8,128)} %chi_far_in.1.mine_ref, bf16[2,120,256]{2,1,0:T(8,128)(2,1)} %copy-done.19, f32[16,120,256]{2,1,0:T(8,128)} %finish_next.1.rest_0_), custom_call_target="tpu_custom_call", output_to_operand_aliasing={{}: (4, {})} | custom-call | flops 1048576 | bytes 65536 | tf_op jit(solution)/shard_map/finish_far/pallas_call | solution.py:268
  (108 shorter events, 11.6 us)
Async XLA Ops:
  0.0 10.6 %copy-start = (f32[8,128]{1,0:T(8,128)S(1)}, f32[8,128]{1,0:T(8,128)}, u32[]{:S(2)}) copy-start(f32[8,128]{1,0:T(8,128)} %param.15) | copy-start | bytes 12292
  0.0 10.3 %copy-start.21 = (s32[2]{0:T(128)S(1)}, s32[2]{0:T(128)}, u32[]{:S(2)}) copy-start(s32[2]{0:T(128)} %param.18) | copy-start | bytes 28
  0.0 10.4 %copy-start.23 = (f32[16]{0:T(128)S(1)}, f32[16]{0:T(128)}, u32[]{:S(2)}) copy-start(f32[16]{0:T(128)} %param.17) | copy-start | bytes 196
  0.0 14.4 %copy-start.20 = (bf16[1,8192]{1,0:T(2,128)(2,1)S(1)}, bf16[1,8192]{1,0:T(2,128)(2,1)}, u32[]{:S(2)}) copy-start(bf16[1,8192]{1,0:T(2,128)(2,1)} %param.16) | copy-start | bytes 49156
  1.1 15.8 %copy-start.24 = (s32[120]{0:T(128)S(1)}, s32[120]{0:T(128)}, u32[]{:S(2)}) copy-start(s32[120]{0:T(128)} %param.19) | copy-start | bytes 1444
  1.1 15.8 %copy-start.22 = (s32[256]{0:T(256)S(1)}, s32[256]{0:T(256)}, u32[]{:S(2)}) copy-start(s32[256]{0:T(256)} %param.20) | copy-start | bytes 3076
  2.9 23.0 %all-to-all-start = ((bf16[8,8,8192]{2,1,0:T(8,128)(2,1)}), bf16[8,8,8192]{2,1,0:T(8,128)(2,1)S(1)}, u32[]{:S(2)}, u32[]{:S(2)}) async-start(bf16[8,8,8192]{2,1,0:T(8,128)(2,1)} %broadcast_select_fusion), calls=%async_computation | async-start | bytes 2097152 | tf_op jit(solution)/shard_map/all_to_all | solution.py:308
  57.9 11.5 %collective-permute-start = (bf16[128,8704]{1,0:T(8,128)(2,1)S(1)}, bf16[128,8704]{1,0:T(8,128)(2,1)}, u32[]{:S(2)}, u32[]{:S(2)}) collective-permute-start(bf16[128,8704]{1,0:T(8,128)(2,1)S(1)} %bitcast.33), channel_id=1, source_target_pairs={{0,1},{1,0},{2,3},{3,2},{4,5},{5,4},{6,7},{7,6},{8,9},{9,8},{10,11... | collective-permute-start | bytes 6684680 | tf_op jit(solution)/shard_map/ppermute | solution.py:53
  61.1 8.4 %collective-permute-start.1 = (bf16[8,8192]{1,0:T(8,128)(2,1)S(1)}, bf16[8,8192]{1,0:T(8,128)(2,1)S(1)}, u32[]{:S(2)}, u32[]{:S(2)}) collective-permute-start(bf16[8,8192]{1,0:T(8,128)(2,1)S(1)} %reshape.52.cond.cond_a), channel_id=1, source_target_pairs={{0,1},{1,0},{2,3},{3,2},{4,5},{5,4},{6,7},{7,6},{8,9},{9,8},{10,11... | collective-permute-start | bytes 393224 | tf_op jit(solution)/shard_map/ppermute | solution.py:53
  69.5 14.4 %collective-permute-start.3 = (bf16[1024,256]{1,0:T(8,128)(2,1)}, bf16[1024,256]{1,0:T(8,128)(2,1)S(1)}, u32[]{:S(2)}, u32[]{:S(2)}) collective-permute-start(bf16[1024,256]{1,0:T(8,128)(2,1)} %slab_00.1.refs_6_.refs_8_.refs_4_), channel_id=1, source_target_pairs={{0,24},{1,25},{2,26},{3,27},{4,28},{5,29},{6,30},{7,31},{8,16},{9,... | collective-permute-start | bytes 1572872 | tf_op jit(solution)/shard_map/ppermute | solution.py:53
  71.0 13.0 %collective-permute-start.2 = (bf16[1024,256]{1,0:T(8,128)(2,1)}, bf16[1024,256]{1,0:T(8,128)(2,1)S(1)}, u32[]{:S(2)}, u32[]{:S(2)}) collective-permute-start(bf16[1024,256]{1,0:T(8,128)(2,1)} %slab_00.1.refs_6_.refs_8_.refs_4_), channel_id=1, source_target_pairs={{0,8},{1,9},{2,10},{3,11},{4,12},{5,13},{6,14},{7,15},{8,0},{9,1},... | collective-permute-start | bytes 1572872 | tf_op jit(solution)/shard_map/ppermute | solution.py:53
  83.9 11.6 %copy-start.2 = (bf16[1024,256]{1,0:T(8,128)(2,1)}, bf16[1024,256]{1,0:T(8,128)(2,1)S(1)}, u32[]{:S(2)}) copy-start(bf16[1024,256]{1,0:T(8,128)(2,1)S(1)} %collective-permute-done.3.refs_4_.refs_6_) | copy-start | bytes 1572868
  83.9 11.6 %copy-start.3 = (bf16[1024,256]{1,0:T(8,128)(2,1)}, bf16[1024,256]{1,0:T(8,128)(2,1)S(1)}, u32[]{:S(2)}) copy-start(bf16[1024,256]{1,0:T(8,128)(2,1)S(1)} %collective-permute-done.2.refs_2_.refs_4_) | copy-start | bytes 1572868
  83.9 26.1 %collective-permute-start.6 = (bf16[2,120,2048]{2,1,0:T(8,128)(2,1)}, bf16[2,120,2048]{2,1,0:T(8,128)(2,1)}, u32[]{:S(2)}, u32[]{:S(2)}) collective-permute-start(bf16[2,120,2048]{2,1,0:T(8,128)(2,1)} %rho_rows.1.refs_0_), channel_id=1, source_target_pairs={{0,1},{1,0},{2,3},{3,2},{4,5},{5,4},{6,7},{7,6},{8,9},{9,8},{10,11... | collective-permute-start | bytes 2949128 | tf_op jit(solution)/shard_map/ppermute | solution.py:53
  85.5 24.5 %collective-permute-start.5 = (bf16[2,120,2048]{2,1,0:T(8,128)(2,1)}, bf16[2,120,2048]{2,1,0:T(8,128)(2,1)S(1)}, u32[]{:S(2)}, u32[]{:S(2)}) collective-permute-start(bf16[2,120,2048]{2,1,0:T(8,128)(2,1)} %rho_rows.1.refs_0_), channel_id=1, source_target_pairs={{0,6},{1,7},{2,0},{3,1},{4,2},{5,3},{6,4},{7,5},{8,14},{9,15},{10,... | collective-permute-start | bytes 2949128 | tf_op jit(solution)/shard_map/ppermute | solution.py:53
  86.5 24.5 %collective-permute-start.4 = (bf16[2,120,2048]{2,1,0:T(8,128)(2,1)}, bf16[2,120,2048]{2,1,0:T(8,128)(2,1)S(1)}, u32[]{:S(2)}, u32[]{:S(2)}) collective-permute-start(bf16[2,120,2048]{2,1,0:T(8,128)(2,1)} %rho_rows.1.refs_0_), channel_id=1, source_target_pairs={{0,2},{1,3},{2,4},{3,5},{4,6},{5,7},{6,0},{7,1},{8,10},{9,11},{10,... | collective-permute-start | bytes 2949128 | tf_op jit(solution)/shard_map/ppermute | solution.py:53
  87.7 9.2 %copy-start.9 = (bf16[8,8192]{1,0:T(8,128)(2,1)S(1)}, bf16[8,8192]{1,0:T(8,128)(2,1)}, u32[]{:S(2)}) copy-start(bf16[8,8192]{1,0:T(8,128)(2,1)} %copy-done.8) | copy-start | bytes 393220
  87.7 9.2 %copy-start.14 = (bf16[8,8192]{1,0:T(8,128)(2,1)S(1)}, bf16[8,8192]{1,0:T(8,128)(2,1)}, u32[]{:S(2)}) copy-start(bf16[8,8192]{1,0:T(8,128)(2,1)} %copy-done.13) | copy-start | bytes 393220
  95.5 14.4 %collective-permute-start.8 = (bf16[1024,256]{1,0:T(8,128)(2,1)}, bf16[1024,256]{1,0:T(8,128)(2,1)S(1)}, u32[]{:S(2)}, u32[]{:S(2)}) collective-permute-start(bf16[1024,256]{1,0:T(8,128)(2,1)} %slab_01.1.refs_7_.refs_9_.refs_5_), channel_id=1, source_target_pairs={{0,24},{1,25},{2,26},{3,27},{4,28},{5,29},{6,30},{7,31},{8,16},{9,... | collective-permute-start | bytes 1572872 | tf_op jit(solution)/shard_map/ppermute | solution.py:53
  96.9 13.1 %collective-permute-start.7 = (bf16[1024,256]{1,0:T(8,128)(2,1)}, bf16[1024,256]{1,0:T(8,128)(2,1)S(1)}, u32[]{:S(2)}, u32[]{:S(2)}) collective-permute-start(bf16[1024,256]{1,0:T(8,128)(2,1)} %slab_01.1.refs_7_.refs_9_.refs_5_), channel_id=1, source_target_pairs={{0,8},{1,9},{2,10},{3,11},{4,12},{5,13},{6,14},{7,15},{8,0},{9,1},... | collective-permute-start | bytes 1572872 | tf_op jit(solution)/shard_map/ppermute | solution.py:53
  110.0 4.0 %copy-start.4 = (bf16[1024,256]{1,0:T(8,128)(2,1)}, bf16[1024,256]{1,0:T(8,128)(2,1)S(1)}, u32[]{:S(2)}) copy-start(bf16[1024,256]{1,0:T(8,128)(2,1)S(1)} %collective-permute-done.8.refs_5_.refs_7_) | copy-start | bytes 1572868
  110.0 8.9 %copy-start.6 = (bf16[2,120,2048]{2,1,0:T(8,128)(2,1)}, bf16[2,120,2048]{2,1,0:T(8,128)(2,1)S(1)}, u32[]{:S(2)}) copy-start(bf16[2,120,2048]{2,1,0:T(8,128)(2,1)S(1)} %collective-permute-done.5.refs_2_) | copy-start | bytes 2949124
  111.0 7.9 %copy-start.7 = (bf16[2,120,2048]{2,1,0:T(8,128)(2,1)}, bf16[2,120,2048]{2,1,0:T(8,128)(2,1)S(1)}, u32[]{:S(2)}) copy-start(bf16[2,120,2048]{2,1,0:T(8,128)(2,1)S(1)} %collective-permute-done.4.refs_0_) | copy-start | bytes 2949124
  111.0 9.2 %collective-permute-start.11 = (bf16[2,120,2048]{2,1,0:T(8,128)(2,1)S(1)}, bf16[2,120,2048]{2,1,0:T(8,128)(2,1)S(1)}, u32[]{:S(2)}, u32[]{:S(2)}) collective-permute-start(bf16[2,120,2048]{2,1,0:T(8,128)(2,1)S(1)} %collective-permute-done.4.refs_0_), channel_id=1, source_target_pairs={{0,1},{1,0},{2,3},{3,2},{4,5},{5,4},{6,7},{7,6},{8,9},{9,8},{10,11... | collective-permute-start | bytes 2949128 | tf_op jit(solution)/shard_map/ppermute | solution.py:53
  112.1 8.1 %collective-permute-start.12 = (bf16[2,120,2048]{2,1,0:T(8,128)(2,1)S(1)}, bf16[2,120,2048]{2,1,0:T(8,128)(2,1)S(1)}, u32[]{:S(2)}, u32[]{:S(2)}) collective-permute-start(bf16[2,120,2048]{2,1,0:T(8,128)(2,1)S(1)} %collective-permute-done.5.refs_2_), channel_id=1, source_target_pairs={{0,1},{1,0},{2,3},{3,2},{4,5},{5,4},{6,7},{7,6},{8,9},{9,8},{10,11... | collective-permute-start | bytes 2949128 | tf_op jit(solution)/shard_map/ppermute | solution.py:53
  112.1 16.7 %collective-permute-start.10 = (bf16[120,2048]{1,0:T(8,128)(2,1)S(1)}, bf16[120,2048]{1,0:T(8,128)(2,1)S(1)}, u32[]{:S(2)}, u32[]{:S(2)}) collective-permute-start(bf16[120,2048]{1,0:T(8,128)(2,1)S(1)} %slice_bitcast_fusion), channel_id=1, source_target_pairs={{0,6},{1,7},{2,0},{3,1},{4,2},{5,3},{6,4},{7,5},{8,14},{9,15},{10,... | collective-permute-start | bytes 1474568 | tf_op jit(solution)/shard_map/ppermute | solution.py:53
  114.0 14.8 %collective-permute-start.9 = (bf16[120,2048]{1,0:T(8,128)(2,1)S(1)}, bf16[120,2048]{1,0:T(8,128)(2,1)}, u32[]{:S(2)}, u32[]{:S(2)}) collective-permute-start(bf16[120,2048]{1,0:T(8,128)(2,1)S(1)} %slice_bitcast_fusion.1), channel_id=1, source_target_pairs={{0,2},{1,3},{2,4},{3,5},{4,6},{5,7},{6,0},{7,1},{8,10},{9,11},{10,... | collective-permute-start | bytes 1474568 | tf_op jit(solution)/shard_map/ppermute | solution.py:53
  118.9 9.9 %collective-permute-start.13 = (bf16[2,120,256]{2,1,0:T(8,128)(2,1)}, bf16[2,120,256]{2,1,0:T(8,128)(2,1)S(1)}, u32[]{:S(2)}, u32[]{:S(2)}) collective-permute-start(bf16[2,120,256]{2,1,0:T(8,128)(2,1)} %get-tuple-element.58), channel_id=1, source_target_pairs={{0,8},{1,9},{2,10},{3,11},{4,12},{5,13},{6,14},{7,15},{8,0},{9,1},... | collective-permute-start | bytes 368648 | tf_op jit(solution)/shard_map/ppermute | solution.py:53
  129.5 3.3 %collective-permute-start.15 = (bf16[120,2048]{1,0:T(8,128)(2,1)}, bf16[120,2048]{1,0:T(8,128)(2,1)S(1)}, u32[]{:S(2)}, u32[]{:S(2)}) collective-permute-start(bf16[120,2048]{1,0:T(8,128)(2,1)} %collective-permute-done.9.refs_0_), channel_id=1, source_target_pairs={{0,1},{1,0},{2,3},{3,2},{4,5},{5,4},{6,7},{7,6},{8,9},{9,8},{10,11... | collective-permute-start | bytes 1474568 | tf_op jit(solution)/shard_map/ppermute | solution.py:53
  130.4 2.4 %collective-permute-start.14 = (bf16[120,2048]{1,0:T(8,128)(2,1)S(1)}, bf16[120,2048]{1,0:T(8,128)(2,1)S(1)}, u32[]{:S(2)}, u32[]{:S(2)}) collective-permute-start(bf16[120,2048]{1,0:T(8,128)(2,1)S(1)} %collective-permute-done.10.refs_1_), channel_id=1, source_target_pairs={{0,1},{1,0},{2,3},{3,2},{4,5},{5,4},{6,7},{7,6},{8,9},{9,8},{10,11... | collective-permute-start | bytes 1474568 | tf_op jit(solution)/shard_map/ppermute | solution.py:53
  130.5 11.9 %collective-permute-start.17 = (bf16[4,120,256]{2,1,0:T(8,128)(2,1)}, bf16[4,120,256]{2,1,0:T(8,128)(2,1)S(1)}, u32[]{:S(2)}, u32[]{:S(2)}) collective-permute-start(bf16[4,120,256]{2,1,0:T(8,128)(2,1)} %get-tuple-element.62), channel_id=1, source_target_pairs={{0,8},{1,9},{2,10},{3,11},{4,12},{5,13},{6,14},{7,15},{8,0},{9,1},... | collective-permute-start | bytes 737288 | tf_op jit(solution)/shard_map/ppermute | solution.py:53
  138.2 13.1 %collective-permute-start.16 = (bf16[2,120,256]{2,1,0:T(8,128)(2,1)}, bf16[2,120,256]{2,1,0:T(8,128)(2,1)S(1)}, u32[]{:S(2)}, u32[]{:S(2)}) collective-permute-start(bf16[2,120,256]{2,1,0:T(8,128)(2,1)} %chi_far_out.1), channel_id=1, source_target_pairs={{0,8},{1,9},{2,10},{3,11},{4,12},{5,13},{6,14},{7,15},{8,0},{9,1},... | collective-permute-start | bytes 368648 | tf_op jit(solution)/shard_map/ppermute | solution.py:53
  (12 other events, 19.5 us)

commit v4 on v3

--- a/solution.py
+++ b/solution.py
@@ -9,7 +9,7 @@
 
 BOX = 64
 KC = 2048
-VMEM = 56 * 1024 * 1024
+VMEM = 32 * 1024 * 1024
 BF = jnp.bfloat16
 F32 = jnp.float32
 
@@ -96,9 +96,9 @@
     )(val, cond, zeta, weight, root)
 
 
-def rho_body(zeta, cond_a, cond_b, val_a, val_b, root, out, lhs, rhs, acc):
+def rho_body(zeta, cond, val_a, val_b, root, out, lhs, rhs, acc):
     step = pl.program_id(0)
-    conds = cond_a.shape[0]
+    conds = cond.shape[0]
     rows = zeta.shape[0]
 
     @pl.when(step == 0)
@@ -108,34 +108,29 @@
     rhs[0:128, :] = val_a[...]
     rhs[128:256, :] = val_b[...]
     lhs[0:rows, :] = zeta[...]
-    for side, cond in ((0, cond_a), (1, cond_b)):
-        for c in range(0, conds, 4):
-            left = jnp.concatenate(
-                [lhs[...] * cond[c + i : c + i + 1, :] for i in range(4)], axis=0
-            )
-            part = nt_dot(left, rhs[...])
-            first = (side * conds + c) * 128
-            span = slice(first, first + 512)
-            acc[span] = jnp.where(step == 0, part, acc[span] + part)
+    for c in range(0, conds, 4):
+        left = jnp.concatenate([lhs[...] * cond[c + i : c + i + 1, :] for i in range(4)], axis=0)
+        part = nt_dot(left, rhs[...])
+        span = slice(c * 128, (c + 4) * 128)
+        acc[span] = jnp.where(step == 0, part, acc[span] + part)
 
     @pl.when(step == pl.num_programs(0) - 1)
     def _():
-        for c in range(2 * conds):
+        for c in range(conds):
             block = acc[c * 128 : c * 128 + rows, :] * root[:, 0:1]
             out[0, :, c * 128 : (c + 1) * 128] = block[:, 0:128].astype(BF)
             out[1, :, c * 128 : (c + 1) * 128] = block[:, 128:256].astype(BF)
 
 
-def rho_kernel(zeta, cond_a, cond_b, val_a, val_b, root):
-    conds, points = cond_a.shape
+def rho_kernel(zeta, cond, val_a, val_b, root, name):
+    conds, points = cond.shape
     rows = zeta.shape[0]
-    pairs = 2 * conds * 128
+    pairs = conds * 128
     return pl.pallas_call(
         rho_body,
         grid=(points // KC,),
         in_specs=[
             pl.BlockSpec((rows, KC), lambda k: (0, k)),
-            pl.BlockSpec((conds, KC), lambda k: (0, k)),
             pl.BlockSpec((conds, KC), lambda k: (0, k)),
             pl.BlockSpec((128, KC), lambda k: (0, k)),
             pl.BlockSpec((128, KC), lambda k: (0, k)),
@@ -150,91 +145,55 @@
         ],
         compiler_params=pltpu.CompilerParams(vmem_limit_bytes=VMEM),
         cost_estimate=pl.CostEstimate(flops=1 << 20, bytes_accessed=1 << 16, transcendentals=0),
-        name="rho_rows",
-    )(zeta, cond_a, cond_b, val_a, val_b, root)
+        name=name,
+    )(zeta, cond, val_a, val_b, root)
 
 
 def chi_kernel(parts, sides, name):
-    arrays, picks = [], []
-    for first, second, crossed in parts:
-        pick = []
-        for array, index in (first, second):
-            known = [i for i, (a, x) in enumerate(arrays) if a is array]
-            if not known:
-                arrays.append((array, crossed))
-                known = [len(arrays) - 1]
-            pick.append((known[0], index))
-        picks.append(pick)
-    rows, depth = arrays[0][0].shape[-2:]
+    arrays = [array for part in parts for array in part[:2]]
+    crossed = [part[2] for part in parts]
+    rows, blk = arrays[0].shape[-2:]
     given, count = len(arrays), len(parts)
-    blk = depth // 2
-    slabs, found = [], []
+    slabs = [slab for halves, _ in sides for half in halves for slab in half]
+    places, at = [], 0
     for halves, _ in sides:
         for half in halves:
-            found.append([len(slabs), len(slabs) + len(half) - 1])
-            slabs += half
+            places.append([(at, 0), (at + len(half) - 1, blk if len(half) == 1 else 0)])
+            at += len(half)
     cols = slabs[0].shape[1]
 
     def body(*refs):
         ins = refs[:given]
         slab_refs = refs[given : given + len(slabs)]
         outs = refs[given + len(slabs) : given + len(slabs) + len(sides)]
-        lhs, acc = refs[given + len(slabs) + len(sides) :]
-        step = pl.program_id(0)
-
-        @pl.when(step == 0)
-        def _():
-            lhs[...] = jnp.zeros_like(lhs)
-
-        for half in range(2):
+        lhs = refs[-1]
+        lhs[...] = jnp.zeros_like(lhs)
+        totals = [None] * len(sides)
+        for side in range(2):
+            for half in range(2):
+                at = side * 2 + half
+                for i in range(count):
+                    other = 1 if crossed[i] else 0
+                    block = ins[2 * i + (side ^ other)][half ^ other]
+                    lhs[at, i * 128 : i * 128 + rows, :] = block
+                for which in range(len(sides)):
+                    slab, first = places[2 * which + half][side]
+                    part = jnp.dot(
+                        lhs[at], slab_refs[slab][first : first + blk], preferred_element_type=F32
+                    )
+                    totals[which] = part if totals[which] is None else totals[which] + part
+        for total, out in zip(totals, outs):
             for i in range(count):
-                array, index = picks[i][half]
-                block = ins[array][...] if index is None else ins[array][index]
-                lhs[half, i * 128 : i * 128 + rows, :] = block
-
-        def product(side, block):
-            first, second = found[2 * side][block], found[2 * side + 1][block]
-            return jnp.dot(
-                lhs[0], slab_refs[first][...], preferred_element_type=F32
-            ) + jnp.dot(lhs[1], slab_refs[second][...], preferred_element_type=F32)
-
-        @pl.when(step == 0)
-        def _():
-            for side in range(len(sides)):
-                acc[side] = product(side, 0)
-
-        @pl.when(step == 1)
-        def _():
-            for side, ref in enumerate(outs):
-                total = acc[side] + product(side, 1)
-                for i in range(count):
-                    ref[i] = total[i * 128 : i * 128 + rows, :].astype(ref.dtype)
-
-    def spec(array, crossed):
-        if array.ndim == 3:
-            return pl.BlockSpec((2, rows, blk), lambda k: (0, 0, 1 - k if crossed else k))
-        return pl.BlockSpec((rows, blk), lambda k: (0, 1 - k if crossed else k))
-
-    def slab_spec(slab):
-        if slab.shape[0] == blk:
-            return pl.BlockSpec((blk, cols), lambda k: (0, 0))
-        return pl.BlockSpec((blk, cols), lambda k: (k, 0))
-
-    whole = pl.BlockSpec((count, rows, cols), lambda k: (0, 0, 0))
+                out[i] = total[i * 128 : i * 128 + rows, :].astype(out.dtype)
+
     return pl.pallas_call(
         body,
-        grid=(2,),
-        in_specs=[spec(a, x) for a, x in arrays] + [slab_spec(slab) for slab in slabs],
-        out_specs=[whole] * len(sides),
         out_shape=[jax.ShapeDtypeStruct((count, rows, cols), dtype) for _, dtype in sides],
-        scratch_shapes=[
-            pltpu.VMEM((2, count * 128, blk), BF),
-            pltpu.VMEM((len(sides), count * 128, cols), F32),
-        ],
+        scratch_shapes=[pltpu.VMEM((4, count * 128, blk), BF)],
         compiler_params=pltpu.CompilerParams(vmem_limit_bytes=VMEM),
         cost_estimate=pl.CostEstimate(flops=1 << 20, bytes_accessed=1 << 16, transcendentals=0),
         name=name,
-    )(*[a for a, _ in arrays], *slabs)
+    )(*arrays, *slabs)
 
 
 def finish_kernel(place, chi, mine, theirs, before, name):
@@ -346,46 +305,52 @@
     own_00, other, cond_other = lax.optimization_barrier((own_00, other, cond_other))
     out_00 = send(own_00, Y_PAIR)
     out_10 = send(own_00, Y_CROSS)
-    rho = rho_kernel(zeta_rows, cond_mine, cond_other, mine, other, root_rows)
-    rho, cond_other, out_00, out_10 = lax.optimization_barrier((rho, cond_other, out_00, out_10))
-
-    from_down = send(rho, Z_UP)
-    from_up = send(rho, Z_DOWN)
-    rho_x = send(rho, CORE)
+
+    rho_0 = rho_kernel(zeta_rows, cond_mine, mine, other, root_rows, "rho_0")
+    rho_0, cond_other = lax.optimization_barrier((rho_0, cond_other))
+    down_0 = send(rho_0, Z_UP)
+    up_0 = send(rho_0, Z_DOWN)
+    rho_1 = rho_kernel(zeta_rows, cond_other, mine, other, root_rows, "rho_1")
+    rho_0x = send(rho_0, CORE)
+    rho_1, cond_other, out_00, out_10, rho_0x = lax.optimization_barrier(
+        (rho_1, cond_other, out_00, out_10, rho_0x)
+    )
+    down_1 = send(rho_1, Z_UP)
+    up_1 = send(rho_1, Z_DOWN)
     own_01 = slab_kernel(mine, cond_other, zeta_slab, weight[0][1], root_slab, "slab_01")
-    own_01, other = lax.optimization_barrier((own_01, other))
+    rho_1x = send(rho_1, CORE)
+    own_01, other, down_0, up_0, rho_1x = lax.optimization_barrier(
+        (own_01, other, down_0, up_0, rho_1x)
+    )
+    far_0 = send(down_0, Z_UP)
     out_01 = send(own_01, Y_PAIR)
     out_11 = send(own_01, Y_CROSS)
-    cond = jnp.concatenate([cond_mine, cond_other], axis=0)
-    own_1 = slab_kernel(other, cond, zeta_slab, weight[1][2], root_slab, "slab_1")
-    from_down, from_up, rho_x, out_01, out_11, own_1 = lax.optimization_barrier(
-        (from_down, from_up, rho_x, out_01, out_11, own_1)
+    own_10 = slab_kernel(other, cond_mine, zeta_slab, weight[1][0], root_slab, "slab_10")
+    own_10, other, down_1, up_1 = lax.optimization_barrier((own_10, other, down_1, up_1))
+    far_1 = send(up_1, Z_DOWN)
+    own_11 = slab_kernel(other, cond_other, zeta_slab, weight[1][1], root_slab, "slab_11")
+    own_11, out_01, out_11, far_0, far_1, down_0, up_0, down_1, up_1 = lax.optimization_barrier(
+        (own_11, out_01, out_11, far_0, far_1, down_0, up_0, down_1, up_1)
     )
     out_side = ([[out_00, out_01], [out_10, out_11]], BF)
-    in_side = ([[own_00, own_01], [own_1]], F32)
-
-    def both(array, crossed):
-        if crossed:
-            return ((array, 1), (array, 0), True)
-        return ((array, 0), (array, 1), False)
-
-    far_0 = send(from_down[0], Z_UP)
-    far_1 = send(from_up[1], Z_DOWN)
-    from_down_x = send(from_down, CORE)
-    from_up_x = send(from_up, CORE)
-    near = [both(rho, False), both(rho_x, True)]
+    in_side = ([[own_00, own_01], [own_10, own_11]], F32)
+
+    near = [(rho_0, rho_1, False), (rho_0x, rho_1x, True)]
     near_out, near_in = chi_kernel(near, [out_side, in_side], "chi_own")
     got_near = send(near_out, Y_PAIR)
-    mid = [both(from_down, False), both(from_down_x, True), both(from_up, False), both(from_up_x, True)]
+    mid = [
+        (down_0, down_1, False),
+        (send(down_0, CORE), send(down_1, CORE), True),
+        (up_0, up_1, False),
+        (send(up_0, CORE), send(up_1, CORE), True),
+    ]
     mid_out, mid_in = chi_kernel(mid, [out_side, in_side], "chi_next")
     got_mid = send(mid_out, Y_PAIR)
     far_0, far_1, near_in, mid_in, got_near = lax.optimization_barrier(
         (far_0, far_1, near_in, mid_in, got_near)
     )
 
-    far_0x = send(far_0, CORE)
-    far_1x = send(far_1, CORE)
-    far = [((far_0, None), (far_1, None), False), ((far_1x, None), (far_0x, None), True)]
+    far = [(far_0, far_1, False), (send(far_0, CORE), send(far_1, CORE), True)]
     (far_out,) = chi_kernel(far, [out_side], "chi_far_out")
     got_far = send(far_out, Y_PAIR)
     (far_in,) = chi_kernel(far, [in_side], "chi_far_in")

time: 155 us -> 147 us (0.948)
  Pallas kernels: 69.1 us -> 53.2 us
  waiting for transfers between devices: 10.7 us -> 17.6 us
  starting transfers between devices: 23 us -> 27.9 us
  other arithmetic: 5.98 us -> 3.07 us
  local copies, waits for them, and re-layouts: 10.7 us -> 8.86 us
    pallas_call x4, Pallas kernels: 19.2 us -> 7.98 us  [chi_kernel(): pl.pallas_call(body, out_shape=[jax.ShapeDtypeStruct((count, rows, cols),...]
    ppermute x18 -> x23, waiting for transfers between devices: 2.29 us -> 8.65 us  [send(): return lax.ppermute(value, ('band', 'grow'), pairs)]
    ppermute x18 -> x23, starting transfers between devices: 15.5 us -> 20.5 us  [send(): return lax.ppermute(value, ('band', 'grow'), pairs)]
    pallas_call x3, Pallas kernels: 9.65 us -> 6.62 us  [finish_kernel(): pl.pallas_call(body, grid_spec=pltpu.PrefetchScalarGridSpec(num_scalar_pr...]
    pallas_call x3 -> x4, Pallas kernels: 27.8 us -> 25 us  [slab_kernel(): pl.pallas_call(slab_body, grid=(points // KC,), in_specs=[pl.BlockSpec((1...]
    concatenate x3, other arithmetic: 1.86 us -> 0.23 us  [on_device(): place = jnp.concatenate([yl * 4 + slots, (1 - yl) * 4 + slots, core[None]])]
    pallas_call x1 -> x2, Pallas kernels: 12.4 us -> 13.6 us  [rho_kernel(): pl.pallas_call(rho_body, grid=(points // KC,), in_specs=[pl.BlockSpec((ro...]
    unnamed x50 -> x36, local copies, waits for them, and re-layouts: 6.06 us -> 5.8 us
  transfers between devices with their start and end apart: 19 -> 24, of which waited for: 3 -> 7; matrix products, arithmetic and copies ran while one was open for 4% -> 2% of each run, Pallas kernels for 43% -> 35%
where the time goes in v4:
time: 147 us; the launch traced here: 146 us
  Pallas kernels  53.2 us (36%)
  blocking collectives  31.2 us (21%)
  starting transfers between devices  27.9 us (19%)
  waiting for transfers between devices  17.6 us (12%)
  local copies, waits for them, and re-layouts  8.86 us (6%)
  between operations  4.2 us (3%)
  other arithmetic  3.07 us (2%)
    all_to_all x1, blocking collectives, on_device(): lax.all_to_all(jnp.broadcast_to(payload[None], (8, 16, width)), 'grow', s...  31.2 us
    pallas_call x4, Pallas kernels, slab_kernel(): pl.pallas_call(slab_body, grid=(points // KC,), in_specs=[pl.BlockSpec((1...  25 us
    ppermute x23, starting transfers between devices, send(): return lax.ppermute(value, ('band', 'grow'), pairs)  20.5 us
    pallas_call x2, Pallas kernels, rho_kernel(): pl.pallas_call(rho_body, grid=(points // KC,), in_specs=[pl.BlockSpec((ro...  13.6 us
    all_to_all x1, waiting for transfers between devices, on_device(): lax.all_to_all(pieces, 'band', split_axis=0, concat_axis=0, tiled=True)  8.91 us
    ppermute x23, waiting for transfers between devices, send(): return lax.ppermute(value, ('band', 'grow'), pairs)  8.65 us
    pallas_call x4, Pallas kernels, chi_kernel(): pl.pallas_call(body, out_shape=[jax.ShapeDtypeStruct((count, rows, cols),...  7.98 us
    all_to_all x1, starting transfers between devices, on_device(): lax.all_to_all(pieces, 'band', split_axis=0, concat_axis=0, tiled=True)  7.48 us
  transfers between devices with their start and end apart: 24, of which 7 were waited for; matrix products, arithmetic and copies ran while one was open for 2% of the time, Pallas kernels for 35%

profile of v4, /device:TPU:1, one launch (start us, length us, event | category | flops | bytes accessed | tf_op | source)
XLA Modules:
  0.0 146.0 jit_solution(14329525891029428777)
XLA Ops:
  0.1 1.0 dynamic-slice_bitcast_fusion.3
  1.1 1.8 %broadcast_select_fusion = bf16[8,8,8192]{2,1,0:T(8,128)(2,1)} fusion(pred[8]{0:T(512)(128)(4,1)} %constant.209, bf16[8,8192]{1,0:T(8,128)(2,1)S(1)} %get-tuple-element.96, bf16[8,8192]{1,0:T(8,128)(2,1)S(1)} %get-tuple-element.95), kind=kLoop, calls=%fused_computation.1 | loop fusion | flops 524288 | bytes 1310728 | tf_op jit(solution)/shard_map/jit(_where)/select_n | solution.py:266
  2.9 7.5 %all-to-all-start = ((bf16[8,8,8192]{2,1,0:T(8,128)(2,1)}), bf16[8,8,8192]{2,1,0:T(8,128)(2,1)S(1)}, u32[]{:S(2)}, u32[]{:S(2)}) async-start(bf16[8,8,8192]{2,1,0:T(8,128)(2,1)} %broadcast_select_fusion), calls=%async_computation | async-start | bytes 2097152 | tf_op jit(solution)/shard_map/all_to_all | solution.py:267
  16.9 8.9 %all-to-all-done = bf16[8,8,8192]{2,1,0:T(8,128)(2,1)S(1)} async-done(((bf16[8,8,8192]{2,1,0:T(8,128)(2,1)}), bf16[8,8,8192]{2,1,0:T(8,128)(2,1)S(1)}, u32[]{:S(2)}, u32[]{:S(2)}) %all-to-all-start) | async-done | bytes 1048608 | tf_op jit(solution)/shard_map/all_to_all | solution.py:267
  26.1 31.2 %all_to_all.10 = bf16[8,16,8704]{2,1,0:T(8,128)(2,1)S(1)} all-to-all(bf16[8,16,8704]{2,1,0:T(8,128)(2,1)S(1)} %broadcast_in_dim.74), channel_id=1, replica_groups={{0,2,4,6,8,10,12,14},{1,3,5,7,9,11,13,15},{16,18,20,22,24,26,28,30},{17..., dimensions={0} | all-to-all | bytes 4456448 | tf_op jit(solution)/shard_map/all_to_all | solution.py:292
  57.3 3.0 %collective-permute-start = (bf16[128,8704]{1,0:T(8,128)(2,1)S(1)}, bf16[128,8704]{1,0:T(8,128)(2,1)}, u32[]{:S(2)}, u32[]{:S(2)}) collective-permute-start(bf16[128,8704]{1,0:T(8,128)(2,1)S(1)} %bitcast.29), channel_id=1, source_target_pairs={{0,1},{1,0},{2,3},{3,2},{4,5},{5,4},{6,7},{7,6},{8,9},{9,8},{10,11... | collective-permute-start | bytes 6684680 | tf_op jit(solution)/shard_map/ppermute | solution.py:53
  60.5 2.2 %copy-done.1 = bf16[256,8192]{1,0:T(8,128)(2,1)S(1)} copy-done((bf16[256,8192]{1,0:T(8,128)(2,1)S(1)}, bf16[256,8192]{1,0:T(8,128)(2,1)}, u32[]{:S(2)}) %copy-start.1) | copy-done | bytes 4194328
  62.7 5.9 %slab_00.1.refs_8_.refs_12_.refs_4_ = bf16[1024,256]{1,0:T(8,128)(2,1)S(1)} custom-call(bf16[128,8704]{1,0:T(8,128)(2,1)S(1)} %bitcast.31, bf16[8,8192]{1,0:T(8,128)(2,1)S(1)} %reshape.52.cond, bf16[256,8192]{1,0:T(8,128)(2,1)S(1)} %copy-done.1, f32[128,8]{1,0:T(8,128)S(1)} %get-tuple-element.50.weight, f32[1,256]{1,0:T(1,128)S(1)} %bitcast.38), custom_call_target="tpu_custom_call" | custom-call | flops 1048576 | bytes 65536 | tf_op jit(solution)/shard_map/slab_00/pallas_call | solution.py:80
  68.6 1.5 %collective-permute-start.3 = (bf16[1024,256]{1,0:T(8,128)(2,1)S(1)}, bf16[1024,256]{1,0:T(8,128)(2,1)S(1)}, u32[]{:S(2)}, u32[]{:S(2)}) collective-permute-start(bf16[1024,256]{1,0:T(8,128)(2,1)S(1)} %slab_00.1.refs_8_.refs_12_.refs_4_), channel_id=1, source_target_pairs={{0,24},{1,25},{2,26},{3,27},{4,28},{5,29},{6,30},{7,31},{8,16},{9,... | collective-permute-start | bytes 1572872 | tf_op jit(solution)/shard_map/ppermute | solution.py:53
  70.7 6.8 %rho_0.1.refs_0_ = bf16[2,120,1024]{2,1,0:T(8,128)(2,1)S(1)} custom-call(bf16[120,8192]{1,0:T(8,128)(2,1)S(1)} %copy-done.4, bf16[8,8192]{1,0:T(8,128)(2,1)S(1)} %reshape.52.cond, bf16[128,8704]{1,0:T(8,128)(2,1)S(1)} %bitcast.32, bf16[128,8704]{1,0:T(8,128)(2,1)} %collective-permute-done.val_b.val, f32[120,128]{1,0:T(8,128)S(1)} %broadcast_in_dim.72.root), custom_call_target="tpu_custom_call" | custom-call | flops 1048576 | bytes 65536 | tf_op jit(solution)/shard_map/rho_0/pallas_call | solution.py:129
  77.5 1.1 collective-permute-start.4
  78.7 0.8 collective-permute-start.6
  80.2 6.8 %rho_1.1.refs_1_ = bf16[2,120,1024]{2,1,0:T(8,128)(2,1)S(1)} custom-call(bf16[120,8192]{1,0:T(8,128)(2,1)S(1)} %copy-done.4, bf16[8,8192]{1,0:T(8,128)(2,1)S(1)} %collective-permute-done.1.cond, bf16[128,8704]{1,0:T(8,128)(2,1)S(1)} %bitcast.33, bf16[128,8704]{1,0:T(8,128)(2,1)} %collective-permute-done.val_b.val, f32[120,128]{1,0:T(8,128)S(1)} %broadcast_in_dim.72.root), custom_call_target="tpu_custom_call" | custom-call | flops 1048576 | bytes 65536 | tf_op jit(solution)/shard_map/rho_1/pallas_call | solution.py:129
  87.7 2.1 %collective-permute-start.9 = (bf16[2,120,1024]{2,1,0:T(8,128)(2,1)S(1)}, bf16[2,120,1024]{2,1,0:T(8,128)(2,1)S(1)}, u32[]{:S(2)}, u32[]{:S(2)}) collective-permute-start(bf16[2,120,1024]{2,1,0:T(8,128)(2,1)S(1)} %rho_1.1.refs_1_), channel_id=1, source_target_pairs={{0,6},{1,7},{2,0},{3,1},{4,2},{5,3},{6,4},{7,5},{8,14},{9,15},{10,... | collective-permute-start | bytes 1474568 | tf_op jit(solution)/shard_map/ppermute | solution.py:53
  89.8 5.9 %slab_01.1.refs_9_.refs_13_.refs_5_ = bf16[1024,256]{1,0:T(8,128)(2,1)S(1)} custom-call(bf16[128,8704]{1,0:T(8,128)(2,1)S(1)} %bitcast.34, bf16[8,8192]{1,0:T(8,128)(2,1)S(1)} %collective-permute-done.1.cond, bf16[256,8192]{1,0:T(8,128)(2,1)S(1)} %copy-done.2, f32[128,8]{1,0:T(8,128)S(1)} %copy-done.11, f32[1,256]{1,0:T(1,128)S(1)} %bitcast.39), custom_call_target="tpu_custom_call" | custom-call | flops 1048576 | bytes 65536 | tf_op jit(solution)/shard_map/slab_01/pallas_call | solution.py:80
  96.6 0.8 collective-permute-start.10
  97.4 6.6 %slab_10.1.refs_10_.refs_14_.refs_6_ = bf16[1024,256]{1,0:T(8,128)(2,1)S(1)} custom-call(bf16[128,8704]{1,0:T(8,128)(2,1)} %collective-permute-done.val_b.val, bf16[8,8192]{1,0:T(8,128)(2,1)S(1)} %reshape.52.cond, bf16[256,8192]{1,0:T(8,128)(2,1)S(1)} %copy-done.2, f32[128,8]{1,0:T(8,128)S(1)} %get-tuple-element.62.weight, f32[1,256]{1,0:T(1,128)S(1)} %bitcast.40), custom_call_target="tpu_custom_call" | custom-call | flops 1048576 | bytes 65536 | tf_op jit(solution)/shard_map/slab_10/pallas_call | solution.py:80
  104.0 2.7 %collective-permute-start.13 = (bf16[2,120,1024]{2,1,0:T(8,128)(2,1)S(1)}, bf16[2,120,1024]{2,1,0:T(8,128)(2,1)}, u32[]{:S(2)}, u32[]{:S(2)}) collective-permute-start(bf16[2,120,1024]{2,1,0:T(8,128)(2,1)S(1)} %collective-permute-done.9.refs_5_), channel_id=1, source_target_pairs={{0,6},{1,7},{2,0},{3,1},{4,2},{5,3},{6,4},{7,5},{8,14},{9,15},{10,... | collective-permute-start | bytes 1474568 | tf_op jit(solution)/shard_map/ppermute | solution.py:53
  106.7 6.6 %slab_11.1.refs_11_.refs_15_.refs_7_ = bf16[1024,256]{1,0:T(8,128)(2,1)S(1)} custom-call(bf16[128,8704]{1,0:T(8,128)(2,1)} %collective-permute-done.val_b.val, bf16[8,8192]{1,0:T(8,128)(2,1)S(1)} %collective-permute-done.1.cond, bf16[256,8192]{1,0:T(8,128)(2,1)S(1)} %copy-done.2, f32[128,8]{1,0:T(8,128)S(1)} %get-tuple-element.64.weight, f32[1,256]{1,0:T(1,128)S(1)} %bitcast.41), custom_call_target="tpu_custom_call" | custom-call | flops 1048576 | bytes 65536 | tf_op jit(solution)/shard_map/slab_11/pallas_call | solution.py:80
  113.3 2.7 %collective-permute-done.13.refs_1_ = bf16[2,120,1024]{2,1,0:T(8,128)(2,1)} collective-permute-done((bf16[2,120,1024]{2,1,0:T(8,128)(2,1)S(1)}, bf16[2,120,1024]{2,1,0:T(8,128)(2,1)}, u32[]{:S(2)}, u32[]{:S(2)}) %collective-permute-start.13) | collective-permute-done | bytes 491552 | tf_op jit(solution)/shard_map/ppermute | solution.py:53
  116.0 3.2 %collective-permute-done.12.refs_0_ = bf16[2,120,1024]{2,1,0:T(8,128)(2,1)} collective-permute-done((bf16[2,120,1024]{2,1,0:T(8,128)(2,1)S(1)}, bf16[2,120,1024]{2,1,0:T(8,128)(2,1)}, u32[]{:S(2)}, u32[]{:S(2)}) %collective-permute-start.12) | collective-permute-done | bytes 491552 | tf_op jit(solution)/shard_map/ppermute | solution.py:53
  119.3 2.4 %collective-permute-start.14 = (bf16[2,120,1024]{2,1,0:T(8,128)(2,1)S(1)}, bf16[2,120,1024]{2,1,0:T(8,128)(2,1)S(1)}, u32[]{:S(2)}, u32[]{:S(2)}) collective-permute-start(bf16[2,120,1024]{2,1,0:T(8,128)(2,1)S(1)} %collective-permute-done.5.refs_0_), channel_id=1, source_target_pairs={{0,1},{1,0},{2,3},{3,2},{4,5},{5,4},{6,7},{7,6},{8,9},{9,8},{10,11... | collective-permute-start | bytes 1474568 | tf_op jit(solution)/shard_map/ppermute | solution.py:53
  122.3 1.3 chi_own.1
  125.3 2.3 %chi_next.1 = (bf16[4,120,256]{2,1,0:T(8,128)(2,1)S(1)}, f32[4,120,256]{2,1,0:T(8,128)S(1)}) custom-call(bf16[2,120,1024]{2,1,0:T(8,128)(2,1)S(1)} %collective-permute-done.5.refs_0_, bf16[2,120,1024]{2,1,0:T(8,128)(2,1)S(1)} %collective-permute-done.8.refs_1_, bf16[2,120,1024]{2,1,0:T(8,128)(2,1)S(1)} %collective-permute-done.14.refs_2_, ...), custom_call_target="tpu_custom_call" | custom-call | flops 1048576 | bytes 65536 | tf_op jit(solution)/shard_map/chi_next/pallas_call | solution.py:189
  130.4 0.9 collective-permute-done.19.refs_2_
  132.0 1.0 copy-done.6
  133.1 1.0 copy-done.8
  134.1 2.2 %chi_far_out.1 = bf16[2,120,256]{2,1,0:T(8,128)(2,1)S(1)} custom-call(bf16[2,120,1024]{2,1,0:T(8,128)(2,1)} %collective-permute-done.12.refs_0_, bf16[2,120,1024]{2,1,0:T(8,128)(2,1)} %collective-permute-done.13.refs_1_, bf16[2,120,1024]{2,1,0:T(8,128)(2,1)} %collective-permute-done.19.refs_2_, bf16[2,120,1024]{2,1,0:T(8,128)(2,1)} %collective-permute-done.20.refs_3_, ...), custom_call_target="tpu_custom_call" | custom-call | flops 1048576 | bytes 65536 | tf_op jit(solution)/shard_map/chi_far_out/pallas_call | solution.py:189
  137.2 1.4 finish_own.1.rest_0_
  138.6 3.8 %finish_next.1.rest_0_ = f32[16,120,256]{2,1,0:T(8,128)} custom-call(s32[5]{0:T(128)S(1)} %pad_add_fusion.1.place_ref, f32[16,120,256]{2,1,0:T(8,128)S(1)} %bitcast.36, f32[4,120,256]{2,1,0:T(8,128)S(1)} %copy-done.10, bf16[4,120,256]{2,1,0:T(8,128)(2,1)} %collective-permute-done.22.theirs_ref, ...), custom_call_target="tpu_custom_call", output_to_operand_aliasing={{}: (4, {})} | custom-call | flops 1048576 | bytes 65536 | tf_op jit(solution)/shard_map/finish_next/pallas_call | solution.py:227
  142.4 2.2 %chi_far_in.1.mine_ref = f32[2,120,256]{2,1,0:T(8,128)S(1)} custom-call(bf16[2,120,1024]{2,1,0:T(8,128)(2,1)} %collective-permute-done.12.refs_0_, bf16[2,120,1024]{2,1,0:T(8,128)(2,1)} %collective-permute-done.13.refs_1_, bf16[2,120,1024]{2,1,0:T(8,128)(2,1)} %collective-permute-done.19.refs_2_, bf16[2,120,1024]{2,1,0:T(8,128)(2,1)} %collective-permute-done.20.refs_3_, ...), custom_call_target="tpu_custom_call" | custom-call | flops 1048576 | bytes 65536 | tf_op jit(solution)/shard_map/chi_far_in/pallas_call | solution.py:189
  144.6 1.4 finish_far.1
  (99 shorter events, 12.7 us)
Async XLA Ops:
  0.0 10.8 %copy-start = (f32[8,128]{1,0:T(8,128)S(1)}, f32[8,128]{1,0:T(8,128)}, u32[]{:S(2)}) copy-start(f32[8,128]{1,0:T(8,128)} %param.15) | copy-start | bytes 12292
  0.0 10.4 %copy-start.16 = (f32[16]{0:T(128)S(1)}, f32[16]{0:T(128)}, u32[]{:S(2)}) copy-start(f32[16]{0:T(128)} %param.17) | copy-start | bytes 196
  0.1 14.7 %copy-start.13 = (bf16[1,8192]{1,0:T(2,128)(2,1)S(1)}, bf16[1,8192]{1,0:T(2,128)(2,1)}, u32[]{:S(2)}) copy-start(bf16[1,8192]{1,0:T(2,128)(2,1)} %param.16) | copy-start | bytes 49156
  0.1 16.1 %copy-start.15 = (s32[256]{0:T(256)S(1)}, s32[256]{0:T(256)}, u32[]{:S(2)}) copy-start(s32[256]{0:T(256)} %param.20) | copy-start | bytes 3076
  2.9 23.0 %all-to-all-start = ((bf16[8,8,8192]{2,1,0:T(8,128)(2,1)}), bf16[8,8,8192]{2,1,0:T(8,128)(2,1)S(1)}, u32[]{:S(2)}, u32[]{:S(2)}) async-start(bf16[8,8,8192]{2,1,0:T(8,128)(2,1)} %broadcast_select_fusion), calls=%async_computation | async-start | bytes 2097152 | tf_op jit(solution)/shard_map/all_to_all | solution.py:267
  57.3 11.3 %collective-permute-start = (bf16[128,8704]{1,0:T(8,128)(2,1)S(1)}, bf16[128,8704]{1,0:T(8,128)(2,1)}, u32[]{:S(2)}, u32[]{:S(2)}) collective-permute-start(bf16[128,8704]{1,0:T(8,128)(2,1)S(1)} %bitcast.29), channel_id=1, source_target_pairs={{0,1},{1,0},{2,3},{3,2},{4,5},{5,4},{6,7},{7,6},{8,9},{9,8},{10,11... | collective-permute-start | bytes 6684680 | tf_op jit(solution)/shard_map/ppermute | solution.py:53
  60.4 8.2 %collective-permute-start.1 = (bf16[8,8192]{1,0:T(8,128)(2,1)S(1)}, bf16[8,8192]{1,0:T(8,128)(2,1)S(1)}, u32[]{:S(2)}, u32[]{:S(2)}) collective-permute-start(bf16[8,8192]{1,0:T(8,128)(2,1)S(1)} %reshape.52.cond), channel_id=1, source_target_pairs={{0,1},{1,0},{2,3},{3,2},{4,5},{5,4},{6,7},{7,6},{8,9},{9,8},{10,11... | collective-permute-start | bytes 393224 | tf_op jit(solution)/shard_map/ppermute | solution.py:53
  68.6 18.3 %collective-permute-start.3 = (bf16[1024,256]{1,0:T(8,128)(2,1)S(1)}, bf16[1024,256]{1,0:T(8,128)(2,1)S(1)}, u32[]{:S(2)}, u32[]{:S(2)}) collective-permute-start(bf16[1024,256]{1,0:T(8,128)(2,1)S(1)} %slab_00.1.refs_8_.refs_12_.refs_4_), channel_id=1, source_target_pairs={{0,24},{1,25},{2,26},{3,27},{4,28},{5,29},{6,30},{7,31},{8,16},{9,... | collective-permute-start | bytes 1572872 | tf_op jit(solution)/shard_map/ppermute | solution.py:53
  70.1 16.9 %collective-permute-start.2 = (bf16[1024,256]{1,0:T(8,128)(2,1)S(1)}, bf16[1024,256]{1,0:T(8,128)(2,1)S(1)}, u32[]{:S(2)}, u32[]{:S(2)}) collective-permute-start(bf16[1024,256]{1,0:T(8,128)(2,1)S(1)} %slab_00.1.refs_8_.refs_12_.refs_4_), channel_id=1, source_target_pairs={{0,8},{1,9},{2,10},{3,11},{4,12},{5,13},{6,14},{7,15},{8,0},{9,1},... | collective-permute-start | bytes 1572872 | tf_op jit(solution)/shard_map/ppermute | solution.py:53
  77.5 12.3 %copy-start.2 = (bf16[256,8192]{1,0:T(8,128)(2,1)S(1)}, bf16[256,8192]{1,0:T(8,128)(2,1)}, u32[]{:S(2)}) copy-start(bf16[256,8192]{1,0:T(8,128)(2,1)} %zeta.11) | copy-start | bytes 12582916
  77.5 12.3 %copy-start.11 = (f32[128,8]{1,0:T(8,128)S(1)}, f32[128,8]{1,0:T(8,128)}, u32[]{:S(2)}) copy-start(f32[128,8]{1,0:T(8,128)} %get-tuple-element.59.weight) | copy-start | bytes 12292
  77.5 9.4 %collective-permute-start.4 = (bf16[2,120,1024]{2,1,0:T(8,128)(2,1)S(1)}, bf16[2,120,1024]{2,1,0:T(8,128)(2,1)S(1)}, u32[]{:S(2)}, u32[]{:S(2)}) collective-permute-start(bf16[2,120,1024]{2,1,0:T(8,128)(2,1)S(1)} %rho_0.1.refs_0_), channel_id=1, source_target_pairs={{0,1},{1,0},{2,3},{3,2},{4,5},{5,4},{6,7},{7,6},{8,9},{9,8},{10,11... | collective-permute-start | bytes 1474568 | tf_op jit(solution)/shard_map/ppermute | solution.py:53
  78.7 17.0 %collective-permute-start.6 = (bf16[2,120,1024]{2,1,0:T(8,128)(2,1)S(1)}, bf16[2,120,1024]{2,1,0:T(8,128)(2,1)S(1)}, u32[]{:S(2)}, u32[]{:S(2)}) collective-permute-start(bf16[2,120,1024]{2,1,0:T(8,128)(2,1)S(1)} %rho_0.1.refs_0_), channel_id=1, source_target_pairs={{0,6},{1,7},{2,0},{3,1},{4,2},{5,3},{6,4},{7,5},{8,14},{9,15},{10,... | collective-permute-start | bytes 1474568 | tf_op jit(solution)/shard_map/ppermute | solution.py:53
  79.5 16.2 %collective-permute-start.5 = (bf16[2,120,1024]{2,1,0:T(8,128)(2,1)S(1)}, bf16[2,120,1024]{2,1,0:T(8,128)(2,1)S(1)}, u32[]{:S(2)}, u32[]{:S(2)}) collective-permute-start(bf16[2,120,1024]{2,1,0:T(8,128)(2,1)S(1)} %rho_0.1.refs_0_), channel_id=1, source_target_pairs={{0,2},{1,3},{2,4},{3,5},{4,6},{5,7},{6,0},{7,1},{8,10},{9,11},{10,... | collective-permute-start | bytes 1474568 | tf_op jit(solution)/shard_map/ppermute | solution.py:53
  87.0 38.3 %copy-start.5 = (bf16[1024,256]{1,0:T(8,128)(2,1)}, bf16[1024,256]{1,0:T(8,128)(2,1)S(1)}, u32[]{:S(2)}) copy-start(bf16[1024,256]{1,0:T(8,128)(2,1)S(1)} %collective-permute-done.3.refs_6_.refs_10_) | copy-start | bytes 1572868
  87.0 38.3 %copy-start.7 = (bf16[1024,256]{1,0:T(8,128)(2,1)}, bf16[1024,256]{1,0:T(8,128)(2,1)S(1)}, u32[]{:S(2)}) copy-start(bf16[1024,256]{1,0:T(8,128)(2,1)S(1)} %collective-permute-done.2.refs_4_.refs_8_) | copy-start | bytes 1572868
  87.0 8.7 %collective-permute-start.7 = (bf16[2,120,1024]{2,1,0:T(8,128)(2,1)S(1)}, bf16[2,120,1024]{2,1,0:T(8,128)(2,1)S(1)}, u32[]{:S(2)}, u32[]{:S(2)}) collective-permute-start(bf16[2,120,1024]{2,1,0:T(8,128)(2,1)S(1)} %rho_1.1.refs_1_), channel_id=1, source_target_pairs={{0,1},{1,0},{2,3},{3,2},{4,5},{5,4},{6,7},{7,6},{8,9},{9,8},{10,11... | collective-permute-start | bytes 1474568 | tf_op jit(solution)/shard_map/ppermute | solution.py:53
  87.7 16.2 %collective-permute-start.9 = (bf16[2,120,1024]{2,1,0:T(8,128)(2,1)S(1)}, bf16[2,120,1024]{2,1,0:T(8,128)(2,1)S(1)}, u32[]{:S(2)}, u32[]{:S(2)}) collective-permute-start(bf16[2,120,1024]{2,1,0:T(8,128)(2,1)S(1)} %rho_1.1.refs_1_), channel_id=1, source_target_pairs={{0,6},{1,7},{2,0},{3,1},{4,2},{5,3},{6,4},{7,5},{8,14},{9,15},{10,... | collective-permute-start | bytes 1474568 | tf_op jit(solution)/shard_map/ppermute | solution.py:53
  89.8 14.2 %collective-permute-start.8 = (bf16[2,120,1024]{2,1,0:T(8,128)(2,1)S(1)}, bf16[2,120,1024]{2,1,0:T(8,128)(2,1)S(1)}, u32[]{:S(2)}, u32[]{:S(2)}) collective-permute-start(bf16[2,120,1024]{2,1,0:T(8,128)(2,1)S(1)} %rho_1.1.refs_1_), channel_id=1, source_target_pairs={{0,2},{1,3},{2,4},{3,5},{4,6},{5,7},{6,0},{7,1},{8,10},{9,11},{10,... | collective-permute-start | bytes 1474568 | tf_op jit(solution)/shard_map/ppermute | solution.py:53
  95.7 23.5 %collective-permute-start.11 = (bf16[1024,256]{1,0:T(8,128)(2,1)S(1)}, bf16[1024,256]{1,0:T(8,128)(2,1)S(1)}, u32[]{:S(2)}, u32[]{:S(2)}) collective-permute-start(bf16[1024,256]{1,0:T(8,128)(2,1)S(1)} %slab_01.1.refs_9_.refs_13_.refs_5_), channel_id=1, source_target_pairs={{0,24},{1,25},{2,26},{3,27},{4,28},{5,29},{6,30},{7,31},{8,16},{9,... | collective-permute-start | bytes 1572872 | tf_op jit(solution)/shard_map/ppermute | solution.py:53
  96.6 22.7 %collective-permute-start.10 = (bf16[1024,256]{1,0:T(8,128)(2,1)S(1)}, bf16[1024,256]{1,0:T(8,128)(2,1)S(1)}, u32[]{:S(2)}, u32[]{:S(2)}) collective-permute-start(bf16[1024,256]{1,0:T(8,128)(2,1)S(1)} %slab_01.1.refs_9_.refs_13_.refs_5_), channel_id=1, source_target_pairs={{0,8},{1,9},{2,10},{3,11},{4,12},{5,13},{6,14},{7,15},{8,0},{9,1},... | collective-permute-start | bytes 1572872 | tf_op jit(solution)/shard_map/ppermute | solution.py:53
  104.0 12.0 %collective-permute-start.13 = (bf16[2,120,1024]{2,1,0:T(8,128)(2,1)S(1)}, bf16[2,120,1024]{2,1,0:T(8,128)(2,1)}, u32[]{:S(2)}, u32[]{:S(2)}) collective-permute-start(bf16[2,120,1024]{2,1,0:T(8,128)(2,1)S(1)} %collective-permute-done.9.refs_5_), channel_id=1, source_target_pairs={{0,6},{1,7},{2,0},{3,1},{4,2},{5,3},{6,4},{7,5},{8,14},{9,15},{10,... | collective-permute-start | bytes 1474568 | tf_op jit(solution)/shard_map/ppermute | solution.py:53
  106.7 12.6 %collective-permute-start.12 = (bf16[2,120,1024]{2,1,0:T(8,128)(2,1)S(1)}, bf16[2,120,1024]{2,1,0:T(8,128)(2,1)}, u32[]{:S(2)}, u32[]{:S(2)}) collective-permute-start(bf16[2,120,1024]{2,1,0:T(8,128)(2,1)S(1)} %collective-permute-done.5.refs_0_), channel_id=1, source_target_pairs={{0,2},{1,3},{2,4},{3,5},{4,6},{5,7},{6,0},{7,1},{8,10},{9,11},{10,... | collective-permute-start | bytes 1474568 | tf_op jit(solution)/shard_map/ppermute | solution.py:53
  119.3 5.0 %collective-permute-start.14 = (bf16[2,120,1024]{2,1,0:T(8,128)(2,1)S(1)}, bf16[2,120,1024]{2,1,0:T(8,128)(2,1)S(1)}, u32[]{:S(2)}, u32[]{:S(2)}) collective-permute-start(bf16[2,120,1024]{2,1,0:T(8,128)(2,1)S(1)} %collective-permute-done.5.refs_0_), channel_id=1, source_target_pairs={{0,1},{1,0},{2,3},{3,2},{4,5},{5,4},{6,7},{7,6},{8,9},{9,8},{10,11... | collective-permute-start | bytes 1474568 | tf_op jit(solution)/shard_map/ppermute | solution.py:53
  121.7 2.6 %collective-permute-start.15 = (bf16[2,120,1024]{2,1,0:T(8,128)(2,1)S(1)}, bf16[2,120,1024]{2,1,0:T(8,128)(2,1)S(1)}, u32[]{:S(2)}, u32[]{:S(2)}) collective-permute-start(bf16[2,120,1024]{2,1,0:T(8,128)(2,1)S(1)} %collective-permute-done.8.refs_1_), channel_id=1, source_target_pairs={{0,1},{1,0},{2,3},{3,2},{4,5},{5,4},{6,7},{7,6},{8,9},{9,8},{10,11... | collective-permute-start | bytes 1474568 | tf_op jit(solution)/shard_map/ppermute | solution.py:53
  121.8 2.8 %collective-permute-start.16 = (bf16[2,120,1024]{2,1,0:T(8,128)(2,1)S(1)}, bf16[2,120,1024]{2,1,0:T(8,128)(2,1)S(1)}, u32[]{:S(2)}, u32[]{:S(2)}) collective-permute-start(bf16[2,120,1024]{2,1,0:T(8,128)(2,1)S(1)} %collective-permute-done.6.refs_4_), channel_id=1, source_target_pairs={{0,1},{1,0},{2,3},{3,2},{4,5},{5,4},{6,7},{7,6},{8,9},{9,8},{10,11... | collective-permute-start | bytes 1474568 | tf_op jit(solution)/shard_map/ppermute | solution.py:53
  122.2 3.1 %collective-permute-start.17 = (bf16[2,120,1024]{2,1,0:T(8,128)(2,1)S(1)}, bf16[2,120,1024]{2,1,0:T(8,128)(2,1)S(1)}, u32[]{:S(2)}, u32[]{:S(2)}) collective-permute-start(bf16[2,120,1024]{2,1,0:T(8,128)(2,1)S(1)} %collective-permute-done.9.refs_5_), channel_id=1, source_target_pairs={{0,1},{1,0},{2,3},{3,2},{4,5},{5,4},{6,7},{7,6},{8,9},{9,8},{10,11... | collective-permute-start | bytes 1474568 | tf_op jit(solution)/shard_map/ppermute | solution.py:53
  123.5 4.9 %collective-permute-start.18 = (bf16[2,120,256]{2,1,0:T(8,128)(2,1)S(1)}, bf16[2,120,256]{2,1,0:T(8,128)(2,1)S(1)}, u32[]{:S(2)}, u32[]{:S(2)}) collective-permute-start(bf16[2,120,256]{2,1,0:T(8,128)(2,1)S(1)} %get-tuple-element.86), channel_id=1, source_target_pairs={{0,8},{1,9},{2,10},{3,11},{4,12},{5,13},{6,14},{7,15},{8,0},{9,1},... | collective-permute-start | bytes 368648 | tf_op jit(solution)/shard_map/ppermute | solution.py:53
  129.1 2.2 %collective-permute-start.19 = (bf16[2,120,1024]{2,1,0:T(8,128)(2,1)}, bf16[2,120,1024]{2,1,0:T(8,128)(2,1)}, u32[]{:S(2)}, u32[]{:S(2)}) collective-permute-start(bf16[2,120,1024]{2,1,0:T(8,128)(2,1)} %collective-permute-done.12.refs_0_), channel_id=1, source_target_pairs={{0,1},{1,0},{2,3},{3,2},{4,5},{5,4},{6,7},{7,6},{8,9},{9,8},{10,11... | collective-permute-start | bytes 1474568 | tf_op jit(solution)/shard_map/ppermute | solution.py:53
  129.5 2.5 %collective-permute-start.20 = (bf16[2,120,1024]{2,1,0:T(8,128)(2,1)}, bf16[2,120,1024]{2,1,0:T(8,128)(2,1)}, u32[]{:S(2)}, u32[]{:S(2)}) collective-permute-start(bf16[2,120,1024]{2,1,0:T(8,128)(2,1)} %collective-permute-done.13.refs_1_), channel_id=1, source_target_pairs={{0,1},{1,0},{2,3},{3,2},{4,5},{5,4},{6,7},{7,6},{8,9},{9,8},{10,11... | collective-permute-start | bytes 1474568 | tf_op jit(solution)/shard_map/ppermute | solution.py:53
  129.7 8.9 %collective-permute-start.22 = (bf16[4,120,256]{2,1,0:T(8,128)(2,1)}, bf16[4,120,256]{2,1,0:T(8,128)(2,1)}, u32[]{:S(2)}, u32[]{:S(2)}) collective-permute-start(bf16[4,120,256]{2,1,0:T(8,128)(2,1)} %copy-done.12), channel_id=1, source_target_pairs={{0,8},{1,9},{2,10},{3,11},{4,12},{5,13},{6,14},{7,15},{8,0},{9,1},... | collective-permute-start | bytes 737288 | tf_op jit(solution)/shard_map/ppermute | solution.py:53
  136.3 8.3 %collective-permute-start.21 = (bf16[2,120,256]{2,1,0:T(8,128)(2,1)S(1)}, bf16[2,120,256]{2,1,0:T(8,128)(2,1)S(1)}, u32[]{:S(2)}, u32[]{:S(2)}) collective-permute-start(bf16[2,120,256]{2,1,0:T(8,128)(2,1)S(1)} %chi_far_out.1), channel_id=1, source_target_pairs={{0,8},{1,9},{2,10},{3,11},{4,12},{5,13},{6,14},{7,15},{8,0},{9,1},... | collective-permute-start | bytes 368648 | tf_op jit(solution)/shard_map/ppermute | solution.py:53
  (10 other events, 42.6 us)

commit v5 on v4

--- a/solution.py
+++ b/solution.py
@@ -9,7 +9,7 @@
 
 BOX = 64
 KC = 2048
-VMEM = 32 * 1024 * 1024
+VMEM = 16 * 1024 * 1024
 BF = jnp.bfloat16
 F32 = jnp.float32
 
@@ -196,44 +196,49 @@
     )(*arrays, *slabs)
 
 
-def finish_kernel(place, chi, mine, theirs, before, name):
-    blocks, rows, cols = chi.shape
-    count = mine.shape[0] // 2
-
-    def body(place_ref, chi_ref, mine_ref, theirs_ref, *rest):
-        out = rest[-1]
+def finish_kernel(place, chi, sources, before, name):
+    _, rows, cols = chi.shape
+    counts = [source[4] for source in sources]
+    firsts = [sum(counts[:i]) for i in range(len(counts))]
+
+    def body(place_ref, chi_ref, *refs):
+        out = refs[-1]
         step = pl.program_id(0)
-        core = place_ref[2 * count]
-        for first, src in ((0, mine_ref), (count, theirs_ref)):
+        core = place_ref[sum(counts)]
+        for i, (first, count) in enumerate(zip(firsts, counts)):
 
             @pl.when(jnp.logical_and(step >= first, step < first + count))
-            def _(src=src):
-                out[core] = chi_ref[core] - src[0].astype(F32)
-                out[1 - core] = chi_ref[1 - core] - src[1].astype(F32)
-
-    def where(i, place_ref):
-        return (place_ref[i], 0, 0)
-
-    block = (2, rows, cols)
-    specs = [
-        pl.BlockSpec(block, where),
-        pl.BlockSpec(block, lambda i, place_ref: (jnp.minimum(i, count - 1), 0, 0)),
-        pl.BlockSpec(block, lambda i, place_ref: (jnp.maximum(i - count, 0), 0, 0)),
-    ]
-    operands = [place, chi, mine, theirs]
+            def _(mine=refs[2 * i], theirs=refs[2 * i + 1]):
+                out[core] = chi_ref[core] - mine[0].astype(F32)
+                out[1 - core] = chi_ref[1 - core] - theirs[0].astype(F32)
+
+    def where(i, p):
+        return (p[i], 0, 0)
+
+    def slot(first, count, start):
+        return lambda i, p: (start + jnp.clip(i - first, 0, count - 1), 0, 0)
+
+    specs = [pl.BlockSpec((2, rows, cols), where)]
+    operands = [place, chi]
+    for (mine, start, theirs, start_x, count), first in zip(sources, firsts):
+        specs.append(pl.BlockSpec((1, rows, cols), slot(first, count, start)))
+        specs.append(pl.BlockSpec((1, rows, cols), slot(first, count, start_x)))
+        operands += [mine, theirs]
+    aliases = {}
     if before is not None:
+        aliases = {len(operands): 0}
         specs.append(pl.BlockSpec(memory_space=pl.ANY))
         operands.append(before)
     return pl.pallas_call(
         body,
         grid_spec=pltpu.PrefetchScalarGridSpec(
             num_scalar_prefetch=1,
-            grid=(2 * count,),
+            grid=(sum(counts),),
             in_specs=specs,
-            out_specs=pl.BlockSpec(block, where),
+            out_specs=pl.BlockSpec((2, rows, cols), where),
         ),
         out_shape=jax.ShapeDtypeStruct(chi.shape, F32),
-        input_output_aliases={} if before is None else {4: 0},
+        input_output_aliases=aliases,
         compiler_params=pltpu.CompilerParams(vmem_limit_bytes=VMEM),
         cost_estimate=pl.CostEstimate(flops=1 << 20, bytes_accessed=1 << 16, transcendentals=0),
         name=name,
@@ -329,45 +334,56 @@
     own_10, other, down_1, up_1 = lax.optimization_barrier((own_10, other, down_1, up_1))
     far_1 = send(up_1, Z_DOWN)
     own_11 = slab_kernel(other, cond_other, zeta_slab, weight[1][1], root_slab, "slab_11")
-    own_11, out_01, out_11, far_0, far_1, down_0, up_0, down_1, up_1 = lax.optimization_barrier(
-        (own_11, out_01, out_11, far_0, far_1, down_0, up_0, down_1, up_1)
-    )
     out_side = ([[out_00, out_01], [out_10, out_11]], BF)
     in_side = ([[own_00, own_01], [own_10, own_11]], F32)
 
-    near = [(rho_0, rho_1, False), (rho_0x, rho_1x, True)]
-    near_out, near_in = chi_kernel(near, [out_side, in_side], "chi_own")
+    own = [(rho_0, rho_1, False), (rho_0x, rho_1x, True)]
+    own_out, own_in = chi_kernel(own, [out_side, in_side], "chi_own")
+    got_own = send(own_out, Y_PAIR)
+    near = [(down_0, down_1, False), (up_0, up_1, False)]
+    near_out, near_in = chi_kernel(near, [out_side, in_side], "chi_near")
     got_near = send(near_out, Y_PAIR)
+    own_in, near_in, far_0, far_1, down_0, up_0, down_1, up_1, got_own = lax.optimization_barrier(
+        (own_in, near_in, far_0, far_1, down_0, up_0, down_1, up_1, got_own)
+    )
+
     mid = [
-        (down_0, down_1, False),
         (send(down_0, CORE), send(down_1, CORE), True),
-        (up_0, up_1, False),
         (send(up_0, CORE), send(up_1, CORE), True),
     ]
     mid_out, mid_in = chi_kernel(mid, [out_side, in_side], "chi_next")
     got_mid = send(mid_out, Y_PAIR)
-    far_0, far_1, near_in, mid_in, got_near = lax.optimization_barrier(
-        (far_0, far_1, near_in, mid_in, got_near)
-    )
-
-    far = [(far_0, far_1, False), (send(far_0, CORE), send(far_1, CORE), True)]
-    (far_out,) = chi_kernel(far, [out_side], "chi_far_out")
+    far_0x, far_1x = send(far_0, CORE), send(far_1, CORE)
+    far_0x, far_1x, mid_in, got_near = lax.optimization_barrier((far_0x, far_1x, mid_in, got_near))
+    far = [(far_0, far_1, False), (far_0x, far_1x, True)]
+    far_out, far_in = chi_kernel(far, [out_side, in_side], "chi_far")
     got_far = send(far_out, Y_PAIR)
-    (far_in,) = chi_kernel(far, [in_side], "chi_far_in")
 
     yl = grow // 8
     z = yz % 4
+
+    def blocks(*pairs):
+        return jnp.stack([side * 4 + (z + s) % 4 for side, s in pairs] + [core]).astype(jnp.int32)
+
     total_rows, cols = chi_prev.shape
-    done = None
     chi = chi_prev.reshape(16, total_rows // 16, cols)
-    for steps, inner, outer, name in (
-        ((0,), near_in, got_near, "finish_own"),
-        ((3, 1), mid_in, got_mid, "finish_next"),
-        ((2,), far_in, got_far, "finish_far"),
-    ):
-        slots = jnp.stack([(z + s) % 4 for s in steps])
-        place = jnp.concatenate([yl * 4 + slots, (1 - yl) * 4 + slots, core[None]])
-        done = finish_kernel(place.astype(jnp.int32), chi, inner, outer, done, name)
+    here, there = yl, 1 - yl
+    done = finish_kernel(
+        blocks((here, 0), (here, 3), (here, 1), (here, 2), (there, 0), (there, 3), (there, 1)),
+        chi,
+        [
+            (own_in, 0, own_in, 1, 1),
+            (near_in, 0, mid_in, 0, 2),
+            (far_in, 0, far_in, 1, 1),
+            (got_own, 0, got_own, 1, 1),
+            (got_near, 0, got_mid, 0, 2),
+        ],
+        None,
+        "finish_most",
+    )
+    done = finish_kernel(
+        blocks((there, 2)), chi, [(got_far, 0, got_far, 1, 1)], done, "finish_far"
+    )
     return done.reshape(total_rows, cols)
 
 

time: 147 us -> 137 us (0.932)
  Pallas kernels: 53.2 us -> 49.6 us
  local copies, waits for them, and re-layouts: 8.86 us -> 5.36 us
  waiting for transfers between devices: 17.6 us -> 15.3 us
    unnamed x36 -> x20, local copies, waits for them, and re-layouts: 5.8 us -> 2.22 us
    ppermute x23 -> x24, waiting for transfers between devices: 8.65 us -> 5.77 us  [send(): return lax.ppermute(value, ('band', 'grow'), pairs)]
    pallas_call x3 -> x2, Pallas kernels: 6.62 us -> 4.78 us  [finish_kernel(): pl.pallas_call(body, grid_spec=pltpu.PrefetchScalarGridSpec(num_scalar_pr...]
    pallas_call x4, Pallas kernels: 7.98 us -> 6.32 us  [chi_kernel(): pl.pallas_call(body, out_shape=[jax.ShapeDtypeStruct((count, rows, cols),...]
    ppermute x23 -> x24, starting transfers between devices: 20.5 us -> 21.2 us  [send(): return lax.ppermute(value, ('band', 'grow'), pairs)]
  transfers between devices with their start and end apart: 24 -> 25, of which waited for: 7 -> 9; matrix products, arithmetic and copies ran while one was open for 2% -> 2% of each run, Pallas kernels for 35% -> 35%
where the time goes in v5:
time: 137 us
  Pallas kernels  49.6 us (36%)
  blocking collectives  31.2 us (23%)
  starting transfers between devices  28.7 us (21%)
  waiting for transfers between devices  15.3 us (11%)
  local copies, waits for them, and re-layouts  5.36 us (4%)
  between operations  4.17 us (3%)
  other arithmetic  2.23 us (2%)
    all_to_all x1, blocking collectives, on_device(): lax.all_to_all(jnp.broadcast_to(payload[None], (8, 16, width)), 'grow', s...  31.2 us
    pallas_call x4, Pallas kernels, slab_kernel(): pl.pallas_call(slab_body, grid=(points // KC,), in_specs=[pl.BlockSpec((1...  24.9 us
    ppermute x24, starting transfers between devices, send(): return lax.ppermute(value, ('band', 'grow'), pairs)  21.2 us
    pallas_call x2, Pallas kernels, rho_kernel(): pl.pallas_call(rho_body, grid=(points // KC,), in_specs=[pl.BlockSpec((ro...  13.6 us
    all_to_all x1, waiting for transfers between devices, on_device(): lax.all_to_all(pieces, 'band', split_axis=0, concat_axis=0, tiled=True)  9.52 us
    all_to_all x1, starting transfers between devices, on_device(): lax.all_to_all(pieces, 'band', split_axis=0, concat_axis=0, tiled=True)  7.48 us
    pallas_call x4, Pallas kernels, chi_kernel(): pl.pallas_call(body, out_shape=[jax.ShapeDtypeStruct((count, rows, cols),...  6.32 us
    ppermute x24, waiting for transfers between devices, send(): return lax.ppermute(value, ('band', 'grow'), pairs)  5.77 us
  transfers between devices with their start and end apart: 25, of which 9 were waited for; matrix products, arithmetic and copies ran while one was open for 2% of the time, Pallas kernels for 35%

profile of v5, /device:TPU:1, one launch (start us, length us, event | category | flops | bytes accessed | tf_op | source)
XLA Modules:
  0.0 136.6 jit_solution(5210089905665589555)
XLA Ops:
  0.1 1.0 dynamic-slice_bitcast_fusion.3
  1.1 1.8 %broadcast_select_fusion = bf16[8,8,8192]{2,1,0:T(8,128)(2,1)} fusion(pred[8]{0:T(512)(128)(4,1)} %constant.217, bf16[8,8192]{1,0:T(8,128)(2,1)S(1)} %get-tuple-element.102, bf16[8,8192]{1,0:T(8,128)(2,1)S(1)} %get-tuple-element.101), kind=kLoop, calls=%fused_computation.1 | loop fusion | flops 524288 | bytes 1310728 | tf_op jit(solution)/shard_map/jit(_where)/select_n | solution.py:271
  2.9 7.5 %all-to-all-start = ((bf16[8,8,8192]{2,1,0:T(8,128)(2,1)}), bf16[8,8,8192]{2,1,0:T(8,128)(2,1)S(1)}, u32[]{:S(2)}, u32[]{:S(2)}) async-start(bf16[8,8,8192]{2,1,0:T(8,128)(2,1)} %broadcast_select_fusion), calls=%async_computation | async-start | bytes 2097152 | tf_op jit(solution)/shard_map/all_to_all | solution.py:272
  16.3 9.5 %all-to-all-done = bf16[8,8,8192]{2,1,0:T(8,128)(2,1)S(1)} async-done(((bf16[8,8,8192]{2,1,0:T(8,128)(2,1)}), bf16[8,8,8192]{2,1,0:T(8,128)(2,1)S(1)}, u32[]{:S(2)}, u32[]{:S(2)}) %all-to-all-start) | async-done | bytes 1048608 | tf_op jit(solution)/shard_map/all_to_all | solution.py:272
  26.1 31.2 %all_to_all.10 = bf16[8,16,8704]{2,1,0:T(8,128)(2,1)S(1)} all-to-all(bf16[8,16,8704]{2,1,0:T(8,128)(2,1)S(1)} %broadcast_in_dim.68), channel_id=1, replica_groups={{0,2,4,6,8,10,12,14},{1,3,5,7,9,11,13,15},{16,18,20,22,24,26,28,30},{17..., dimensions={0} | all-to-all | bytes 4456448 | tf_op jit(solution)/shard_map/all_to_all | solution.py:297
  57.3 3.0 %collective-permute-start = (bf16[128,8704]{1,0:T(8,128)(2,1)S(1)}, bf16[128,8704]{1,0:T(8,128)(2,1)}, u32[]{:S(2)}, u32[]{:S(2)}) collective-permute-start(bf16[128,8704]{1,0:T(8,128)(2,1)S(1)} %bitcast.31), channel_id=1, source_target_pairs={{0,1},{1,0},{2,3},{3,2},{4,5},{5,4},{6,7},{7,6},{8,9},{9,8},{10,11... | collective-permute-start | bytes 6684680 | tf_op jit(solution)/shard_map/ppermute | solution.py:53
  60.5 2.2 %copy-done.1 = bf16[256,8192]{1,0:T(8,128)(2,1)S(1)} copy-done((bf16[256,8192]{1,0:T(8,128)(2,1)S(1)}, bf16[256,8192]{1,0:T(8,128)(2,1)}, u32[]{:S(2)}) %copy-start.1) | copy-done | bytes 4194328
  62.7 5.9 %slab_00.1.refs_8_ = bf16[1024,256]{1,0:T(8,128)(2,1)S(1)} custom-call(bf16[128,8704]{1,0:T(8,128)(2,1)S(1)} %bitcast.33, bf16[8,8192]{1,0:T(8,128)(2,1)S(1)} %reshape.48.cond, bf16[256,8192]{1,0:T(8,128)(2,1)S(1)} %copy-done.1, f32[128,8]{1,0:T(8,128)S(1)} %get-tuple-element.53.weight, f32[1,256]{1,0:T(1,128)S(1)} %bitcast.39), custom_call_target="tpu_custom_call" | custom-call | flops 1048576 | bytes 65536 | tf_op jit(solution)/shard_map/slab_00/pallas_call | solution.py:80
  68.6 1.5 %collective-permute-start.3 = (bf16[1024,256]{1,0:T(8,128)(2,1)S(1)}, bf16[1024,256]{1,0:T(8,128)(2,1)S(1)}, u32[]{:S(2)}, u32[]{:S(2)}) collective-permute-start(bf16[1024,256]{1,0:T(8,128)(2,1)S(1)} %slab_00.1.refs_8_), channel_id=1, source_target_pairs={{0,24},{1,25},{2,26},{3,27},{4,28},{5,29},{6,30},{7,31},{8,16},{9,... | collective-permute-start | bytes 1572872 | tf_op jit(solution)/shard_map/ppermute | solution.py:53
  70.7 6.8 %rho_0.1.refs_0_ = bf16[2,120,1024]{2,1,0:T(8,128)(2,1)S(1)} custom-call(bf16[120,8192]{1,0:T(8,128)(2,1)S(1)} %copy-done.4, bf16[8,8192]{1,0:T(8,128)(2,1)S(1)} %reshape.48.cond, bf16[128,8704]{1,0:T(8,128)(2,1)S(1)} %bitcast.34, bf16[128,8704]{1,0:T(8,128)(2,1)} %collective-permute-done.val_b.val, f32[120,128]{1,0:T(8,128)S(1)} %broadcast_in_dim.66.root), custom_call_target="tpu_custom_call" | custom-call | flops 1048576 | bytes 65536 | tf_op jit(solution)/shard_map/rho_0/pallas_call | solution.py:129
  77.5 1.1 collective-permute-start.4
  78.7 0.8 collective-permute-start.6
  80.1 6.8 %rho_1.1.refs_1_ = bf16[2,120,1024]{2,1,0:T(8,128)(2,1)S(1)} custom-call(bf16[120,8192]{1,0:T(8,128)(2,1)S(1)} %copy-done.4, bf16[8,8192]{1,0:T(8,128)(2,1)S(1)} %collective-permute-done.1.cond, bf16[128,8704]{1,0:T(8,128)(2,1)S(1)} %bitcast.35, bf16[128,8704]{1,0:T(8,128)(2,1)} %collective-permute-done.val_b.val, f32[120,128]{1,0:T(8,128)S(1)} %broadcast_in_dim.66.root), custom_call_target="tpu_custom_call" | custom-call | flops 1048576 | bytes 65536 | tf_op jit(solution)/shard_map/rho_1/pallas_call | solution.py:129
  87.0 0.7 collective-permute-start.7
  87.7 2.1 %collective-permute-start.11 = (bf16[2,120,1024]{2,1,0:T(8,128)(2,1)S(1)}, bf16[2,120,1024]{2,1,0:T(8,128)(2,1)S(1)}, u32[]{:S(2)}, u32[]{:S(2)}) collective-permute-start(bf16[2,120,1024]{2,1,0:T(8,128)(2,1)S(1)} %rho_1.1.refs_1_), channel_id=1, source_target_pairs={{0,6},{1,7},{2,0},{3,1},{4,2},{5,3},{6,4},{7,5},{8,14},{9,15},{10,... | collective-permute-start | bytes 1474568 | tf_op jit(solution)/shard_map/ppermute | solution.py:53
  89.8 5.9 %slab_01.1.refs_9_ = bf16[1024,256]{1,0:T(8,128)(2,1)S(1)} custom-call(bf16[128,8704]{1,0:T(8,128)(2,1)S(1)} %bitcast.36, bf16[8,8192]{1,0:T(8,128)(2,1)S(1)} %collective-permute-done.1.cond, bf16[256,8192]{1,0:T(8,128)(2,1)S(1)} %copy-done.2, f32[128,8]{1,0:T(8,128)S(1)} %get-tuple-element.64.weight, f32[1,256]{1,0:T(1,128)S(1)} %bitcast.40), custom_call_target="tpu_custom_call" | custom-call | flops 1048576 | bytes 65536 | tf_op jit(solution)/shard_map/slab_01/pallas_call | solution.py:80
  95.7 0.8 collective-permute-start.9
  96.5 0.8 collective-permute-start.8
  97.3 6.6 %slab_10.1.refs_10_ = bf16[1024,256]{1,0:T(8,128)(2,1)S(1)} custom-call(bf16[128,8704]{1,0:T(8,128)(2,1)} %collective-permute-done.val_b.val, bf16[8,8192]{1,0:T(8,128)(2,1)S(1)} %reshape.48.cond, bf16[256,8192]{1,0:T(8,128)(2,1)S(1)} %copy-done.2, f32[128,8]{1,0:T(8,128)S(1)} %get-tuple-element.70.weight, f32[1,256]{1,0:T(1,128)S(1)} %bitcast.41), custom_call_target="tpu_custom_call" | custom-call | flops 1048576 | bytes 65536 | tf_op jit(solution)/shard_map/slab_10/pallas_call | solution.py:80
  104.0 2.7 %collective-permute-start.13 = (bf16[2,120,1024]{2,1,0:T(8,128)(2,1)S(1)}, bf16[2,120,1024]{2,1,0:T(8,128)(2,1)S(1)}, u32[]{:S(2)}, u32[]{:S(2)}) collective-permute-start(bf16[2,120,1024]{2,1,0:T(8,128)(2,1)S(1)} %collective-permute-done.11.refs_3_), channel_id=1, source_target_pairs={{0,6},{1,7},{2,0},{3,1},{4,2},{5,3},{6,4},{7,5},{8,14},{9,15},{10,... | collective-permute-start | bytes 1474568 | tf_op jit(solution)/shard_map/ppermute | solution.py:53
  106.7 6.6 %slab_11.1.refs_11_ = bf16[1024,256]{1,0:T(8,128)(2,1)S(1)} custom-call(bf16[128,8704]{1,0:T(8,128)(2,1)} %collective-permute-done.val_b.val, bf16[8,8192]{1,0:T(8,128)(2,1)S(1)} %collective-permute-done.1.cond, bf16[256,8192]{1,0:T(8,128)(2,1)S(1)} %copy-done.2, f32[128,8]{1,0:T(8,128)S(1)} %get-tuple-element.73.weight, f32[1,256]{1,0:T(1,128)S(1)} %bitcast.42), custom_call_target="tpu_custom_call" | custom-call | flops 1048576 | bytes 65536 | tf_op jit(solution)/shard_map/slab_11/pallas_call | solution.py:80
  113.3 1.3 chi_own.1
  114.6 0.7 collective-permute-start.14
  115.3 1.3 chi_near.1
  116.5 2.6 %collective-permute-done.12.refs_0_ = bf16[2,120,1024]{2,1,0:T(8,128)(2,1)S(1)} collective-permute-done((bf16[2,120,1024]{2,1,0:T(8,128)(2,1)S(1)}, bf16[2,120,1024]{2,1,0:T(8,128)(2,1)S(1)}, u32[]{:S(2)}, u32[]{:S(2)}) %collective-permute-start.12) | collective-permute-done | bytes 491552 | tf_op jit(solution)/shard_map/ppermute | solution.py:53
  119.1 2.4 %collective-permute-start.17 = (bf16[2,120,1024]{2,1,0:T(8,128)(2,1)S(1)}, bf16[2,120,1024]{2,1,0:T(8,128)(2,1)S(1)}, u32[]{:S(2)}, u32[]{:S(2)}) collective-permute-start(bf16[2,120,1024]{2,1,0:T(8,128)(2,1)S(1)} %collective-permute-done.5.refs_0_), channel_id=1, source_target_pairs={{0,1},{1,0},{2,3},{3,2},{4,5},{5,4},{6,7},{7,6},{8,9},{9,8},{10,11... | collective-permute-start | bytes 1474568 | tf_op jit(solution)/shard_map/ppermute | solution.py:53
  124.4 0.7 collective-permute-done.20.refs_3_
  125.1 1.9 %chi_next.1 = (bf16[2,120,256]{2,1,0:T(8,128)(2,1)}, f32[2,120,256]{2,1,0:T(8,128)S(1)}) custom-call(bf16[2,120,1024]{2,1,0:T(8,128)(2,1)S(1)} %collective-permute-done.17.refs_0_, bf16[2,120,1024]{2,1,0:T(8,128)(2,1)S(1)} %collective-permute-done.18.refs_1_, bf16[2,120,1024]{2,1,0:T(8,128)(2,1)S(1)} %collective-permute-done.19.refs_2_, ...), custom_call_target="tpu_custom_call" | custom-call | flops 1048576 | bytes 65536 | tf_op jit(solution)/shard_map/chi_next/pallas_call | solution.py:189
  128.3 1.9 %chi_far.1 = (bf16[2,120,256]{2,1,0:T(8,128)(2,1)}, f32[2,120,256]{2,1,0:T(8,128)S(1)}) custom-call(bf16[2,120,1024]{2,1,0:T(8,128)(2,1)S(1)} %collective-permute-done.12.refs_0_, bf16[2,120,1024]{2,1,0:T(8,128)(2,1)S(1)} %collective-permute-done.13.refs_1_, bf16[2,120,1024]{2,1,0:T(8,128)(2,1)S(1)} %collective-permute-done.15.refs_2_, ...), custom_call_target="tpu_custom_call" | custom-call | flops 1048576 | bytes 65536 | tf_op jit(solution)/shard_map/chi_far/pallas_call | solution.py:189
  130.9 0.8 collective-permute-done.23.refs_9_
  131.8 3.5 %finish_most.1.refs_2_ = f32[16,120,256]{2,1,0:T(8,128)} custom-call(s32[8]{0:T(128)S(1)} %stack.44.place_ref, f32[16,120,256]{2,1,0:T(8,128)S(1)} %bitcast.37, f32[2,120,256]{2,1,0:T(8,128)S(1)} %get-tuple-element.92.refs_0_.refs_1_, f32[2,120,256]{2,1,0:T(8,128)S(1)} %get-tuple-element.92.refs_0_.refs_1_, f32[2,120,256]{2,1,0:T(8,128)S(1)} %get-tuple-element.93.refs_2_, ...), custom_call_target="tpu_custom_call" | custom-call | flops 1048576 | bytes 65536 | tf_op jit(solution)/shard_map/finish_most/pallas_call | solution.py:232
  135.3 1.3 finish_far.1
  (82 shorter events, 8.8 us)
Async XLA Ops:
  0.0 10.8 %copy-start = (f32[8,128]{1,0:T(8,128)S(1)}, f32[8,128]{1,0:T(8,128)}, u32[]{:S(2)}) copy-start(f32[8,128]{1,0:T(8,128)} %param.15) | copy-start | bytes 12292
  0.0 10.3 %copy-start.6 = (s32[2]{0:T(128)S(1)}, s32[2]{0:T(128)}, u32[]{:S(2)}) copy-start(s32[2]{0:T(128)} %param.18) | copy-start | bytes 28
  0.0 10.4 %copy-start.9 = (s32[120]{0:T(128)S(1)}, s32[120]{0:T(128)}, u32[]{:S(2)}) copy-start(s32[120]{0:T(128)} %param.19) | copy-start | bytes 1444
  0.0 10.4 %copy-start.8 = (f32[16]{0:T(128)S(1)}, f32[16]{0:T(128)}, u32[]{:S(2)}) copy-start(f32[16]{0:T(128)} %param.17) | copy-start | bytes 196
  0.1 14.7 %copy-start.5 = (bf16[1,8192]{1,0:T(2,128)(2,1)S(1)}, bf16[1,8192]{1,0:T(2,128)(2,1)}, u32[]{:S(2)}) copy-start(bf16[1,8192]{1,0:T(2,128)(2,1)} %param.16) | copy-start | bytes 49156
  0.1 16.1 %copy-start.7 = (s32[256]{0:T(256)S(1)}, s32[256]{0:T(256)}, u32[]{:S(2)}) copy-start(s32[256]{0:T(256)} %param.20) | copy-start | bytes 3076
  2.9 23.0 %all-to-all-start = ((bf16[8,8,8192]{2,1,0:T(8,128)(2,1)}), bf16[8,8,8192]{2,1,0:T(8,128)(2,1)S(1)}, u32[]{:S(2)}, u32[]{:S(2)}) async-start(bf16[8,8,8192]{2,1,0:T(8,128)(2,1)} %broadcast_select_fusion), calls=%async_computation | async-start | bytes 2097152 | tf_op jit(solution)/shard_map/all_to_all | solution.py:272
  57.3 11.3 %collective-permute-start = (bf16[128,8704]{1,0:T(8,128)(2,1)S(1)}, bf16[128,8704]{1,0:T(8,128)(2,1)}, u32[]{:S(2)}, u32[]{:S(2)}) collective-permute-start(bf16[128,8704]{1,0:T(8,128)(2,1)S(1)} %bitcast.31), channel_id=1, source_target_pairs={{0,1},{1,0},{2,3},{3,2},{4,5},{5,4},{6,7},{7,6},{8,9},{9,8},{10,11... | collective-permute-start | bytes 6684680 | tf_op jit(solution)/shard_map/ppermute | solution.py:53
  60.4 8.2 %collective-permute-start.1 = (bf16[8,8192]{1,0:T(8,128)(2,1)S(1)}, bf16[8,8192]{1,0:T(8,128)(2,1)S(1)}, u32[]{:S(2)}, u32[]{:S(2)}) collective-permute-start(bf16[8,8192]{1,0:T(8,128)(2,1)S(1)} %reshape.48.cond), channel_id=1, source_target_pairs={{0,1},{1,0},{2,3},{3,2},{4,5},{5,4},{6,7},{7,6},{8,9},{9,8},{10,11... | collective-permute-start | bytes 393224 | tf_op jit(solution)/shard_map/ppermute | solution.py:53
  68.6 18.3 %collective-permute-start.3 = (bf16[1024,256]{1,0:T(8,128)(2,1)S(1)}, bf16[1024,256]{1,0:T(8,128)(2,1)S(1)}, u32[]{:S(2)}, u32[]{:S(2)}) collective-permute-start(bf16[1024,256]{1,0:T(8,128)(2,1)S(1)} %slab_00.1.refs_8_), channel_id=1, source_target_pairs={{0,24},{1,25},{2,26},{3,27},{4,28},{5,29},{6,30},{7,31},{8,16},{9,... | collective-permute-start | bytes 1572872 | tf_op jit(solution)/shard_map/ppermute | solution.py:53
  70.1 16.9 %collective-permute-start.2 = (bf16[1024,256]{1,0:T(8,128)(2,1)S(1)}, bf16[1024,256]{1,0:T(8,128)(2,1)S(1)}, u32[]{:S(2)}, u32[]{:S(2)}) collective-permute-start(bf16[1024,256]{1,0:T(8,128)(2,1)S(1)} %slab_00.1.refs_8_), channel_id=1, source_target_pairs={{0,8},{1,9},{2,10},{3,11},{4,12},{5,13},{6,14},{7,15},{8,0},{9,1},... | collective-permute-start | bytes 1572872 | tf_op jit(solution)/shard_map/ppermute | solution.py:53
  77.5 12.2 %copy-start.2 = (bf16[256,8192]{1,0:T(8,128)(2,1)S(1)}, bf16[256,8192]{1,0:T(8,128)(2,1)}, u32[]{:S(2)}) copy-start(bf16[256,8192]{1,0:T(8,128)(2,1)} %zeta.11) | copy-start | bytes 12582916
  77.5 9.4 %collective-permute-start.4 = (bf16[2,120,1024]{2,1,0:T(8,128)(2,1)S(1)}, bf16[2,120,1024]{2,1,0:T(8,128)(2,1)S(1)}, u32[]{:S(2)}, u32[]{:S(2)}) collective-permute-start(bf16[2,120,1024]{2,1,0:T(8,128)(2,1)S(1)} %rho_0.1.refs_0_), channel_id=1, source_target_pairs={{0,1},{1,0},{2,3},{3,2},{4,5},{5,4},{6,7},{7,6},{8,9},{9,8},{10,11... | collective-permute-start | bytes 1474568 | tf_op jit(solution)/shard_map/ppermute | solution.py:53
  78.7 17.0 %collective-permute-start.6 = (bf16[2,120,1024]{2,1,0:T(8,128)(2,1)S(1)}, bf16[2,120,1024]{2,1,0:T(8,128)(2,1)S(1)}, u32[]{:S(2)}, u32[]{:S(2)}) collective-permute-start(bf16[2,120,1024]{2,1,0:T(8,128)(2,1)S(1)} %rho_0.1.refs_0_), channel_id=1, source_target_pairs={{0,6},{1,7},{2,0},{3,1},{4,2},{5,3},{6,4},{7,5},{8,14},{9,15},{10,... | collective-permute-start | bytes 1474568 | tf_op jit(solution)/shard_map/ppermute | solution.py:53
  79.5 16.2 %collective-permute-start.5 = (bf16[2,120,1024]{2,1,0:T(8,128)(2,1)S(1)}, bf16[2,120,1024]{2,1,0:T(8,128)(2,1)S(1)}, u32[]{:S(2)}, u32[]{:S(2)}) collective-permute-start(bf16[2,120,1024]{2,1,0:T(8,128)(2,1)S(1)} %rho_0.1.refs_0_), channel_id=1, source_target_pairs={{0,2},{1,3},{2,4},{3,5},{4,6},{5,7},{6,0},{7,1},{8,10},{9,11},{10,... | collective-permute-start | bytes 1474568 | tf_op jit(solution)/shard_map/ppermute | solution.py:53
  87.0 8.7 %collective-permute-start.7 = (bf16[2,120,1024]{2,1,0:T(8,128)(2,1)S(1)}, bf16[2,120,1024]{2,1,0:T(8,128)(2,1)S(1)}, u32[]{:S(2)}, u32[]{:S(2)}) collective-permute-start(bf16[2,120,1024]{2,1,0:T(8,128)(2,1)S(1)} %rho_1.1.refs_1_), channel_id=1, source_target_pairs={{0,1},{1,0},{2,3},{3,2},{4,5},{5,4},{6,7},{7,6},{8,9},{9,8},{10,11... | collective-permute-start | bytes 1474568 | tf_op jit(solution)/shard_map/ppermute | solution.py:53
  87.7 16.2 %collective-permute-start.11 = (bf16[2,120,1024]{2,1,0:T(8,128)(2,1)S(1)}, bf16[2,120,1024]{2,1,0:T(8,128)(2,1)S(1)}, u32[]{:S(2)}, u32[]{:S(2)}) collective-permute-start(bf16[2,120,1024]{2,1,0:T(8,128)(2,1)S(1)} %rho_1.1.refs_1_), channel_id=1, source_target_pairs={{0,6},{1,7},{2,0},{3,1},{4,2},{5,3},{6,4},{7,5},{8,14},{9,15},{10,... | collective-permute-start | bytes 1474568 | tf_op jit(solution)/shard_map/ppermute | solution.py:53
  89.8 14.2 %collective-permute-start.10 = (bf16[2,120,1024]{2,1,0:T(8,128)(2,1)S(1)}, bf16[2,120,1024]{2,1,0:T(8,128)(2,1)S(1)}, u32[]{:S(2)}, u32[]{:S(2)}) collective-permute-start(bf16[2,120,1024]{2,1,0:T(8,128)(2,1)S(1)} %rho_1.1.refs_1_), channel_id=1, source_target_pairs={{0,2},{1,3},{2,4},{3,5},{4,6},{5,7},{6,0},{7,1},{8,10},{9,11},{10,... | collective-permute-start | bytes 1474568 | tf_op jit(solution)/shard_map/ppermute | solution.py:53
  95.7 17.6 %collective-permute-start.9 = (bf16[1024,256]{1,0:T(8,128)(2,1)S(1)}, bf16[1024,256]{1,0:T(8,128)(2,1)S(1)}, u32[]{:S(2)}, u32[]{:S(2)}) collective-permute-start(bf16[1024,256]{1,0:T(8,128)(2,1)S(1)} %slab_01.1.refs_9_), channel_id=1, source_target_pairs={{0,24},{1,25},{2,26},{3,27},{4,28},{5,29},{6,30},{7,31},{8,16},{9,... | collective-permute-start | bytes 1572872 | tf_op jit(solution)/shard_map/ppermute | solution.py:53
  96.5 16.8 %collective-permute-start.8 = (bf16[1024,256]{1,0:T(8,128)(2,1)S(1)}, bf16[1024,256]{1,0:T(8,128)(2,1)S(1)}, u32[]{:S(2)}, u32[]{:S(2)}) collective-permute-start(bf16[1024,256]{1,0:T(8,128)(2,1)S(1)} %slab_01.1.refs_9_), channel_id=1, source_target_pairs={{0,8},{1,9},{2,10},{3,11},{4,12},{5,13},{6,14},{7,15},{8,0},{9,1},... | collective-permute-start | bytes 1572872 | tf_op jit(solution)/shard_map/ppermute | solution.py:53
  104.0 12.5 %collective-permute-start.13 = (bf16[2,120,1024]{2,1,0:T(8,128)(2,1)S(1)}, bf16[2,120,1024]{2,1,0:T(8,128)(2,1)S(1)}, u32[]{:S(2)}, u32[]{:S(2)}) collective-permute-start(bf16[2,120,1024]{2,1,0:T(8,128)(2,1)S(1)} %collective-permute-done.11.refs_3_), channel_id=1, source_target_pairs={{0,6},{1,7},{2,0},{3,1},{4,2},{5,3},{6,4},{7,5},{8,14},{9,15},{10,... | collective-permute-start | bytes 1474568 | tf_op jit(solution)/shard_map/ppermute | solution.py:53
  106.7 12.5 %collective-permute-start.12 = (bf16[2,120,1024]{2,1,0:T(8,128)(2,1)S(1)}, bf16[2,120,1024]{2,1,0:T(8,128)(2,1)S(1)}, u32[]{:S(2)}, u32[]{:S(2)}) collective-permute-start(bf16[2,120,1024]{2,1,0:T(8,128)(2,1)S(1)} %collective-permute-done.5.refs_0_), channel_id=1, source_target_pairs={{0,2},{1,3},{2,4},{3,5},{4,6},{5,7},{6,0},{7,1},{8,10},{9,11},{10,... | collective-permute-start | bytes 1474568 | tf_op jit(solution)/shard_map/ppermute | solution.py:53
  114.6 4.6 %collective-permute-start.14 = (bf16[2,120,256]{2,1,0:T(8,128)(2,1)S(1)}, bf16[2,120,256]{2,1,0:T(8,128)(2,1)S(1)}, u32[]{:S(2)}, u32[]{:S(2)}) collective-permute-start(bf16[2,120,256]{2,1,0:T(8,128)(2,1)S(1)} %get-tuple-element.80), channel_id=1, source_target_pairs={{0,8},{1,9},{2,10},{3,11},{4,12},{5,13},{6,14},{7,15},{8,0},{9,1},... | collective-permute-start | bytes 368648 | tf_op jit(solution)/shard_map/ppermute | solution.py:53
  119.1 3.9 %collective-permute-start.17 = (bf16[2,120,1024]{2,1,0:T(8,128)(2,1)S(1)}, bf16[2,120,1024]{2,1,0:T(8,128)(2,1)S(1)}, u32[]{:S(2)}, u32[]{:S(2)}) collective-permute-start(bf16[2,120,1024]{2,1,0:T(8,128)(2,1)S(1)} %collective-permute-done.5.refs_0_), channel_id=1, source_target_pairs={{0,1},{1,0},{2,3},{3,2},{4,5},{5,4},{6,7},{7,6},{8,9},{9,8},{10,11... | collective-permute-start | bytes 1474568 | tf_op jit(solution)/shard_map/ppermute | solution.py:53
  121.5 2.2 %collective-permute-start.18 = (bf16[2,120,1024]{2,1,0:T(8,128)(2,1)S(1)}, bf16[2,120,1024]{2,1,0:T(8,128)(2,1)S(1)}, u32[]{:S(2)}, u32[]{:S(2)}) collective-permute-start(bf16[2,120,1024]{2,1,0:T(8,128)(2,1)S(1)} %collective-permute-done.10.refs_1_), channel_id=1, source_target_pairs={{0,1},{1,0},{2,3},{3,2},{4,5},{5,4},{6,7},{7,6},{8,9},{9,8},{10,11... | collective-permute-start | bytes 1474568 | tf_op jit(solution)/shard_map/ppermute | solution.py:53
  121.5 2.9 %collective-permute-start.19 = (bf16[2,120,1024]{2,1,0:T(8,128)(2,1)S(1)}, bf16[2,120,1024]{2,1,0:T(8,128)(2,1)S(1)}, u32[]{:S(2)}, u32[]{:S(2)}) collective-permute-start(bf16[2,120,1024]{2,1,0:T(8,128)(2,1)S(1)} %collective-permute-done.6.refs_2_), channel_id=1, source_target_pairs={{0,1},{1,0},{2,3},{3,2},{4,5},{5,4},{6,7},{7,6},{8,9},{9,8},{10,11... | collective-permute-start | bytes 1474568 | tf_op jit(solution)/shard_map/ppermute | solution.py:53
  122.0 3.1 %collective-permute-start.20 = (bf16[2,120,1024]{2,1,0:T(8,128)(2,1)S(1)}, bf16[2,120,1024]{2,1,0:T(8,128)(2,1)S(1)}, u32[]{:S(2)}, u32[]{:S(2)}) collective-permute-start(bf16[2,120,1024]{2,1,0:T(8,128)(2,1)S(1)} %collective-permute-done.11.refs_3_), channel_id=1, source_target_pairs={{0,1},{1,0},{2,3},{3,2},{4,5},{5,4},{6,7},{7,6},{8,9},{9,8},{10,11... | collective-permute-start | bytes 1474568 | tf_op jit(solution)/shard_map/ppermute | solution.py:53
  122.0 6.2 %collective-permute-start.15 = (bf16[2,120,1024]{2,1,0:T(8,128)(2,1)S(1)}, bf16[2,120,1024]{2,1,0:T(8,128)(2,1)S(1)}, u32[]{:S(2)}, u32[]{:S(2)}) collective-permute-start(bf16[2,120,1024]{2,1,0:T(8,128)(2,1)S(1)} %collective-permute-done.12.refs_0_), channel_id=1, source_target_pairs={{0,1},{1,0},{2,3},{3,2},{4,5},{5,4},{6,7},{7,6},{8,9},{9,8},{10,11... | collective-permute-start | bytes 1474568 | tf_op jit(solution)/shard_map/ppermute | solution.py:53
  123.0 5.2 %collective-permute-start.16 = (bf16[2,120,1024]{2,1,0:T(8,128)(2,1)S(1)}, bf16[2,120,1024]{2,1,0:T(8,128)(2,1)S(1)}, u32[]{:S(2)}, u32[]{:S(2)}) collective-permute-start(bf16[2,120,1024]{2,1,0:T(8,128)(2,1)S(1)} %collective-permute-done.13.refs_1_), channel_id=1, source_target_pairs={{0,1},{1,0},{2,3},{3,2},{4,5},{5,4},{6,7},{7,6},{8,9},{9,8},{10,11... | collective-permute-start | bytes 1474568 | tf_op jit(solution)/shard_map/ppermute | solution.py:53
  123.7 4.5 %collective-permute-start.21 = (bf16[2,120,256]{2,1,0:T(8,128)(2,1)S(1)}, bf16[2,120,256]{2,1,0:T(8,128)(2,1)S(1)}, u32[]{:S(2)}, u32[]{:S(2)}) collective-permute-start(bf16[2,120,256]{2,1,0:T(8,128)(2,1)S(1)} %get-tuple-element.88), channel_id=1, source_target_pairs={{0,8},{1,9},{2,10},{3,11},{4,12},{5,13},{6,14},{7,15},{8,0},{9,1},... | collective-permute-start | bytes 368648 | tf_op jit(solution)/shard_map/ppermute | solution.py:53
  127.0 4.7 %collective-permute-start.23 = (bf16[2,120,256]{2,1,0:T(8,128)(2,1)}, bf16[2,120,256]{2,1,0:T(8,128)(2,1)S(1)}, u32[]{:S(2)}, u32[]{:S(2)}) collective-permute-start(bf16[2,120,256]{2,1,0:T(8,128)(2,1)} %get-tuple-element.98), channel_id=1, source_target_pairs={{0,8},{1,9},{2,10},{3,11},{4,12},{5,13},{6,14},{7,15},{8,0},{9,1},... | collective-permute-start | bytes 368648 | tf_op jit(solution)/shard_map/ppermute | solution.py:53
  130.2 5.1 %collective-permute-start.22 = (bf16[2,120,256]{2,1,0:T(8,128)(2,1)}, bf16[2,120,256]{2,1,0:T(8,128)(2,1)S(1)}, u32[]{:S(2)}, u32[]{:S(2)}) collective-permute-start(bf16[2,120,256]{2,1,0:T(8,128)(2,1)} %get-tuple-element.91), channel_id=1, source_target_pairs={{0,8},{1,9},{2,10},{3,11},{4,12},{5,13},{6,14},{7,15},{8,0},{9,1},... | collective-permute-start | bytes 368648 | tf_op jit(solution)/shard_map/ppermute | solution.py:53
  (3 other events, 13.7 us)

commit v6 on v5

--- a/solution.py
+++ b/solution.py
@@ -8,8 +8,8 @@
 from jax.sharding import PartitionSpec as P
 
 BOX = 64
-KC = 2048
-VMEM = 16 * 1024 * 1024
+GROUP = 4
+VMEM = 32 * 1024 * 1024
 BF = jnp.bfloat16
 F32 = jnp.float32
 
@@ -57,20 +57,17 @@
     return lax.dot_general(left, right, (((1,), (1,)), ((), ())), preferred_element_type=F32)
 
 
-def slab_body(val, cond, zeta, weight, root, out, acc):
-    step = pl.program_id(0)
-    conds = cond.shape[0]
-    for c in range(0, conds, 4):
-        lhs = jnp.concatenate([val[...] * cond[c + i : c + i + 1, :] for i in range(4)], axis=0)
-        part = nt_dot(lhs, zeta[...])
-        rows = slice(c * 128, (c + 4) * 128)
-        acc[rows] = jnp.where(step == 0, part, acc[rows] + part)
-
-    @pl.when(step == pl.num_programs(0) - 1)
-    def _():
-        for c in range(conds):
-            rows = slice(c * 128, (c + 1) * 128)
-            out[rows] = (acc[rows] * root[...] * weight[:, c : c + 1]).astype(BF)
+def slab_body(val, cond, zeta, weight, root, out):
+    conds, points = cond.shape
+    for c in range(0, conds, GROUP):
+        left = jnp.concatenate(
+            [val[:, :points] * cond[c + i : c + i + 1, :] for i in range(GROUP)], axis=0
+        )
+        part = nt_dot(left, zeta[...])
+        for i in range(GROUP):
+            at = c + i
+            block = part[i * 128 : (i + 1) * 128] * root[...] * weight[:, at : at + 1]
+            out[at * 128 : (at + 1) * 128] = block.astype(BF)
 
 
 def slab_kernel(val, cond, zeta, weight, root, name):
@@ -79,47 +76,39 @@
     cols = zeta.shape[0]
     return pl.pallas_call(
         slab_body,
-        grid=(points // KC,),
+        grid=(1,),
         in_specs=[
-            pl.BlockSpec((128, KC), lambda k: (0, k)),
-            pl.BlockSpec((conds, KC), lambda k: (0, k)),
-            pl.BlockSpec((cols, KC), lambda k: (0, k)),
+            pl.BlockSpec((128, points), lambda k: (0, 0)),
+            pl.BlockSpec((conds, points), lambda k: (0, 0)),
+            pl.BlockSpec((cols, points), lambda k: (0, 0)),
             pl.BlockSpec((128, conds), lambda k: (0, 0)),
             pl.BlockSpec((1, cols), lambda k: (0, 0)),
         ],
         out_specs=pl.BlockSpec((pairs, cols), lambda k: (0, 0)),
         out_shape=jax.ShapeDtypeStruct((pairs, cols), BF),
-        scratch_shapes=[pltpu.VMEM((pairs, cols), F32)],
         compiler_params=pltpu.CompilerParams(vmem_limit_bytes=VMEM),
         cost_estimate=pl.CostEstimate(flops=1 << 20, bytes_accessed=1 << 16, transcendentals=0),
         name=name,
     )(val, cond, zeta, weight, root)
 
 
-def rho_body(zeta, cond, val_a, val_b, root, out, lhs, rhs, acc):
-    step = pl.program_id(0)
+def rho_body(zeta, cond, val_a, val_b, root, out, lhs, rhs):
     conds = cond.shape[0]
     rows = zeta.shape[0]
-
-    @pl.when(step == 0)
-    def _():
-        lhs[...] = jnp.zeros_like(lhs)
-
+    lhs[...] = jnp.zeros_like(lhs)
     rhs[0:128, :] = val_a[...]
     rhs[128:256, :] = val_b[...]
     lhs[0:rows, :] = zeta[...]
-    for c in range(0, conds, 4):
-        left = jnp.concatenate([lhs[...] * cond[c + i : c + i + 1, :] for i in range(4)], axis=0)
+    for c in range(0, conds, GROUP):
+        left = jnp.concatenate(
+            [lhs[...] * cond[c + i : c + i + 1, :] for i in range(GROUP)], axis=0
+        )
         part = nt_dot(left, rhs[...])
-        span = slice(c * 128, (c + 4) * 128)
-        acc[span] = jnp.where(step == 0, part, acc[span] + part)
-
-    @pl.when(step == pl.num_programs(0) - 1)
-    def _():
-        for c in range(conds):
-            block = acc[c * 128 : c * 128 + rows, :] * root[:, 0:1]
-            out[0, :, c * 128 : (c + 1) * 128] = block[:, 0:128].astype(BF)
-            out[1, :, c * 128 : (c + 1) * 128] = block[:, 128:256].astype(BF)
+        for i in range(GROUP):
+            block = part[i * 128 : i * 128 + rows, :] * root[:, 0:1]
+            at = slice((c + i) * 128, (c + i + 1) * 128)
+            out[0, :, at] = block[:, 0:128].astype(BF)
+            out[1, :, at] = block[:, 128:256].astype(BF)
 
 
 def rho_kernel(zeta, cond, val_a, val_b, root, name):
@@ -128,21 +117,17 @@
     pairs = conds * 128
     return pl.pallas_call(
         rho_body,
-        grid=(points // KC,),
+        grid=(1,),
         in_specs=[
-            pl.BlockSpec((rows, KC), lambda k: (0, k)),
-            pl.BlockSpec((conds, KC), lambda k: (0, k)),
-            pl.BlockSpec((128, KC), lambda k: (0, k)),
-            pl.BlockSpec((128, KC), lambda k: (0, k)),
+            pl.BlockSpec((rows, points), lambda k: (0, 0)),
+            pl.BlockSpec((conds, points), lambda k: (0, 0)),
+            pl.BlockSpec((128, points), lambda k: (0, 0)),
+            pl.BlockSpec((128, points), lambda k: (0, 0)),
             pl.BlockSpec((rows, 128), lambda k: (0, 0)),
         ],
         out_specs=pl.BlockSpec((2, rows, pairs), lambda k: (0, 0, 0)),
         out_shape=jax.ShapeDtypeStruct((2, rows, pairs), BF),
-        scratch_shapes=[
-            pltpu.VMEM((128, KC), BF),
-            pltpu.VMEM((256, KC), BF),
-            pltpu.VMEM((pairs, 256), F32),
-        ],
+        scratch_shapes=[pltpu.VMEM((128, points), BF), pltpu.VMEM((256, points), BF)],
         compiler_params=pltpu.CompilerParams(vmem_limit_bytes=VMEM),
         cost_estimate=pl.CostEstimate(flops=1 << 20, bytes_accessed=1 << 16, transcendentals=0),
         name=name,

time: 137 us -> 133 us (0.971)
  Pallas kernels: 49.6 us -> 44.8 us
    pallas_call x6, Pallas kernels: 38.5 us -> 33.7 us  [the longest x4 21.2 us: slab_kernel(): pl.pallas_call(slab_body, grid=(1,), in_specs=[pl.BlockSpec((128, points)...]
  transfers between devices with their start and end apart: 25 -> 25, of which waited for: 9 -> 10; matrix products, arithmetic and copies ran while one was open for 2% -> 2% of each run, Pallas kernels for 35% -> 33%
where the time goes in v6:
time: 133 us; the launch traced here: 132 us
  Pallas kernels  44.8 us (34%)
  blocking collectives  31.2 us (23%)
  starting transfers between devices  29.1 us (22%)
  waiting for transfers between devices  15.5 us (12%)
  local copies, waits for them, and re-layouts  5.36 us (4%)
  between operations  4.15 us (3%)
  other arithmetic  2.23 us (2%)
    all_to_all x1, blocking collectives, on_device(): lax.all_to_all(jnp.broadcast_to(payload[None], (8, 16, width)), 'grow', s...  31.2 us
    ppermute x24, starting transfers between devices, send(): return lax.ppermute(value, ('band', 'grow'), pairs)  21.7 us
    pallas_call x4, Pallas kernels, slab_kernel(): pl.pallas_call(slab_body, grid=(1,), in_specs=[pl.BlockSpec((128, points)...  21.2 us
    pallas_call x2, Pallas kernels, rho_kernel(): pl.pallas_call(rho_body, grid=(1,), in_specs=[pl.BlockSpec((rows, points)...  12.5 us
    all_to_all x1, waiting for transfers between devices, on_device(): lax.all_to_all(pieces, 'band', split_axis=0, concat_axis=0, tiled=True)  9.52 us
    all_to_all x1, starting transfers between devices, on_device(): lax.all_to_all(pieces, 'band', split_axis=0, concat_axis=0, tiled=True)  7.48 us
    pallas_call x4, Pallas kernels, chi_kernel(): pl.pallas_call(body, out_shape=[jax.ShapeDtypeStruct((count, rows, cols),...  6.32 us
    ppermute x24, waiting for transfers between devices, send(): return lax.ppermute(value, ('band', 'grow'), pairs)  5.94 us
  transfers between devices with their start and end apart: 25, of which 10 were waited for; matrix products, arithmetic and copies ran while one was open for 2% of the time, Pallas kernels for 33%

profile of v6, /device:TPU:1, one launch (start us, length us, event | category | flops | bytes accessed | tf_op | source)
XLA Modules:
  0.0 132.4 jit_solution(510733914731137552)
XLA Ops:
  0.1 1.0 dynamic-slice_bitcast_fusion.3
  1.1 1.8 %broadcast_select_fusion = bf16[8,8,8192]{2,1,0:T(8,128)(2,1)} fusion(pred[8]{0:T(512)(128)(4,1)} %constant.217, bf16[8,8192]{1,0:T(8,128)(2,1)S(1)} %get-tuple-element.102, bf16[8,8192]{1,0:T(8,128)(2,1)S(1)} %get-tuple-element.101), kind=kLoop, calls=%fused_computation.1 | loop fusion | flops 524288 | bytes 1310728 | tf_op jit(solution)/shard_map/jit(_where)/select_n | solution.py:256
  2.9 7.5 %all-to-all-start = ((bf16[8,8,8192]{2,1,0:T(8,128)(2,1)}), bf16[8,8,8192]{2,1,0:T(8,128)(2,1)S(1)}, u32[]{:S(2)}, u32[]{:S(2)}) async-start(bf16[8,8,8192]{2,1,0:T(8,128)(2,1)} %broadcast_select_fusion), calls=%async_computation | async-start | bytes 2097152 | tf_op jit(solution)/shard_map/all_to_all | solution.py:257
  16.3 9.5 %all-to-all-done = bf16[8,8,8192]{2,1,0:T(8,128)(2,1)S(1)} async-done(((bf16[8,8,8192]{2,1,0:T(8,128)(2,1)}), bf16[8,8,8192]{2,1,0:T(8,128)(2,1)S(1)}, u32[]{:S(2)}, u32[]{:S(2)}) %all-to-all-start) | async-done | bytes 1048608 | tf_op jit(solution)/shard_map/all_to_all | solution.py:257
  26.1 31.2 %all_to_all.10 = bf16[8,16,8704]{2,1,0:T(8,128)(2,1)S(1)} all-to-all(bf16[8,16,8704]{2,1,0:T(8,128)(2,1)S(1)} %broadcast_in_dim.68), channel_id=1, replica_groups={{0,2,4,6,8,10,12,14},{1,3,5,7,9,11,13,15},{16,18,20,22,24,26,28,30},{17..., dimensions={0} | all-to-all | bytes 4456448 | tf_op jit(solution)/shard_map/all_to_all | solution.py:282
  57.3 3.0 %collective-permute-start = (bf16[128,8704]{1,0:T(8,128)(2,1)S(1)}, bf16[128,8704]{1,0:T(8,128)(2,1)}, u32[]{:S(2)}, u32[]{:S(2)}) collective-permute-start(bf16[128,8704]{1,0:T(8,128)(2,1)S(1)} %bitcast.31), channel_id=1, source_target_pairs={{0,1},{1,0},{2,3},{3,2},{4,5},{5,4},{6,7},{7,6},{8,9},{9,8},{10,11... | collective-permute-start | bytes 6684680 | tf_op jit(solution)/shard_map/ppermute | solution.py:53
  60.5 2.2 %copy-done.1 = bf16[256,8192]{1,0:T(8,128)(2,1)S(1)} copy-done((bf16[256,8192]{1,0:T(8,128)(2,1)S(1)}, bf16[256,8192]{1,0:T(8,128)(2,1)}, u32[]{:S(2)}) %copy-start.1) | copy-done | bytes 4194328
  62.7 4.5 %slab_00.1.refs_8_ = bf16[1024,256]{1,0:T(8,128)(2,1)S(1)} custom-call(bf16[128,8704]{1,0:T(8,128)(2,1)S(1)} %bitcast.33, bf16[8,8192]{1,0:T(8,128)(2,1)S(1)} %reshape.48.cond, bf16[256,8192]{1,0:T(8,128)(2,1)S(1)} %copy-done.1, f32[128,8]{1,0:T(8,128)S(1)} %get-tuple-element.53.weight, f32[1,256]{1,0:T(1,128)S(1)} %bitcast.39), custom_call_target="tpu_custom_call" | custom-call | flops 1048576 | bytes 65536 | tf_op jit(solution)/shard_map/slab_00/pallas_call | solution.py:77
  67.3 1.5 %collective-permute-start.3 = (bf16[1024,256]{1,0:T(8,128)(2,1)S(1)}, bf16[1024,256]{1,0:T(8,128)(2,1)S(1)}, u32[]{:S(2)}, u32[]{:S(2)}) collective-permute-start(bf16[1024,256]{1,0:T(8,128)(2,1)S(1)} %slab_00.1.refs_8_), channel_id=1, source_target_pairs={{0,24},{1,25},{2,26},{3,27},{4,28},{5,29},{6,30},{7,31},{8,16},{9,... | collective-permute-start | bytes 1572872 | tf_op jit(solution)/shard_map/ppermute | solution.py:53
  69.3 6.3 %rho_0.1.refs_0_ = bf16[2,120,1024]{2,1,0:T(8,128)(2,1)S(1)} custom-call(bf16[120,8192]{1,0:T(8,128)(2,1)S(1)} %copy-done.4, bf16[8,8192]{1,0:T(8,128)(2,1)S(1)} %reshape.48.cond, bf16[128,8704]{1,0:T(8,128)(2,1)S(1)} %bitcast.34, bf16[128,8704]{1,0:T(8,128)(2,1)} %collective-permute-done.val_b.val, f32[120,128]{1,0:T(8,128)S(1)} %broadcast_in_dim.66.root), custom_call_target="tpu_custom_call" | custom-call | flops 1048576 | bytes 65536 | tf_op jit(solution)/shard_map/rho_0/pallas_call | solution.py:118
  75.6 1.1 collective-permute-start.4
  76.7 0.9 collective-permute-start.6
  78.2 6.3 %rho_1.1.refs_1_ = bf16[2,120,1024]{2,1,0:T(8,128)(2,1)S(1)} custom-call(bf16[120,8192]{1,0:T(8,128)(2,1)S(1)} %copy-done.4, bf16[8,8192]{1,0:T(8,128)(2,1)S(1)} %collective-permute-done.1.cond, bf16[128,8704]{1,0:T(8,128)(2,1)S(1)} %bitcast.35, bf16[128,8704]{1,0:T(8,128)(2,1)} %collective-permute-done.val_b.val, f32[120,128]{1,0:T(8,128)S(1)} %broadcast_in_dim.66.root), custom_call_target="tpu_custom_call" | custom-call | flops 1048576 | bytes 65536 | tf_op jit(solution)/shard_map/rho_1/pallas_call | solution.py:118
  85.2 2.1 %collective-permute-start.11 = (bf16[2,120,1024]{2,1,0:T(8,128)(2,1)S(1)}, bf16[2,120,1024]{2,1,0:T(8,128)(2,1)S(1)}, u32[]{:S(2)}, u32[]{:S(2)}) collective-permute-start(bf16[2,120,1024]{2,1,0:T(8,128)(2,1)S(1)} %rho_1.1.refs_1_), channel_id=1, source_target_pairs={{0,6},{1,7},{2,0},{3,1},{4,2},{5,3},{6,4},{7,5},{8,14},{9,15},{10,... | collective-permute-start | bytes 1474568 | tf_op jit(solution)/shard_map/ppermute | solution.py:53
  87.3 4.5 %slab_01.1.refs_9_ = bf16[1024,256]{1,0:T(8,128)(2,1)S(1)} custom-call(bf16[128,8704]{1,0:T(8,128)(2,1)S(1)} %bitcast.36, bf16[8,8192]{1,0:T(8,128)(2,1)S(1)} %collective-permute-done.1.cond, bf16[256,8192]{1,0:T(8,128)(2,1)S(1)} %copy-done.2, f32[128,8]{1,0:T(8,128)S(1)} %get-tuple-element.64.weight, f32[1,256]{1,0:T(1,128)S(1)} %bitcast.40), custom_call_target="tpu_custom_call" | custom-call | flops 1048576 | bytes 65536 | tf_op jit(solution)/shard_map/slab_01/pallas_call | solution.py:77
  92.6 0.8 collective-permute-start.8
  93.4 6.1 %slab_10.1.refs_10_ = bf16[1024,256]{1,0:T(8,128)(2,1)S(1)} custom-call(bf16[128,8704]{1,0:T(8,128)(2,1)} %collective-permute-done.val_b.val, bf16[8,8192]{1,0:T(8,128)(2,1)S(1)} %reshape.48.cond, bf16[256,8192]{1,0:T(8,128)(2,1)S(1)} %copy-done.2, f32[128,8]{1,0:T(8,128)S(1)} %get-tuple-element.70.weight, f32[1,256]{1,0:T(1,128)S(1)} %bitcast.41), custom_call_target="tpu_custom_call" | custom-call | flops 1048576 | bytes 65536 | tf_op jit(solution)/shard_map/slab_10/pallas_call | solution.py:77
  100.1 1.7 %collective-permute-done.10.refs_1_ = bf16[2,120,1024]{2,1,0:T(8,128)(2,1)S(1)} collective-permute-done((bf16[2,120,1024]{2,1,0:T(8,128)(2,1)S(1)}, bf16[2,120,1024]{2,1,0:T(8,128)(2,1)S(1)}, u32[]{:S(2)}, u32[]{:S(2)}) %collective-permute-start.10) | collective-permute-done | bytes 491552 | tf_op jit(solution)/shard_map/ppermute | solution.py:53
  102.3 0.9 collective-permute-start.12
  103.3 6.1 %slab_11.1.refs_11_ = bf16[1024,256]{1,0:T(8,128)(2,1)S(1)} custom-call(bf16[128,8704]{1,0:T(8,128)(2,1)} %collective-permute-done.val_b.val, bf16[8,8192]{1,0:T(8,128)(2,1)S(1)} %collective-permute-done.1.cond, bf16[256,8192]{1,0:T(8,128)(2,1)S(1)} %copy-done.2, f32[128,8]{1,0:T(8,128)S(1)} %get-tuple-element.73.weight, f32[1,256]{1,0:T(1,128)S(1)} %bitcast.42), custom_call_target="tpu_custom_call" | custom-call | flops 1048576 | bytes 65536 | tf_op jit(solution)/shard_map/slab_11/pallas_call | solution.py:77
  109.4 1.3 chi_own.1
  110.7 1.1 collective-permute-start.14
  111.7 1.3 chi_near.1
  113.3 1.4 %collective-permute-done.12.refs_0_ = bf16[2,120,1024]{2,1,0:T(8,128)(2,1)S(1)} collective-permute-done((bf16[2,120,1024]{2,1,0:T(8,128)(2,1)S(1)}, bf16[2,120,1024]{2,1,0:T(8,128)(2,1)S(1)}, u32[]{:S(2)}, u32[]{:S(2)}) %collective-permute-start.12) | collective-permute-done | bytes 491552 | tf_op jit(solution)/shard_map/ppermute | solution.py:53
  114.8 2.6 %collective-permute-start.17 = (bf16[2,120,1024]{2,1,0:T(8,128)(2,1)S(1)}, bf16[2,120,1024]{2,1,0:T(8,128)(2,1)S(1)}, u32[]{:S(2)}, u32[]{:S(2)}) collective-permute-start(bf16[2,120,1024]{2,1,0:T(8,128)(2,1)S(1)} %collective-permute-done.5.refs_0_), channel_id=1, source_target_pairs={{0,1},{1,0},{2,3},{3,2},{4,5},{5,4},{6,7},{7,6},{8,9},{9,8},{10,11... | collective-permute-start | bytes 1474568 | tf_op jit(solution)/shard_map/ppermute | solution.py:53
  119.6 1.0 collective-permute-start.21
  121.0 1.9 %chi_next.1 = (bf16[2,120,256]{2,1,0:T(8,128)(2,1)}, f32[2,120,256]{2,1,0:T(8,128)S(1)}) custom-call(bf16[2,120,1024]{2,1,0:T(8,128)(2,1)S(1)} %collective-permute-done.17.refs_0_, bf16[2,120,1024]{2,1,0:T(8,128)(2,1)S(1)} %collective-permute-done.18.refs_1_, bf16[2,120,1024]{2,1,0:T(8,128)(2,1)S(1)} %collective-permute-done.19.refs_2_, ...), custom_call_target="tpu_custom_call" | custom-call | flops 1048576 | bytes 65536 | tf_op jit(solution)/shard_map/chi_next/pallas_call | solution.py:174
  122.9 1.0 collective-permute-start.23
  124.1 1.9 %chi_far.1 = (bf16[2,120,256]{2,1,0:T(8,128)(2,1)}, f32[2,120,256]{2,1,0:T(8,128)S(1)}) custom-call(bf16[2,120,1024]{2,1,0:T(8,128)(2,1)S(1)} %collective-permute-done.12.refs_0_, bf16[2,120,1024]{2,1,0:T(8,128)(2,1)S(1)} %collective-permute-done.13.refs_1_, bf16[2,120,1024]{2,1,0:T(8,128)(2,1)S(1)} %collective-permute-done.15.refs_2_, ...), custom_call_target="tpu_custom_call" | custom-call | flops 1048576 | bytes 65536 | tf_op jit(solution)/shard_map/chi_far/pallas_call | solution.py:174
  126.0 1.0 collective-permute-start.22
  127.6 3.5 %finish_most.1.refs_2_ = f32[16,120,256]{2,1,0:T(8,128)} custom-call(s32[8]{0:T(128)S(1)} %stack.44.place_ref, f32[16,120,256]{2,1,0:T(8,128)S(1)} %bitcast.37, f32[2,120,256]{2,1,0:T(8,128)S(1)} %get-tuple-element.92.refs_0_.refs_1_, f32[2,120,256]{2,1,0:T(8,128)S(1)} %get-tuple-element.92.refs_0_.refs_1_, f32[2,120,256]{2,1,0:T(8,128)S(1)} %get-tuple-element.93.refs_2_, ...), custom_call_target="tpu_custom_call" | custom-call | flops 1048576 | bytes 65536 | tf_op jit(solution)/shard_map/finish_most/pallas_call | solution.py:217
  131.1 1.3 finish_far.1
  (82 shorter events, 10.1 us)
Async XLA Ops:
  0.0 10.8 %copy-start = (f32[8,128]{1,0:T(8,128)S(1)}, f32[8,128]{1,0:T(8,128)}, u32[]{:S(2)}) copy-start(f32[8,128]{1,0:T(8,128)} %param.15) | copy-start | bytes 12292
  0.0 10.3 %copy-start.6 = (s32[2]{0:T(128)S(1)}, s32[2]{0:T(128)}, u32[]{:S(2)}) copy-start(s32[2]{0:T(128)} %param.18) | copy-start | bytes 28
  0.0 10.4 %copy-start.9 = (s32[120]{0:T(128)S(1)}, s32[120]{0:T(128)}, u32[]{:S(2)}) copy-start(s32[120]{0:T(128)} %param.19) | copy-start | bytes 1444
  0.0 10.4 %copy-start.8 = (f32[16]{0:T(128)S(1)}, f32[16]{0:T(128)}, u32[]{:S(2)}) copy-start(f32[16]{0:T(128)} %param.17) | copy-start | bytes 196
  0.1 14.7 %copy-start.5 = (bf16[1,8192]{1,0:T(2,128)(2,1)S(1)}, bf16[1,8192]{1,0:T(2,128)(2,1)}, u32[]{:S(2)}) copy-start(bf16[1,8192]{1,0:T(2,128)(2,1)} %param.16) | copy-start | bytes 49156
  0.1 16.1 %copy-start.7 = (s32[256]{0:T(256)S(1)}, s32[256]{0:T(256)}, u32[]{:S(2)}) copy-start(s32[256]{0:T(256)} %param.20) | copy-start | bytes 3076
  2.9 23.0 %all-to-all-start = ((bf16[8,8,8192]{2,1,0:T(8,128)(2,1)}), bf16[8,8,8192]{2,1,0:T(8,128)(2,1)S(1)}, u32[]{:S(2)}, u32[]{:S(2)}) async-start(bf16[8,8,8192]{2,1,0:T(8,128)(2,1)} %broadcast_select_fusion), calls=%async_computation | async-start | bytes 2097152 | tf_op jit(solution)/shard_map/all_to_all | solution.py:257
  57.3 9.9 %collective-permute-start = (bf16[128,8704]{1,0:T(8,128)(2,1)S(1)}, bf16[128,8704]{1,0:T(8,128)(2,1)}, u32[]{:S(2)}, u32[]{:S(2)}) collective-permute-start(bf16[128,8704]{1,0:T(8,128)(2,1)S(1)} %bitcast.31), channel_id=1, source_target_pairs={{0,1},{1,0},{2,3},{3,2},{4,5},{5,4},{6,7},{7,6},{8,9},{9,8},{10,11... | collective-permute-start | bytes 6684680 | tf_op jit(solution)/shard_map/ppermute | solution.py:53
  60.4 6.8 %collective-permute-start.1 = (bf16[8,8192]{1,0:T(8,128)(2,1)S(1)}, bf16[8,8192]{1,0:T(8,128)(2,1)S(1)}, u32[]{:S(2)}, u32[]{:S(2)}) collective-permute-start(bf16[8,8192]{1,0:T(8,128)(2,1)S(1)} %reshape.48.cond), channel_id=1, source_target_pairs={{0,1},{1,0},{2,3},{3,2},{4,5},{5,4},{6,7},{7,6},{8,9},{9,8},{10,11... | collective-permute-start | bytes 393224 | tf_op jit(solution)/shard_map/ppermute | solution.py:53
  67.3 17.2 %collective-permute-start.3 = (bf16[1024,256]{1,0:T(8,128)(2,1)S(1)}, bf16[1024,256]{1,0:T(8,128)(2,1)S(1)}, u32[]{:S(2)}, u32[]{:S(2)}) collective-permute-start(bf16[1024,256]{1,0:T(8,128)(2,1)S(1)} %slab_00.1.refs_8_), channel_id=1, source_target_pairs={{0,24},{1,25},{2,26},{3,27},{4,28},{5,29},{6,30},{7,31},{8,16},{9,... | collective-permute-start | bytes 1572872 | tf_op jit(solution)/shard_map/ppermute | solution.py:53
  68.7 15.8 %collective-permute-start.2 = (bf16[1024,256]{1,0:T(8,128)(2,1)S(1)}, bf16[1024,256]{1,0:T(8,128)(2,1)S(1)}, u32[]{:S(2)}, u32[]{:S(2)}) collective-permute-start(bf16[1024,256]{1,0:T(8,128)(2,1)S(1)} %slab_00.1.refs_8_), channel_id=1, source_target_pairs={{0,8},{1,9},{2,10},{3,11},{4,12},{5,13},{6,14},{7,15},{8,0},{9,1},... | collective-permute-start | bytes 1572872 | tf_op jit(solution)/shard_map/ppermute | solution.py:53
  75.6 11.7 %copy-start.2 = (bf16[256,8192]{1,0:T(8,128)(2,1)S(1)}, bf16[256,8192]{1,0:T(8,128)(2,1)}, u32[]{:S(2)}) copy-start(bf16[256,8192]{1,0:T(8,128)(2,1)} %zeta.11) | copy-start | bytes 12582916
  75.6 8.9 %collective-permute-start.4 = (bf16[2,120,1024]{2,1,0:T(8,128)(2,1)S(1)}, bf16[2,120,1024]{2,1,0:T(8,128)(2,1)S(1)}, u32[]{:S(2)}, u32[]{:S(2)}) collective-permute-start(bf16[2,120,1024]{2,1,0:T(8,128)(2,1)S(1)} %rho_0.1.refs_0_), channel_id=1, source_target_pairs={{0,1},{1,0},{2,3},{3,2},{4,5},{5,4},{6,7},{7,6},{8,9},{9,8},{10,11... | collective-permute-start | bytes 1474568 | tf_op jit(solution)/shard_map/ppermute | solution.py:53
  76.7 15.1 %collective-permute-start.6 = (bf16[2,120,1024]{2,1,0:T(8,128)(2,1)S(1)}, bf16[2,120,1024]{2,1,0:T(8,128)(2,1)S(1)}, u32[]{:S(2)}, u32[]{:S(2)}) collective-permute-start(bf16[2,120,1024]{2,1,0:T(8,128)(2,1)S(1)} %rho_0.1.refs_0_), channel_id=1, source_target_pairs={{0,6},{1,7},{2,0},{3,1},{4,2},{5,3},{6,4},{7,5},{8,14},{9,15},{10,... | collective-permute-start | bytes 1474568 | tf_op jit(solution)/shard_map/ppermute | solution.py:53
  77.6 14.2 %collective-permute-start.5 = (bf16[2,120,1024]{2,1,0:T(8,128)(2,1)S(1)}, bf16[2,120,1024]{2,1,0:T(8,128)(2,1)S(1)}, u32[]{:S(2)}, u32[]{:S(2)}) collective-permute-start(bf16[2,120,1024]{2,1,0:T(8,128)(2,1)S(1)} %rho_0.1.refs_0_), channel_id=1, source_target_pairs={{0,2},{1,3},{2,4},{3,5},{4,6},{5,7},{6,0},{7,1},{8,10},{9,11},{10,... | collective-permute-start | bytes 1474568 | tf_op jit(solution)/shard_map/ppermute | solution.py:53
  84.5 7.3 %collective-permute-start.7 = (bf16[2,120,1024]{2,1,0:T(8,128)(2,1)S(1)}, bf16[2,120,1024]{2,1,0:T(8,128)(2,1)S(1)}, u32[]{:S(2)}, u32[]{:S(2)}) collective-permute-start(bf16[2,120,1024]{2,1,0:T(8,128)(2,1)S(1)} %rho_1.1.refs_1_), channel_id=1, source_target_pairs={{0,1},{1,0},{2,3},{3,2},{4,5},{5,4},{6,7},{7,6},{8,9},{9,8},{10,11... | collective-permute-start | bytes 1474568 | tf_op jit(solution)/shard_map/ppermute | solution.py:53
  85.2 14.9 %collective-permute-start.11 = (bf16[2,120,1024]{2,1,0:T(8,128)(2,1)S(1)}, bf16[2,120,1024]{2,1,0:T(8,128)(2,1)S(1)}, u32[]{:S(2)}, u32[]{:S(2)}) collective-permute-start(bf16[2,120,1024]{2,1,0:T(8,128)(2,1)S(1)} %rho_1.1.refs_1_), channel_id=1, source_target_pairs={{0,6},{1,7},{2,0},{3,1},{4,2},{5,3},{6,4},{7,5},{8,14},{9,15},{10,... | collective-permute-start | bytes 1474568 | tf_op jit(solution)/shard_map/ppermute | solution.py:53
  87.3 14.5 %collective-permute-start.10 = (bf16[2,120,1024]{2,1,0:T(8,128)(2,1)S(1)}, bf16[2,120,1024]{2,1,0:T(8,128)(2,1)S(1)}, u32[]{:S(2)}, u32[]{:S(2)}) collective-permute-start(bf16[2,120,1024]{2,1,0:T(8,128)(2,1)S(1)} %rho_1.1.refs_1_), channel_id=1, source_target_pairs={{0,2},{1,3},{2,4},{3,5},{4,6},{5,7},{6,0},{7,1},{8,10},{9,11},{10,... | collective-permute-start | bytes 1474568 | tf_op jit(solution)/shard_map/ppermute | solution.py:53
  91.8 17.6 %collective-permute-start.9 = (bf16[1024,256]{1,0:T(8,128)(2,1)S(1)}, bf16[1024,256]{1,0:T(8,128)(2,1)S(1)}, u32[]{:S(2)}, u32[]{:S(2)}) collective-permute-start(bf16[1024,256]{1,0:T(8,128)(2,1)S(1)} %slab_01.1.refs_9_), channel_id=1, source_target_pairs={{0,24},{1,25},{2,26},{3,27},{4,28},{5,29},{6,30},{7,31},{8,16},{9,... | collective-permute-start | bytes 1572872 | tf_op jit(solution)/shard_map/ppermute | solution.py:53
  92.6 16.8 %collective-permute-start.8 = (bf16[1024,256]{1,0:T(8,128)(2,1)S(1)}, bf16[1024,256]{1,0:T(8,128)(2,1)S(1)}, u32[]{:S(2)}, u32[]{:S(2)}) collective-permute-start(bf16[1024,256]{1,0:T(8,128)(2,1)S(1)} %slab_01.1.refs_9_), channel_id=1, source_target_pairs={{0,8},{1,9},{2,10},{3,11},{4,12},{5,13},{6,14},{7,15},{8,0},{9,1},... | collective-permute-start | bytes 1572872 | tf_op jit(solution)/shard_map/ppermute | solution.py:53
  101.8 11.5 %collective-permute-start.13 = (bf16[2,120,1024]{2,1,0:T(8,128)(2,1)S(1)}, bf16[2,120,1024]{2,1,0:T(8,128)(2,1)S(1)}, u32[]{:S(2)}, u32[]{:S(2)}) collective-permute-start(bf16[2,120,1024]{2,1,0:T(8,128)(2,1)S(1)} %collective-permute-done.11.refs_3_), channel_id=1, source_target_pairs={{0,6},{1,7},{2,0},{3,1},{4,2},{5,3},{6,4},{7,5},{8,14},{9,15},{10,... | collective-permute-start | bytes 1474568 | tf_op jit(solution)/shard_map/ppermute | solution.py:53
  102.3 12.5 %collective-permute-start.12 = (bf16[2,120,1024]{2,1,0:T(8,128)(2,1)S(1)}, bf16[2,120,1024]{2,1,0:T(8,128)(2,1)S(1)}, u32[]{:S(2)}, u32[]{:S(2)}) collective-permute-start(bf16[2,120,1024]{2,1,0:T(8,128)(2,1)S(1)} %collective-permute-done.5.refs_0_), channel_id=1, source_target_pairs={{0,2},{1,3},{2,4},{3,5},{4,6},{5,7},{6,0},{7,1},{8,10},{9,11},{10,... | collective-permute-start | bytes 1474568 | tf_op jit(solution)/shard_map/ppermute | solution.py:53
  110.7 4.1 %collective-permute-start.14 = (bf16[2,120,256]{2,1,0:T(8,128)(2,1)S(1)}, bf16[2,120,256]{2,1,0:T(8,128)(2,1)S(1)}, u32[]{:S(2)}, u32[]{:S(2)}) collective-permute-start(bf16[2,120,256]{2,1,0:T(8,128)(2,1)S(1)} %get-tuple-element.80), channel_id=1, source_target_pairs={{0,8},{1,9},{2,10},{3,11},{4,12},{5,13},{6,14},{7,15},{8,0},{9,1},... | collective-permute-start | bytes 368648 | tf_op jit(solution)/shard_map/ppermute | solution.py:53
  114.8 4.1 %collective-permute-start.17 = (bf16[2,120,1024]{2,1,0:T(8,128)(2,1)S(1)}, bf16[2,120,1024]{2,1,0:T(8,128)(2,1)S(1)}, u32[]{:S(2)}, u32[]{:S(2)}) collective-permute-start(bf16[2,120,1024]{2,1,0:T(8,128)(2,1)S(1)} %collective-permute-done.5.refs_0_), channel_id=1, source_target_pairs={{0,1},{1,0},{2,3},{3,2},{4,5},{5,4},{6,7},{7,6},{8,9},{9,8},{10,11... | collective-permute-start | bytes 1474568 | tf_op jit(solution)/shard_map/ppermute | solution.py:53
  117.4 2.2 %collective-permute-start.18 = (bf16[2,120,1024]{2,1,0:T(8,128)(2,1)S(1)}, bf16[2,120,1024]{2,1,0:T(8,128)(2,1)S(1)}, u32[]{:S(2)}, u32[]{:S(2)}) collective-permute-start(bf16[2,120,1024]{2,1,0:T(8,128)(2,1)S(1)} %collective-permute-done.10.refs_1_), channel_id=1, source_target_pairs={{0,1},{1,0},{2,3},{3,2},{4,5},{5,4},{6,7},{7,6},{8,9},{9,8},{10,11... | collective-permute-start | bytes 1474568 | tf_op jit(solution)/shard_map/ppermute | solution.py:53
  117.4 3.2 %collective-permute-start.19 = (bf16[2,120,1024]{2,1,0:T(8,128)(2,1)S(1)}, bf16[2,120,1024]{2,1,0:T(8,128)(2,1)S(1)}, u32[]{:S(2)}, u32[]{:S(2)}) collective-permute-start(bf16[2,120,1024]{2,1,0:T(8,128)(2,1)S(1)} %collective-permute-done.6.refs_2_), channel_id=1, source_target_pairs={{0,1},{1,0},{2,3},{3,2},{4,5},{5,4},{6,7},{7,6},{8,9},{9,8},{10,11... | collective-permute-start | bytes 1474568 | tf_op jit(solution)/shard_map/ppermute | solution.py:53
  117.9 3.1 %collective-permute-start.20 = (bf16[2,120,1024]{2,1,0:T(8,128)(2,1)S(1)}, bf16[2,120,1024]{2,1,0:T(8,128)(2,1)S(1)}, u32[]{:S(2)}, u32[]{:S(2)}) collective-permute-start(bf16[2,120,1024]{2,1,0:T(8,128)(2,1)S(1)} %collective-permute-done.11.refs_3_), channel_id=1, source_target_pairs={{0,1},{1,0},{2,3},{3,2},{4,5},{5,4},{6,7},{7,6},{8,9},{9,8},{10,11... | collective-permute-start | bytes 1474568 | tf_op jit(solution)/shard_map/ppermute | solution.py:53
  117.9 6.2 %collective-permute-start.15 = (bf16[2,120,1024]{2,1,0:T(8,128)(2,1)S(1)}, bf16[2,120,1024]{2,1,0:T(8,128)(2,1)S(1)}, u32[]{:S(2)}, u32[]{:S(2)}) collective-permute-start(bf16[2,120,1024]{2,1,0:T(8,128)(2,1)S(1)} %collective-permute-done.12.refs_0_), channel_id=1, source_target_pairs={{0,1},{1,0},{2,3},{3,2},{4,5},{5,4},{6,7},{7,6},{8,9},{9,8},{10,11... | collective-permute-start | bytes 1474568 | tf_op jit(solution)/shard_map/ppermute | solution.py:53
  118.9 5.2 %collective-permute-start.16 = (bf16[2,120,1024]{2,1,0:T(8,128)(2,1)S(1)}, bf16[2,120,1024]{2,1,0:T(8,128)(2,1)S(1)}, u32[]{:S(2)}, u32[]{:S(2)}) collective-permute-start(bf16[2,120,1024]{2,1,0:T(8,128)(2,1)S(1)} %collective-permute-done.13.refs_1_), channel_id=1, source_target_pairs={{0,1},{1,0},{2,3},{3,2},{4,5},{5,4},{6,7},{7,6},{8,9},{9,8},{10,11... | collective-permute-start | bytes 1474568 | tf_op jit(solution)/shard_map/ppermute | solution.py:53
  119.6 4.5 %collective-permute-start.21 = (bf16[2,120,256]{2,1,0:T(8,128)(2,1)S(1)}, bf16[2,120,256]{2,1,0:T(8,128)(2,1)S(1)}, u32[]{:S(2)}, u32[]{:S(2)}) collective-permute-start(bf16[2,120,256]{2,1,0:T(8,128)(2,1)S(1)} %get-tuple-element.88), channel_id=1, source_target_pairs={{0,8},{1,9},{2,10},{3,11},{4,12},{5,13},{6,14},{7,15},{8,0},{9,1},... | collective-permute-start | bytes 368648 | tf_op jit(solution)/shard_map/ppermute | solution.py:53
  122.9 4.7 %collective-permute-start.23 = (bf16[2,120,256]{2,1,0:T(8,128)(2,1)}, bf16[2,120,256]{2,1,0:T(8,128)(2,1)S(1)}, u32[]{:S(2)}, u32[]{:S(2)}) collective-permute-start(bf16[2,120,256]{2,1,0:T(8,128)(2,1)} %get-tuple-element.98), channel_id=1, source_target_pairs={{0,8},{1,9},{2,10},{3,11},{4,12},{5,13},{6,14},{7,15},{8,0},{9,1},... | collective-permute-start | bytes 368648 | tf_op jit(solution)/shard_map/ppermute | solution.py:53
  126.0 5.1 %collective-permute-start.22 = (bf16[2,120,256]{2,1,0:T(8,128)(2,1)}, bf16[2,120,256]{2,1,0:T(8,128)(2,1)S(1)}, u32[]{:S(2)}, u32[]{:S(2)}) collective-permute-start(bf16[2,120,256]{2,1,0:T(8,128)(2,1)} %get-tuple-element.91), channel_id=1, source_target_pairs={{0,8},{1,9},{2,10},{3,11},{4,12},{5,13},{6,14},{7,15},{8,0},{9,1},... | collective-permute-start | bytes 368648 | tf_op jit(solution)/shard_map/ppermute | solution.py:53
  (3 other events, 12.3 us)

commit v7 on v6

--- a/solution.py
+++ b/solution.py
@@ -10,6 +10,7 @@
 BOX = 64
 GROUP = 4
 VMEM = 32 * 1024 * 1024
+SMALL = 16 * 1024 * 1024
 BF = jnp.bfloat16
 F32 = jnp.float32
 
@@ -175,7 +176,7 @@
         body,
         out_shape=[jax.ShapeDtypeStruct((count, rows, cols), dtype) for _, dtype in sides],
         scratch_shapes=[pltpu.VMEM((4, count * 128, blk), BF)],
-        compiler_params=pltpu.CompilerParams(vmem_limit_bytes=VMEM),
+        compiler_params=pltpu.CompilerParams(vmem_limit_bytes=SMALL),
         cost_estimate=pl.CostEstimate(flops=1 << 20, bytes_accessed=1 << 16, transcendentals=0),
         name=name,
     )(*arrays, *slabs)
@@ -224,7 +225,7 @@
         ),
         out_shape=jax.ShapeDtypeStruct(chi.shape, F32),
         input_output_aliases=aliases,
-        compiler_params=pltpu.CompilerParams(vmem_limit_bytes=VMEM),
+        compiler_params=pltpu.CompilerParams(vmem_limit_bytes=SMALL),
         cost_estimate=pl.CostEstimate(flops=1 << 20, bytes_accessed=1 << 16, transcendentals=0),
         name=name,
     )(*operands)
@@ -250,10 +251,10 @@
     points = valence_store.shape[2]
 
     store = valence_store[0]
-    piece_a = lax.dynamic_slice_in_dim(store, yz * 16 + core * 8, 8, 0)
-    piece_b = lax.dynamic_slice_in_dim(store, yz * 16 + (1 - core) * 8, 8, 0)
+    both_cores = lax.dynamic_slice_in_dim(store, yz * 16, 16, 0).reshape(2, 8, points)
     turns = jnp.array([(b // 2 + b % 2) % 2 for b in range(8)])
-    pieces = jnp.where(turns[:, None, None] == 1, piece_b[None], piece_a[None])
+    first = ((turns + core) % 2 == 0)[:, None, None]
+    pieces = jnp.where(first, both_cores[0][None], both_cores[1][None])
     panels = lax.all_to_all(pieces, "band", split_axis=0, concat_axis=0, tiled=True)
     chosen = jnp.concatenate(
         [lax.dynamic_slice_in_dim(panels, owners[i], 1, 0)[0] for i in range(2)], axis=0

time: 133 us -> 133 us (level)
  no operation moved by 1% of the time
where the time goes in v7:
time: 133 us; the launch traced here: 132 us
  Pallas kernels  44.8 us (34%)
  blocking collectives  31.2 us (23%)
  starting transfers between devices  29.2 us (22%)
  waiting for transfers between devices  15.4 us (12%)
  local copies, waits for them, and re-layouts  5.36 us (4%)
  between operations  4.13 us (3%)
  other arithmetic  2.25 us (2%)
    all_to_all x1, blocking collectives, on_device(): lax.all_to_all(jnp.broadcast_to(payload[None], (8, 16, width)), 'grow', s...  31.2 us
    ppermute x24, starting transfers between devices, send(): return lax.ppermute(value, ('band', 'grow'), pairs)  21.7 us
    pallas_call x4, Pallas kernels, slab_kernel(): pl.pallas_call(slab_body, grid=(1,), in_specs=[pl.BlockSpec((128, points)...  21.2 us
    pallas_call x2, Pallas kernels, rho_kernel(): pl.pallas_call(rho_body, grid=(1,), in_specs=[pl.BlockSpec((rows, points)...  12.5 us
    all_to_all x1, waiting for transfers between devices, on_device(): lax.all_to_all(pieces, 'band', split_axis=0, concat_axis=0, tiled=True)  9.52 us
    all_to_all x1, starting transfers between devices, on_device(): lax.all_to_all(pieces, 'band', split_axis=0, concat_axis=0, tiled=True)  7.48 us
    pallas_call x4, Pallas kernels, chi_kernel(): pl.pallas_call(body, out_shape=[jax.ShapeDtypeStruct((count, rows, cols),...  6.33 us
    ppermute x24, waiting for transfers between devices, send(): return lax.ppermute(value, ('band', 'grow'), pairs)  5.87 us
  transfers between devices with their start and end apart: 25, of which 10 were waited for; matrix products, arithmetic and copies ran while one was open for 2% of the time, Pallas kernels for 33%

profile of v7, /device:TPU:1, one launch (start us, length us, event | category | flops | bytes accessed | tf_op | source)
XLA Modules:
  0.0 132.4 jit_solution(14844726693472289010)
XLA Ops:
  0.7 1.0 dynamic-slice_bitcast_fusion.1
  1.8 1.1 broadcast_select_fusion
  2.9 7.5 %all-to-all-start = ((bf16[8,8,8192]{2,1,0:T(8,128)(2,1)}), bf16[8,8,8192]{2,1,0:T(8,128)(2,1)S(1)}, u32[]{:S(2)}, u32[]{:S(2)}) async-start(bf16[8,8,8192]{2,1,0:T(8,128)(2,1)} %broadcast_select_fusion), calls=%async_computation | async-start | bytes 2097152 | tf_op jit(solution)/shard_map/all_to_all | solution.py:258
  16.3 9.5 %all-to-all-done = bf16[8,8,8192]{2,1,0:T(8,128)(2,1)S(1)} async-done(((bf16[8,8,8192]{2,1,0:T(8,128)(2,1)}), bf16[8,8,8192]{2,1,0:T(8,128)(2,1)S(1)}, u32[]{:S(2)}, u32[]{:S(2)}) %all-to-all-start) | async-done | bytes 1048608 | tf_op jit(solution)/shard_map/all_to_all | solution.py:258
  26.1 31.2 %all_to_all.10 = bf16[8,16,8704]{2,1,0:T(8,128)(2,1)S(1)} all-to-all(bf16[8,16,8704]{2,1,0:T(8,128)(2,1)S(1)} %broadcast_in_dim.66), channel_id=1, replica_groups={{0,2,4,6,8,10,12,14},{1,3,5,7,9,11,13,15},{16,18,20,22,24,26,28,30},{17..., dimensions={0} | all-to-all | bytes 4456448 | tf_op jit(solution)/shard_map/all_to_all | solution.py:283
  57.3 3.0 %collective-permute-start = (bf16[128,8704]{1,0:T(8,128)(2,1)S(1)}, bf16[128,8704]{1,0:T(8,128)(2,1)}, u32[]{:S(2)}, u32[]{:S(2)}) collective-permute-start(bf16[128,8704]{1,0:T(8,128)(2,1)S(1)} %bitcast.31), channel_id=1, source_target_pairs={{0,1},{1,0},{2,3},{3,2},{4,5},{5,4},{6,7},{7,6},{8,9},{9,8},{10,11... | collective-permute-start | bytes 6684680 | tf_op jit(solution)/shard_map/ppermute | solution.py:54
  60.5 2.2 %copy-done.1 = bf16[256,8192]{1,0:T(8,128)(2,1)S(1)} copy-done((bf16[256,8192]{1,0:T(8,128)(2,1)S(1)}, bf16[256,8192]{1,0:T(8,128)(2,1)}, u32[]{:S(2)}) %copy-start.1) | copy-done | bytes 4194328
  62.7 4.5 %slab_00.1.refs_8_ = bf16[1024,256]{1,0:T(8,128)(2,1)S(1)} custom-call(bf16[128,8704]{1,0:T(8,128)(2,1)S(1)} %bitcast.33, bf16[8,8192]{1,0:T(8,128)(2,1)S(1)} %reshape.48.cond, bf16[256,8192]{1,0:T(8,128)(2,1)S(1)} %copy-done.1, f32[128,8]{1,0:T(8,128)S(1)} %get-tuple-element.53.weight, f32[1,256]{1,0:T(1,128)S(1)} %bitcast.39), custom_call_target="tpu_custom_call" | custom-call | flops 1048576 | bytes 65536 | tf_op jit(solution)/shard_map/slab_00/pallas_call | solution.py:78
  67.3 1.5 %collective-permute-start.3 = (bf16[1024,256]{1,0:T(8,128)(2,1)S(1)}, bf16[1024,256]{1,0:T(8,128)(2,1)S(1)}, u32[]{:S(2)}, u32[]{:S(2)}) collective-permute-start(bf16[1024,256]{1,0:T(8,128)(2,1)S(1)} %slab_00.1.refs_8_), channel_id=1, source_target_pairs={{0,24},{1,25},{2,26},{3,27},{4,28},{5,29},{6,30},{7,31},{8,16},{9,... | collective-permute-start | bytes 1572872 | tf_op jit(solution)/shard_map/ppermute | solution.py:54
  69.3 6.3 %rho_0.1.refs_0_ = bf16[2,120,1024]{2,1,0:T(8,128)(2,1)S(1)} custom-call(bf16[120,8192]{1,0:T(8,128)(2,1)S(1)} %copy-done.4, bf16[8,8192]{1,0:T(8,128)(2,1)S(1)} %reshape.48.cond, bf16[128,8704]{1,0:T(8,128)(2,1)S(1)} %bitcast.34, bf16[128,8704]{1,0:T(8,128)(2,1)} %collective-permute-done.val_b.val, f32[120,128]{1,0:T(8,128)S(1)} %broadcast_in_dim.64.root), custom_call_target="tpu_custom_call" | custom-call | flops 1048576 | bytes 65536 | tf_op jit(solution)/shard_map/rho_0/pallas_call | solution.py:119
  75.6 1.1 collective-permute-start.4
  76.7 0.9 collective-permute-start.6
  78.2 6.2 %rho_1.1.refs_1_ = bf16[2,120,1024]{2,1,0:T(8,128)(2,1)S(1)} custom-call(bf16[120,8192]{1,0:T(8,128)(2,1)S(1)} %copy-done.4, bf16[8,8192]{1,0:T(8,128)(2,1)S(1)} %collective-permute-done.1.cond, bf16[128,8704]{1,0:T(8,128)(2,1)S(1)} %bitcast.35, bf16[128,8704]{1,0:T(8,128)(2,1)} %collective-permute-done.val_b.val, f32[120,128]{1,0:T(8,128)S(1)} %broadcast_in_dim.64.root), custom_call_target="tpu_custom_call" | custom-call | flops 1048576 | bytes 65536 | tf_op jit(solution)/shard_map/rho_1/pallas_call | solution.py:119
  85.2 2.1 %collective-permute-start.11 = (bf16[2,120,1024]{2,1,0:T(8,128)(2,1)S(1)}, bf16[2,120,1024]{2,1,0:T(8,128)(2,1)S(1)}, u32[]{:S(2)}, u32[]{:S(2)}) collective-permute-start(bf16[2,120,1024]{2,1,0:T(8,128)(2,1)S(1)} %rho_1.1.refs_1_), channel_id=1, source_target_pairs={{0,6},{1,7},{2,0},{3,1},{4,2},{5,3},{6,4},{7,5},{8,14},{9,15},{10,... | collective-permute-start | bytes 1474568 | tf_op jit(solution)/shard_map/ppermute | solution.py:54
  87.3 4.5 %slab_01.1.refs_9_ = bf16[1024,256]{1,0:T(8,128)(2,1)S(1)} custom-call(bf16[128,8704]{1,0:T(8,128)(2,1)S(1)} %bitcast.36, bf16[8,8192]{1,0:T(8,128)(2,1)S(1)} %collective-permute-done.1.cond, bf16[256,8192]{1,0:T(8,128)(2,1)S(1)} %copy-done.2, f32[128,8]{1,0:T(8,128)S(1)} %get-tuple-element.64.weight, f32[1,256]{1,0:T(1,128)S(1)} %bitcast.40), custom_call_target="tpu_custom_call" | custom-call | flops 1048576 | bytes 65536 | tf_op jit(solution)/shard_map/slab_01/pallas_call | solution.py:78
  92.6 0.8 collective-permute-start.8
  93.4 6.1 %slab_10.1.refs_10_ = bf16[1024,256]{1,0:T(8,128)(2,1)S(1)} custom-call(bf16[128,8704]{1,0:T(8,128)(2,1)} %collective-permute-done.val_b.val, bf16[8,8192]{1,0:T(8,128)(2,1)S(1)} %reshape.48.cond, bf16[256,8192]{1,0:T(8,128)(2,1)S(1)} %copy-done.2, f32[128,8]{1,0:T(8,128)S(1)} %get-tuple-element.70.weight, f32[1,256]{1,0:T(1,128)S(1)} %bitcast.41), custom_call_target="tpu_custom_call" | custom-call | flops 1048576 | bytes 65536 | tf_op jit(solution)/shard_map/slab_10/pallas_call | solution.py:78
  100.1 1.7 %collective-permute-done.10.refs_1_ = bf16[2,120,1024]{2,1,0:T(8,128)(2,1)S(1)} collective-permute-done((bf16[2,120,1024]{2,1,0:T(8,128)(2,1)S(1)}, bf16[2,120,1024]{2,1,0:T(8,128)(2,1)S(1)}, u32[]{:S(2)}, u32[]{:S(2)}) %collective-permute-start.10) | collective-permute-done | bytes 491552 | tf_op jit(solution)/shard_map/ppermute | solution.py:54
  102.3 0.9 collective-permute-start.12
  103.3 6.1 %slab_11.1.refs_11_ = bf16[1024,256]{1,0:T(8,128)(2,1)S(1)} custom-call(bf16[128,8704]{1,0:T(8,128)(2,1)} %collective-permute-done.val_b.val, bf16[8,8192]{1,0:T(8,128)(2,1)S(1)} %collective-permute-done.1.cond, bf16[256,8192]{1,0:T(8,128)(2,1)S(1)} %copy-done.2, f32[128,8]{1,0:T(8,128)S(1)} %get-tuple-element.73.weight, f32[1,256]{1,0:T(1,128)S(1)} %bitcast.42), custom_call_target="tpu_custom_call" | custom-call | flops 1048576 | bytes 65536 | tf_op jit(solution)/shard_map/slab_11/pallas_call | solution.py:78
  109.4 1.3 chi_own.1
  110.6 1.1 collective-permute-start.14
  111.7 1.3 chi_near.1
  113.3 1.5 %collective-permute-done.12.refs_0_ = bf16[2,120,1024]{2,1,0:T(8,128)(2,1)S(1)} collective-permute-done((bf16[2,120,1024]{2,1,0:T(8,128)(2,1)S(1)}, bf16[2,120,1024]{2,1,0:T(8,128)(2,1)S(1)}, u32[]{:S(2)}, u32[]{:S(2)}) %collective-permute-start.12) | collective-permute-done | bytes 491552 | tf_op jit(solution)/shard_map/ppermute | solution.py:54
  114.8 2.6 %collective-permute-start.17 = (bf16[2,120,1024]{2,1,0:T(8,128)(2,1)S(1)}, bf16[2,120,1024]{2,1,0:T(8,128)(2,1)S(1)}, u32[]{:S(2)}, u32[]{:S(2)}) collective-permute-start(bf16[2,120,1024]{2,1,0:T(8,128)(2,1)S(1)} %collective-permute-done.5.refs_0_), channel_id=1, source_target_pairs={{0,1},{1,0},{2,3},{3,2},{4,5},{5,4},{6,7},{7,6},{8,9},{9,8},{10,11... | collective-permute-start | bytes 1474568 | tf_op jit(solution)/shard_map/ppermute | solution.py:54
  119.5 1.0 collective-permute-start.21
  120.9 1.9 %chi_next.1 = (bf16[2,120,256]{2,1,0:T(8,128)(2,1)}, f32[2,120,256]{2,1,0:T(8,128)S(1)}) custom-call(bf16[2,120,1024]{2,1,0:T(8,128)(2,1)S(1)} %collective-permute-done.17.refs_0_, bf16[2,120,1024]{2,1,0:T(8,128)(2,1)S(1)} %collective-permute-done.18.refs_1_, bf16[2,120,1024]{2,1,0:T(8,128)(2,1)S(1)} %collective-permute-done.19.refs_2_, ...), custom_call_target="tpu_custom_call" | custom-call | flops 1048576 | bytes 65536 | tf_op jit(solution)/shard_map/chi_next/pallas_call | solution.py:175
  122.8 1.0 collective-permute-start.23
  124.1 1.9 %chi_far.1 = (bf16[2,120,256]{2,1,0:T(8,128)(2,1)}, f32[2,120,256]{2,1,0:T(8,128)S(1)}) custom-call(bf16[2,120,1024]{2,1,0:T(8,128)(2,1)S(1)} %collective-permute-done.12.refs_0_, bf16[2,120,1024]{2,1,0:T(8,128)(2,1)S(1)} %collective-permute-done.13.refs_1_, bf16[2,120,1024]{2,1,0:T(8,128)(2,1)S(1)} %collective-permute-done.15.refs_2_, ...), custom_call_target="tpu_custom_call" | custom-call | flops 1048576 | bytes 65536 | tf_op jit(solution)/shard_map/chi_far/pallas_call | solution.py:175
  126.0 1.0 collective-permute-start.22
  127.6 3.5 %finish_most.1.refs_2_ = f32[16,120,256]{2,1,0:T(8,128)} custom-call(s32[8]{0:T(128)S(1)} %stack.44.place_ref, f32[16,120,256]{2,1,0:T(8,128)S(1)} %bitcast.37, f32[2,120,256]{2,1,0:T(8,128)S(1)} %get-tuple-element.92.refs_0_.refs_1_, f32[2,120,256]{2,1,0:T(8,128)S(1)} %get-tuple-element.92.refs_0_.refs_1_, f32[2,120,256]{2,1,0:T(8,128)S(1)} %get-tuple-element.93.refs_2_, ...), custom_call_target="tpu_custom_call" | custom-call | flops 1048576 | bytes 65536 | tf_op jit(solution)/shard_map/finish_most/pallas_call | solution.py:218
  131.1 1.3 finish_far.1
  (83 shorter events, 10.7 us)
Async XLA Ops:
  0.0 10.8 %copy-start = (f32[8,128]{1,0:T(8,128)S(1)}, f32[8,128]{1,0:T(8,128)}, u32[]{:S(2)}) copy-start(f32[8,128]{1,0:T(8,128)} %param.15) | copy-start | bytes 12292
  0.0 10.3 %copy-start.6 = (s32[2]{0:T(128)S(1)}, s32[2]{0:T(128)}, u32[]{:S(2)}) copy-start(s32[2]{0:T(128)} %param.18) | copy-start | bytes 28
  0.0 10.4 %copy-start.9 = (s32[120]{0:T(128)S(1)}, s32[120]{0:T(128)}, u32[]{:S(2)}) copy-start(s32[120]{0:T(128)} %param.19) | copy-start | bytes 1444
  0.0 10.4 %copy-start.8 = (f32[16]{0:T(128)S(1)}, f32[16]{0:T(128)}, u32[]{:S(2)}) copy-start(f32[16]{0:T(128)} %param.17) | copy-start | bytes 196
  0.7 14.0 %copy-start.5 = (bf16[1,8192]{1,0:T(2,128)(2,1)S(1)}, bf16[1,8192]{1,0:T(2,128)(2,1)}, u32[]{:S(2)}) copy-start(bf16[1,8192]{1,0:T(2,128)(2,1)} %param.16) | copy-start | bytes 49156
  0.7 15.4 %copy-start.7 = (s32[256]{0:T(256)S(1)}, s32[256]{0:T(256)}, u32[]{:S(2)}) copy-start(s32[256]{0:T(256)} %param.20) | copy-start | bytes 3076
  2.9 23.0 %all-to-all-start = ((bf16[8,8,8192]{2,1,0:T(8,128)(2,1)}), bf16[8,8,8192]{2,1,0:T(8,128)(2,1)S(1)}, u32[]{:S(2)}, u32[]{:S(2)}) async-start(bf16[8,8,8192]{2,1,0:T(8,128)(2,1)} %broadcast_select_fusion), calls=%async_computation | async-start | bytes 2097152 | tf_op jit(solution)/shard_map/all_to_all | solution.py:258
  57.3 9.9 %collective-permute-start = (bf16[128,8704]{1,0:T(8,128)(2,1)S(1)}, bf16[128,8704]{1,0:T(8,128)(2,1)}, u32[]{:S(2)}, u32[]{:S(2)}) collective-permute-start(bf16[128,8704]{1,0:T(8,128)(2,1)S(1)} %bitcast.31), channel_id=1, source_target_pairs={{0,1},{1,0},{2,3},{3,2},{4,5},{5,4},{6,7},{7,6},{8,9},{9,8},{10,11... | collective-permute-start | bytes 6684680 | tf_op jit(solution)/shard_map/ppermute | solution.py:54
  60.4 6.8 %collective-permute-start.1 = (bf16[8,8192]{1,0:T(8,128)(2,1)S(1)}, bf16[8,8192]{1,0:T(8,128)(2,1)S(1)}, u32[]{:S(2)}, u32[]{:S(2)}) collective-permute-start(bf16[8,8192]{1,0:T(8,128)(2,1)S(1)} %reshape.48.cond), channel_id=1, source_target_pairs={{0,1},{1,0},{2,3},{3,2},{4,5},{5,4},{6,7},{7,6},{8,9},{9,8},{10,11... | collective-permute-start | bytes 393224 | tf_op jit(solution)/shard_map/ppermute | solution.py:54
  67.3 17.2 %collective-permute-start.3 = (bf16[1024,256]{1,0:T(8,128)(2,1)S(1)}, bf16[1024,256]{1,0:T(8,128)(2,1)S(1)}, u32[]{:S(2)}, u32[]{:S(2)}) collective-permute-start(bf16[1024,256]{1,0:T(8,128)(2,1)S(1)} %slab_00.1.refs_8_), channel_id=1, source_target_pairs={{0,24},{1,25},{2,26},{3,27},{4,28},{5,29},{6,30},{7,31},{8,16},{9,... | collective-permute-start | bytes 1572872 | tf_op jit(solution)/shard_map/ppermute | solution.py:54
  68.7 15.7 %collective-permute-start.2 = (bf16[1024,256]{1,0:T(8,128)(2,1)S(1)}, bf16[1024,256]{1,0:T(8,128)(2,1)S(1)}, u32[]{:S(2)}, u32[]{:S(2)}) collective-permute-start(bf16[1024,256]{1,0:T(8,128)(2,1)S(1)} %slab_00.1.refs_8_), channel_id=1, source_target_pairs={{0,8},{1,9},{2,10},{3,11},{4,12},{5,13},{6,14},{7,15},{8,0},{9,1},... | collective-permute-start | bytes 1572872 | tf_op jit(solution)/shard_map/ppermute | solution.py:54
  75.6 11.7 %copy-start.2 = (bf16[256,8192]{1,0:T(8,128)(2,1)S(1)}, bf16[256,8192]{1,0:T(8,128)(2,1)}, u32[]{:S(2)}) copy-start(bf16[256,8192]{1,0:T(8,128)(2,1)} %zeta.11) | copy-start | bytes 12582916
  75.6 8.9 %collective-permute-start.4 = (bf16[2,120,1024]{2,1,0:T(8,128)(2,1)S(1)}, bf16[2,120,1024]{2,1,0:T(8,128)(2,1)S(1)}, u32[]{:S(2)}, u32[]{:S(2)}) collective-permute-start(bf16[2,120,1024]{2,1,0:T(8,128)(2,1)S(1)} %rho_0.1.refs_0_), channel_id=1, source_target_pairs={{0,1},{1,0},{2,3},{3,2},{4,5},{5,4},{6,7},{7,6},{8,9},{9,8},{10,11... | collective-permute-start | bytes 1474568 | tf_op jit(solution)/shard_map/ppermute | solution.py:54
  76.7 15.1 %collective-permute-start.6 = (bf16[2,120,1024]{2,1,0:T(8,128)(2,1)S(1)}, bf16[2,120,1024]{2,1,0:T(8,128)(2,1)S(1)}, u32[]{:S(2)}, u32[]{:S(2)}) collective-permute-start(bf16[2,120,1024]{2,1,0:T(8,128)(2,1)S(1)} %rho_0.1.refs_0_), channel_id=1, source_target_pairs={{0,6},{1,7},{2,0},{3,1},{4,2},{5,3},{6,4},{7,5},{8,14},{9,15},{10,... | collective-permute-start | bytes 1474568 | tf_op jit(solution)/shard_map/ppermute | solution.py:54
  77.6 14.2 %collective-permute-start.5 = (bf16[2,120,1024]{2,1,0:T(8,128)(2,1)S(1)}, bf16[2,120,1024]{2,1,0:T(8,128)(2,1)S(1)}, u32[]{:S(2)}, u32[]{:S(2)}) collective-permute-start(bf16[2,120,1024]{2,1,0:T(8,128)(2,1)S(1)} %rho_0.1.refs_0_), channel_id=1, source_target_pairs={{0,2},{1,3},{2,4},{3,5},{4,6},{5,7},{6,0},{7,1},{8,10},{9,11},{10,... | collective-permute-start | bytes 1474568 | tf_op jit(solution)/shard_map/ppermute | solution.py:54
  84.5 7.3 %collective-permute-start.7 = (bf16[2,120,1024]{2,1,0:T(8,128)(2,1)S(1)}, bf16[2,120,1024]{2,1,0:T(8,128)(2,1)S(1)}, u32[]{:S(2)}, u32[]{:S(2)}) collective-permute-start(bf16[2,120,1024]{2,1,0:T(8,128)(2,1)S(1)} %rho_1.1.refs_1_), channel_id=1, source_target_pairs={{0,1},{1,0},{2,3},{3,2},{4,5},{5,4},{6,7},{7,6},{8,9},{9,8},{10,11... | collective-permute-start | bytes 1474568 | tf_op jit(solution)/shard_map/ppermute | solution.py:54
  85.2 14.8 %collective-permute-start.11 = (bf16[2,120,1024]{2,1,0:T(8,128)(2,1)S(1)}, bf16[2,120,1024]{2,1,0:T(8,128)(2,1)S(1)}, u32[]{:S(2)}, u32[]{:S(2)}) collective-permute-start(bf16[2,120,1024]{2,1,0:T(8,128)(2,1)S(1)} %rho_1.1.refs_1_), channel_id=1, source_target_pairs={{0,6},{1,7},{2,0},{3,1},{4,2},{5,3},{6,4},{7,5},{8,14},{9,15},{10,... | collective-permute-start | bytes 1474568 | tf_op jit(solution)/shard_map/ppermute | solution.py:54
  87.3 14.5 %collective-permute-start.10 = (bf16[2,120,1024]{2,1,0:T(8,128)(2,1)S(1)}, bf16[2,120,1024]{2,1,0:T(8,128)(2,1)S(1)}, u32[]{:S(2)}, u32[]{:S(2)}) collective-permute-start(bf16[2,120,1024]{2,1,0:T(8,128)(2,1)S(1)} %rho_1.1.refs_1_), channel_id=1, source_target_pairs={{0,2},{1,3},{2,4},{3,5},{4,6},{5,7},{6,0},{7,1},{8,10},{9,11},{10,... | collective-permute-start | bytes 1474568 | tf_op jit(solution)/shard_map/ppermute | solution.py:54
  91.8 17.5 %collective-permute-start.9 = (bf16[1024,256]{1,0:T(8,128)(2,1)S(1)}, bf16[1024,256]{1,0:T(8,128)(2,1)S(1)}, u32[]{:S(2)}, u32[]{:S(2)}) collective-permute-start(bf16[1024,256]{1,0:T(8,128)(2,1)S(1)} %slab_01.1.refs_9_), channel_id=1, source_target_pairs={{0,24},{1,25},{2,26},{3,27},{4,28},{5,29},{6,30},{7,31},{8,16},{9,... | collective-permute-start | bytes 1572872 | tf_op jit(solution)/shard_map/ppermute | solution.py:54
  92.6 16.8 %collective-permute-start.8 = (bf16[1024,256]{1,0:T(8,128)(2,1)S(1)}, bf16[1024,256]{1,0:T(8,128)(2,1)S(1)}, u32[]{:S(2)}, u32[]{:S(2)}) collective-permute-start(bf16[1024,256]{1,0:T(8,128)(2,1)S(1)} %slab_01.1.refs_9_), channel_id=1, source_target_pairs={{0,8},{1,9},{2,10},{3,11},{4,12},{5,13},{6,14},{7,15},{8,0},{9,1},... | collective-permute-start | bytes 1572872 | tf_op jit(solution)/shard_map/ppermute | solution.py:54
  101.8 11.5 %collective-permute-start.13 = (bf16[2,120,1024]{2,1,0:T(8,128)(2,1)S(1)}, bf16[2,120,1024]{2,1,0:T(8,128)(2,1)S(1)}, u32[]{:S(2)}, u32[]{:S(2)}) collective-permute-start(bf16[2,120,1024]{2,1,0:T(8,128)(2,1)S(1)} %collective-permute-done.11.refs_3_), channel_id=1, source_target_pairs={{0,6},{1,7},{2,0},{3,1},{4,2},{5,3},{6,4},{7,5},{8,14},{9,15},{10,... | collective-permute-start | bytes 1474568 | tf_op jit(solution)/shard_map/ppermute | solution.py:54
  102.3 12.5 %collective-permute-start.12 = (bf16[2,120,1024]{2,1,0:T(8,128)(2,1)S(1)}, bf16[2,120,1024]{2,1,0:T(8,128)(2,1)S(1)}, u32[]{:S(2)}, u32[]{:S(2)}) collective-permute-start(bf16[2,120,1024]{2,1,0:T(8,128)(2,1)S(1)} %collective-permute-done.5.refs_0_), channel_id=1, source_target_pairs={{0,2},{1,3},{2,4},{3,5},{4,6},{5,7},{6,0},{7,1},{8,10},{9,11},{10,... | collective-permute-start | bytes 1474568 | tf_op jit(solution)/shard_map/ppermute | solution.py:54
  110.6 4.1 %collective-permute-start.14 = (bf16[2,120,256]{2,1,0:T(8,128)(2,1)S(1)}, bf16[2,120,256]{2,1,0:T(8,128)(2,1)S(1)}, u32[]{:S(2)}, u32[]{:S(2)}) collective-permute-start(bf16[2,120,256]{2,1,0:T(8,128)(2,1)S(1)} %get-tuple-element.80), channel_id=1, source_target_pairs={{0,8},{1,9},{2,10},{3,11},{4,12},{5,13},{6,14},{7,15},{8,0},{9,1},... | collective-permute-start | bytes 368648 | tf_op jit(solution)/shard_map/ppermute | solution.py:54
  114.8 4.1 %collective-permute-start.17 = (bf16[2,120,1024]{2,1,0:T(8,128)(2,1)S(1)}, bf16[2,120,1024]{2,1,0:T(8,128)(2,1)S(1)}, u32[]{:S(2)}, u32[]{:S(2)}) collective-permute-start(bf16[2,120,1024]{2,1,0:T(8,128)(2,1)S(1)} %collective-permute-done.5.refs_0_), channel_id=1, source_target_pairs={{0,1},{1,0},{2,3},{3,2},{4,5},{5,4},{6,7},{7,6},{8,9},{9,8},{10,11... | collective-permute-start | bytes 1474568 | tf_op jit(solution)/shard_map/ppermute | solution.py:54
  117.3 2.2 %collective-permute-start.18 = (bf16[2,120,1024]{2,1,0:T(8,128)(2,1)S(1)}, bf16[2,120,1024]{2,1,0:T(8,128)(2,1)S(1)}, u32[]{:S(2)}, u32[]{:S(2)}) collective-permute-start(bf16[2,120,1024]{2,1,0:T(8,128)(2,1)S(1)} %collective-permute-done.10.refs_1_), channel_id=1, source_target_pairs={{0,1},{1,0},{2,3},{3,2},{4,5},{5,4},{6,7},{7,6},{8,9},{9,8},{10,11... | collective-permute-start | bytes 1474568 | tf_op jit(solution)/shard_map/ppermute | solution.py:54
  117.3 3.2 %collective-permute-start.19 = (bf16[2,120,1024]{2,1,0:T(8,128)(2,1)S(1)}, bf16[2,120,1024]{2,1,0:T(8,128)(2,1)S(1)}, u32[]{:S(2)}, u32[]{:S(2)}) collective-permute-start(bf16[2,120,1024]{2,1,0:T(8,128)(2,1)S(1)} %collective-permute-done.6.refs_2_), channel_id=1, source_target_pairs={{0,1},{1,0},{2,3},{3,2},{4,5},{5,4},{6,7},{7,6},{8,9},{9,8},{10,11... | collective-permute-start | bytes 1474568 | tf_op jit(solution)/shard_map/ppermute | solution.py:54
  117.9 3.1 %collective-permute-start.20 = (bf16[2,120,1024]{2,1,0:T(8,128)(2,1)S(1)}, bf16[2,120,1024]{2,1,0:T(8,128)(2,1)S(1)}, u32[]{:S(2)}, u32[]{:S(2)}) collective-permute-start(bf16[2,120,1024]{2,1,0:T(8,128)(2,1)S(1)} %collective-permute-done.11.refs_3_), channel_id=1, source_target_pairs={{0,1},{1,0},{2,3},{3,2},{4,5},{5,4},{6,7},{7,6},{8,9},{9,8},{10,11... | collective-permute-start | bytes 1474568 | tf_op jit(solution)/shard_map/ppermute | solution.py:54
  117.9 6.2 %collective-permute-start.15 = (bf16[2,120,1024]{2,1,0:T(8,128)(2,1)S(1)}, bf16[2,120,1024]{2,1,0:T(8,128)(2,1)S(1)}, u32[]{:S(2)}, u32[]{:S(2)}) collective-permute-start(bf16[2,120,1024]{2,1,0:T(8,128)(2,1)S(1)} %collective-permute-done.12.refs_0_), channel_id=1, source_target_pairs={{0,1},{1,0},{2,3},{3,2},{4,5},{5,4},{6,7},{7,6},{8,9},{9,8},{10,11... | collective-permute-start | bytes 1474568 | tf_op jit(solution)/shard_map/ppermute | solution.py:54
  118.8 5.2 %collective-permute-start.16 = (bf16[2,120,1024]{2,1,0:T(8,128)(2,1)S(1)}, bf16[2,120,1024]{2,1,0:T(8,128)(2,1)S(1)}, u32[]{:S(2)}, u32[]{:S(2)}) collective-permute-start(bf16[2,120,1024]{2,1,0:T(8,128)(2,1)S(1)} %collective-permute-done.13.refs_1_), channel_id=1, source_target_pairs={{0,1},{1,0},{2,3},{3,2},{4,5},{5,4},{6,7},{7,6},{8,9},{9,8},{10,11... | collective-permute-start | bytes 1474568 | tf_op jit(solution)/shard_map/ppermute | solution.py:54
  119.5 4.5 %collective-permute-start.21 = (bf16[2,120,256]{2,1,0:T(8,128)(2,1)S(1)}, bf16[2,120,256]{2,1,0:T(8,128)(2,1)S(1)}, u32[]{:S(2)}, u32[]{:S(2)}) collective-permute-start(bf16[2,120,256]{2,1,0:T(8,128)(2,1)S(1)} %get-tuple-element.88), channel_id=1, source_target_pairs={{0,8},{1,9},{2,10},{3,11},{4,12},{5,13},{6,14},{7,15},{8,0},{9,1},... | collective-permute-start | bytes 368648 | tf_op jit(solution)/shard_map/ppermute | solution.py:54
  122.8 4.7 %collective-permute-start.23 = (bf16[2,120,256]{2,1,0:T(8,128)(2,1)}, bf16[2,120,256]{2,1,0:T(8,128)(2,1)S(1)}, u32[]{:S(2)}, u32[]{:S(2)}) collective-permute-start(bf16[2,120,256]{2,1,0:T(8,128)(2,1)} %get-tuple-element.98), channel_id=1, source_target_pairs={{0,8},{1,9},{2,10},{3,11},{4,12},{5,13},{6,14},{7,15},{8,0},{9,1},... | collective-permute-start | bytes 368648 | tf_op jit(solution)/shard_map/ppermute | solution.py:54
  126.0 5.1 %collective-permute-start.22 = (bf16[2,120,256]{2,1,0:T(8,128)(2,1)}, bf16[2,120,256]{2,1,0:T(8,128)(2,1)S(1)}, u32[]{:S(2)}, u32[]{:S(2)}) collective-permute-start(bf16[2,120,256]{2,1,0:T(8,128)(2,1)} %get-tuple-element.91), channel_id=1, source_target_pairs={{0,8},{1,9},{2,10},{3,11},{4,12},{5,13},{6,14},{7,15},{8,0},{9,1},... | collective-permute-start | bytes 368648 | tf_op jit(solution)/shard_map/ppermute | solution.py:54
  (3 other events, 12.3 us)
